TPU v7x, 32 devices: a whole 2x2x4 slice. The times are simulated.
32 devices in a mesh: group: 2 (over y), batch: 4 (over x, core), tensor: 4 (over z).
Axes of the slice: x: 2, y: 2, z: 4, core: 2. Of those that a mesh axis runs over, the one named last changes fastest.
Arguments:
- query: bfloat16 [256, 4096], P(('group', 'batch', 'tensor')), parts along dimension 0, may hold values from -200 to 200
- fresh_key: bfloat16 [256, 512], P(('group', 'batch', 'tensor')), parts along dimension 0, may hold values from -6 to 6
- fresh_value: bfloat16 [256, 512], P(('group', 'batch', 'tensor')), parts along dimension 0, may hold values from -12 to 12
- stored_keys: bfloat16 [256, 4, 128, 128], P(('group', 'batch', 'tensor')), parts along dimension 0, may hold values from -6 to 6
- stored_values: bfloat16 [256, 4, 128, 128], P(('group', 'batch', 'tensor')), parts along dimension 0, may hold values from -12 to 12
- cached_length: int32 [256], P(('group', 'batch', 'tensor')), parts along dimension 0, may hold values from 32 to 128
- request_adapter: int32 [256], P(('group', 'batch', 'tensor')), parts along dimension 0, may hold values from 0 to 15, as said below
- rank_per_adapter: int32 [16], replicated, may hold values from 8 to 128, as said below
- output_weight: bfloat16 [4096, 8192], P('tensor'), may hold values from -0.125 to 0.125
- adapter_down_weight: bfloat16 [16, 4096, 128], P('batch', 'tensor'), may hold values from -0.09375 to 0.09375
- adapter_up_weight: bfloat16 [16, 128, 8192], P('batch', None, 'tensor'), may hold values from -0.75 to 0.75
Outputs:
- mixed: bfloat16 [256, 8192], P(('group', 'batch'), 'tensor'), parts along dimension 0
There are 2 independent parts, one for each index of `group`. A program takes and returns all parts, laid end to end along the dimension named above; an argument that names none is the same for every part. Nothing has to cross between parts.
Inputs may be any that keep to these rules, and one draw needn't show every extreme that they name: `rank_per_adapter`: each rank is 128 divided by a power of two. `request_adapter`: adapter a is held by owner a // 4. Among the 32 requests of one batch index (aligned blocks), at most 16 name adapters of one owner; some owner has exactly 16 in every block.
All inputs are finite; a program needn't handle non-finite values.
Results may differ from a plain program's by a relative error of at most 0.013.
Values may be sent and summed in bfloat16 or wider, within the bound.
No kernel may reach another device: no remote copies, remote signals or barrier semaphores. Data moves between devices by JAX's collectives and lax.ppermute only.
A program may use at most 128 MiB of HBM per device.

v0:
```python
import math

import jax
import jax.numpy as jnp
from jax import lax
from jax.sharding import PartitionSpec as P

ADAPTER_SCALE = 16.0


def attend(query, fresh_key, fresh_value, stored_keys, stored_values, cached_length):
    requests = query.shape[0]
    kv_heads = stored_keys.shape[1]
    longest = stored_keys.shape[2]
    head_dim = stored_keys.shape[3]
    group_size = query.shape[1] // (kv_heads * head_dim)
    queries = query.reshape(requests, kv_heads, group_size, head_dim)
    scaling = 1.0 / math.sqrt(head_dim)
    scores = (
        jnp.einsum("rkgd,rkld->rkgl", queries, stored_keys, preferred_element_type=jnp.float32)
        * scaling
    )
    own_score = (
        jnp.einsum(
            "rkgd,rkd->rkg",
            queries,
            fresh_key.reshape(requests, kv_heads, head_dim),
            preferred_element_type=jnp.float32,
        )
        * scaling
    )
    valid = (jnp.arange(longest, dtype=jnp.int32)[None, :] < cached_length[:, None])[
        :, None, None, :
    ]
    scores = jnp.where(valid, scores, -1e30)
    highest = jnp.maximum(jnp.max(scores, axis=-1), own_score)
    exponent = jnp.where(valid, jnp.exp(scores - highest[..., None]), 0.0)
    own_exp = jnp.exp(own_score - highest)
    sum_exp = jnp.sum(exponent, axis=-1) + own_exp
    weights = (exponent / sum_exp[..., None]).astype(jnp.bfloat16)
    own_weight = (own_exp / sum_exp).astype(jnp.bfloat16)
    result = jnp.einsum(
        "rkgl,rkld->rkgd", weights, stored_values, preferred_element_type=jnp.float32
    )
    own_value = fresh_value.reshape(requests, kv_heads, 1, head_dim).astype(jnp.float32)
    result = result + own_weight.astype(jnp.float32)[..., None] * own_value
    return result.reshape(requests, -1).astype(jnp.bfloat16)


def shrink(values, request_ranks):
    keep_mask = jnp.arange(values.shape[-1], dtype=jnp.int32) < request_ranks[..., None]
    rank_factor = ADAPTER_SCALE / request_ranks.astype(jnp.float32)
    return jnp.where(keep_mask, values * rank_factor[..., None], 0.0).astype(jnp.bfloat16)


def per_device(
    query,
    fresh_key,
    fresh_value,
    stored_keys,
    stored_values,
    cached_length,
    request_adapter,
    rank_per_adapter,
    output_weight,
    adapter_down_weight,
    adapter_up_weight,
):
    attention_result = attend(
        query, fresh_key, fresh_value, stored_keys, stored_values, cached_length
    )
    tensor_count = lax.axis_size("tensor")
    requests = query.shape[0]
    tiled_ids = jnp.broadcast_to(request_adapter[:, None], (requests, tensor_count))
    head_rows, row_ids = (
        lax.all_to_all(attention_result, "tensor", split_axis=1, concat_axis=0, tiled=True),
        lax.all_to_all(tiled_ids, "tensor", split_axis=1, concat_axis=0, tiled=True),
    )
    row_ids = row_ids[:, 0]
    row_count = head_rows.shape[0]
    adapter_count = rank_per_adapter.shape[0]
    picked = row_ids[:, None] == jnp.arange(adapter_count, dtype=jnp.int32)[None, :]
    row_rank = jnp.sum(jnp.where(picked, rank_per_adapter[None, :], 0), axis=1)
    products = jnp.dot(head_rows, output_weight, preferred_element_type=jnp.float32)
    base = lax.psum_scatter(
        products.astype(jnp.bfloat16), "tensor", scatter_dimension=1, tiled=True
    ).astype(jnp.float32)
    rank_span = adapter_down_weight.shape[2]
    zero_half = jnp.zeros((), jnp.bfloat16)
    down_all, up_all = (
        lax.all_gather(adapter_down_weight, "batch", axis=0, tiled=True),
        lax.all_gather(adapter_up_weight, "batch", axis=0, tiled=True),
    )
    slot_count = down_all.shape[0]
    one_hot = row_ids[:, None] == jnp.arange(slot_count, dtype=jnp.int32)[None, :]
    low_every = jnp.einsum("rk,skj->rsj", head_rows, down_all, preferred_element_type=jnp.float32)
    low_share = jnp.sum(jnp.where(one_hot[:, :, None], low_every, 0.0), axis=1)
    low_full = lax.psum(low_share.astype(jnp.bfloat16), "tensor").astype(jnp.float32)
    adapter_delta = shrink(low_full, row_rank)
    widened = jnp.where(one_hot[:, :, None], adapter_delta[:, None, :], zero_half).reshape(
        row_count, slot_count * rank_span
    )
    adapted = jnp.dot(
        widened, up_all.reshape(slot_count * rank_span, -1), preferred_element_type=jnp.float32
    ).astype(jnp.bfloat16)
    return (base + adapted.astype(jnp.float32)).astype(jnp.bfloat16)


def solution(mesh):
    in_specs = (
        P(("group", "batch", "tensor"), None),
        P(("group", "batch", "tensor"), None),
        P(("group", "batch", "tensor"), None),
        P(("group", "batch", "tensor"), None, None, None),
        P(("group", "batch", "tensor"), None, None, None),
        P(("group", "batch", "tensor")),
        P(("group", "batch", "tensor")),
        P(),
        P("tensor", None),
        P("batch", "tensor", None),
        P("batch", None, "tensor"),
    )
    out_specs = P(("group", "batch"), "tensor")
    return jax.shard_map(
        per_device, mesh=mesh, in_specs=in_specs, out_specs=out_specs, check_vma=False
    )
```

profile of v0, /device:TPU:0, one launch (start us, length us, event | category | flops | bytes accessed | tf_op | source)
XLA Modules:
  0.0 120.0 jit_solution(14737810705706189444)
XLA Ops:
  7.4 0.0 copy-start
  7.4 0.7 all-gather.3.cloned.1.call-update
  8.1 0.0 reduce-scatter.2.cloned.1.call-start
  8.1 0.7 bitcast_convert_fusion
  8.9 0.7 iota_compare_fusion.2
  9.6 1.0 fusion.18
  10.6 1.6 %fusion.26 = (f32[8,4,8]{2,1,0:T(4,128)S(1)}, f32[8,4,8,128]{3,2,1,0:T(8,128)S(1)}) fusion(bf16[8,4,128,128]{3,2,1,0:T(8,128)(2,1)S(1)} %copy-done, bf16[8,4,8,128]{3,0,2,1:T(8,128)(2,1)} %bitcast.38, pred[8,128]{1,0:T(8,128)(4,1)S(1)} %iota_compare_fusion.2), kind=kOutput, calls=%fused_computation.44 | convolution fusion | flops 8486656 | bytes 1247232 | tf_op jit(solution)/shard_map/rkgd,rkld->rkgl/dot_general | solution.py:20
  12.2 0.2 fusion.9
  12.4 1.7 %fusion.6 = bf16[8,4,8,128]{3,2,1,0:T(8,128)(2,1)S(1)} fusion(bf16[8,4,128,128]{3,2,1,0:T(8,128)(2,1)} %param.15, f32[8,4,8,128]{3,2,1,0:T(8,128)S(1)} %get-tuple-element.8, f32[8,4,128]{2,1,0:T(4,128)S(1)} %copy.18, f32[8,4,8]{2,1,0:T(4,128)S(1)} %get-tuple-element.6, f32[8,4,8]{2,1,0:T(4,128)S(1)} %get-tuple-element.5, ...), kind=kOutput, calls=%fused_computation.11 | convolution fusion | flops 8617984 | bytes 1265664 | tf_op jit(solution)/shard_map/rkgl,rkld->rkgd/dot_general | solution.py:42
  14.2 11.9 %all_to_all.29 = bf16[8,4,1024]{2,0,1:T(8,128)(2,1)S(1)} all-to-all(bf16[8,4,1024]{2,0,1:T(8,128)(2,1)S(1)} %copy.19), channel_id=1, replica_groups=mesh['group'=2,'batch'=4,'tensor'=4] {'tensor'}, dimensions={1} | all-to-all | bytes 131072 | tf_op jit(solution)/shard_map/all_to_all | solution.py:76
  26.0 9.7 %convolution_convert_fusion = bf16[32,8192]{1,0:T(8,128)(2,1)} fusion(bf16[1024,8192]{1,0:T(8,128)(2,1)} %param.19, bf16[8,4,1024]{2,0,1:T(8,128)(2,1)S(1)} %all_to_all.29), kind=kOutput, calls=%fused_computation | convolution fusion | flops 537133056 | bytes 17367040 | tf_op jit(solution)/shard_map/dot_general | solution.py:84
  35.7 0.0 reduce-scatter.2.cloned.1.call-update
  35.8 0.0 all-gather.5.cloned.1.call-start
  35.8 0.7 all-gather.5.cloned.1.call-update
  36.5 0.0 copy-done.1
  36.5 7.9 %all_to_all.30 = s32[8,4,1]{0,2,1:T(1,128)S(1)} all-to-all(s32[8,4,1]{0,2,1:T(1,128)S(1)} %broadcast_in_dim.88), channel_id=1, replica_groups=mesh['group'=2,'batch'=4,'tensor'=4] {'tensor'}, dimensions={1} | all-to-all | bytes 256 | tf_op jit(solution)/shard_map/all_to_all | solution.py:77
  44.5 0.1 eq.12
  44.6 0.1 select_reduce_fusion
  44.7 2.3 %all-gather.3.cloned.1.call-done = bf16[16,1024,128]{2,1,0:T(8,128)(2,1)} async-done(((bf16[4,1024,128]{2,1,0:T(8,128)(2,1)}), bf16[16,1024,128]{2,1,0:T(8,128)(2,1)}) %all-gather.3.cloned.1.call-update) | async-done | bytes 4194320 | tf_op jit(solution)/shard_map/all_gather | solution.py:91
  47.0 3.0 %fusion.4 = bf16[32,128]{1,0:T(8,128)(2,1)S(1)} fusion(bf16[16,1024,128]{2,1,0:T(8,128)(2,1)} %all-gather.3.cloned.1.call-done, pred[32,16]{0,1:T(8,128)(4,1)S(1)} %iota_compare_fusion.1, bf16[8,4,1024]{2,0,1:T(8,128)(2,1)S(1)} %all_to_all.29), kind=kOutput, calls=%fused_computation.7 | convolution fusion | flops 134344704 | bytes 4268544 | tf_op jit(solution)/shard_map/rk,skj->rsj/dot_general | solution.py:96
  50.1 11.8 %psum.7 = bf16[32,128]{1,0:T(8,128)(2,1)S(1)} all-reduce(bf16[32,128]{1,0:T(8,128)(2,1)S(1)} %fusion.4), channel_id=1, replica_groups=mesh['group'=2,'batch'=4,'tensor'=4] {'tensor'}, use_global_device_ids=true, to_apply=%region_5.6 | all-reduce | flops 4096 | bytes 16384 | tf_op jit(solution)/shard_map/psum | solution.py:98
  61.9 0.1 select_convert_fusion
  62.0 44.9 %all-gather.5.cloned.1.call-done = bf16[16,128,2048]{2,1,0:T(8,128)(2,1)} async-done(((bf16[4,128,2048]{2,1,0:T(8,128)(2,1)}), bf16[16,128,2048]{2,1,0:T(8,128)(2,1)}) %all-gather.5.cloned.1.call-update) | async-done | bytes 8388624 | tf_op jit(solution)/shard_map/all_gather | solution.py:92
  106.9 5.6 %fusion.3 = bf16[32,2048]{1,0:T(8,128)(2,1)} fusion(bf16[16,128,2048]{2,1,0:T(8,128)(2,1)} %all-gather.5.cloned.1.call-done, bf16[32,2048]{1,0:T(8,128)(2,1)} %reduce-scatter.2.cloned.1.call-done, pred[32,16]{0,1:T(8,128)(4,1)S(1)} %iota_compare_fusion.1, bf16[32,128]{1,0:T(8,128)(2,1)S(1)} %select_convert_fusion), kind=kOutput, calls=%fused_computation.5 | convolution fusion | flops 268828672 | bytes 8659456 | tf_op jit(solution)/shard_map/dot_general | solution.py:103
  (15 shorter events, 0.2 us)
Async XLA Ops:
  7.4 3.2 %copy-start = (bf16[8,4,128,128]{3,2,1,0:T(8,128)(2,1)S(1)}, bf16[8,4,128,128]{3,2,1,0:T(8,128)(2,1)}, u32[]{:S(2)}) copy-start(bf16[8,4,128,128]{3,2,1,0:T(8,128)(2,1)} %param.14) | copy-start | bytes 3145732
  7.4 39.7 %all-gather.3.cloned.1.call-start = ((), (), s32[]{:S(2)}) async-start(), calls=%async_computation.4 | async-start | bytes 5242880 | tf_op jit(solution)/shard_map/all_gather | solution.py:91
  8.1 53.9 %reduce-scatter.2.cloned.1.call-start = ((), (), s32[]{:S(2)}) async-start(), calls=%async_computation.3 | async-start | bytes 655360 | tf_op jit(solution)/shard_map/reduce_scatter | solution.py:85
  26.0 10.5 %copy-start.1 = (s32[8]{0:T(128)S(1)}, s32[8]{0:T(128)}, u32[]{:S(2)}) copy-start(s32[8]{0:T(128)} %param.17) | copy-start | bytes 100
  26.0 18.5 %copy-start.2 = (s32[16]{0:T(128)S(1)}, s32[16]{0:T(128)}, u32[]{:S(2)}) copy-start(s32[16]{0:T(128)} %param.18) | copy-start | bytes 196
  35.8 71.1 %all-gather.5.cloned.1.call-start = ((), (), s32[]{:S(2)}) async-start(), calls=%async_computation.5 | async-start | bytes 10485760 | tf_op jit(solution)/shard_map/all_gather | solution.py:92
Sparse Core Ops, SparseCore 0:
  9.8 37.2 all-gather.2
  48.6 58.2 all-gather.4
Sparse Core Ops, SparseCore 1:
  35.8 20.0 reduce-scatter.1
where the time goes:
time: 120 us
  waiting for transfers between devices  48.7 us (41%)
  blocking collectives  31.6 us (26%)
  matrix products  22.6 us (19%)
  between operations  14.9 us (12%)
  other arithmetic  1.87 us (2%)
    all_gather x1, waiting for transfers between devices, per_device(): lax.all_gather(adapter_up_weight, 'batch', axis=0, tiled=True)  44.9 us
    all_to_all x1, blocking collectives, per_device(): lax.all_to_all(attention_result, 'tensor', split_axis=1, concat_axis=0, t...  11.9 us
    psum x1, blocking collectives, per_device(): lax.psum(low_share.astype(jnp.bfloat16), 'tensor').astype(jnp.float32)  11.8 us
    dot_general x1, matrix products, per_device(): jnp.dot(head_rows, output_weight, preferred_element_type=jnp.float32)  9.69 us
    all_to_all x1, blocking collectives, per_device(): lax.all_to_all(tiled_ids, 'tensor', split_axis=1, concat_axis=0, tiled=True)  7.94 us
    dot_general x1, matrix products, per_device(): jnp.dot(widened, up_all.reshape(slot_count * rank_span, -1), preferred_el...  5.65 us
    dot_general x1, matrix products, per_device(): jnp.einsum('rk,skj->rsj', head_rows, down_all, preferred_element_type=jnp...  3.04 us
  transfers between devices with their start and end apart: 3, of which 2 were waited for; matrix products, arithmetic and copies ran while one was open for 16% of the time, Pallas kernels for 0%

commit v1 on v0

v1 whole, which is shorter than its diff:
```python
import functools
import math

import jax
import jax.numpy as jnp
from jax import lax
from jax.experimental import pallas as pl
from jax.experimental.pallas import tpu as pltpu
from jax.sharding import PartitionSpec as P

ADAPTER_SCALE = 16.0
F32 = jnp.float32
BF16 = jnp.bfloat16
LANES = 128
MIB = 1024 * 1024


def params(grid_rank=0, vmem=24 * MIB):
    if grid_rank:
        return pltpu.CompilerParams(
            dimension_semantics=("arbitrary",) * grid_rank, vmem_limit_bytes=vmem
        )
    return pltpu.CompilerParams(vmem_limit_bytes=vmem)


def cost(flops, nbytes):
    return pl.CostEstimate(flops=flops, bytes_accessed=nbytes, transcendentals=0)


def sds(shape, dtype=BF16):
    return jax.ShapeDtypeStruct(shape, dtype)


def column_of(ref, count):
    rows = lax.broadcasted_iota(jnp.int32, (count, LANES), 0)
    out = jnp.full((count, LANES), ref[0], jnp.int32)
    for i in range(1, count):
        out = jnp.where(rows == i, ref[i], out)
    return out


def attend_kernel(place, length, adapter, q_ref, fk_ref, fv_ref, k_ref, v_ref, *outs):
    step = pl.program_id(0)
    requests, _, longest, dim = k_ref.shape
    group = q_ref.shape[1] // dim
    rows = group * requests
    scaling = 1.0 / math.sqrt(dim)
    q32 = q_ref[...].astype(F32)
    queries = jnp.concatenate([q32[:, h * dim : (h + 1) * dim] for h in range(group)], axis=0)
    keys = k_ref[...].reshape(requests * longest, dim)
    every = lax.dot_general(
        queries.astype(BF16), keys, (((1,), (1,)), ((), ())), preferred_element_type=F32
    )
    request = lax.rem(lax.broadcasted_iota(jnp.int32, (rows, longest), 0), requests)
    scores = every[:, :longest]
    for r in range(1, requests):
        scores = jnp.where(request == r, every[:, r * longest : (r + 1) * longest], scores)
    lengths = jnp.concatenate([column_of(length, requests)] * group, axis=0)
    valid = lax.broadcasted_iota(jnp.int32, (rows, longest), 1) < lengths
    scores = jnp.where(valid, scores * scaling, -1e30)
    fresh_key = jnp.concatenate([fk_ref[...].astype(F32)] * group, axis=0)
    fresh_value = jnp.concatenate([fv_ref[...].astype(F32)] * group, axis=0)
    own = jnp.sum(queries * fresh_key, axis=1, keepdims=True) * scaling
    highest = jnp.maximum(jnp.max(scores, axis=1, keepdims=True), own)
    exponent = jnp.where(valid, jnp.exp(scores - highest), 0.0)
    own_exp = jnp.exp(own - highest)
    total = jnp.sum(exponent, axis=1, keepdims=True) + own_exp
    weights = exponent / total
    own_weight = (own_exp / total).astype(BF16).astype(F32)
    spread = jnp.concatenate(
        [jnp.where(request == r, weights, 0.0) for r in range(requests)], axis=1
    ).astype(BF16)
    values = v_ref[...].reshape(requests * longest, dim)
    result = jnp.dot(spread, values, preferred_element_type=F32) + own_weight * fresh_value
    pieces = [result[h * requests : (h + 1) * requests] for h in range(group)]
    pieces.append(column_of(adapter, requests).astype(F32))
    block = jnp.concatenate(pieces, axis=1).astype(BF16)
    for i, out in enumerate(outs):

        @pl.when(step == i)
        def _(out=out):
            out[...] = block


def attend_blocks(place, length, adapter, query, fresh_key, fresh_value, keys, values):
    requests, kv, longest, dim = keys.shape
    width = query.shape[1] // kv

    def column(s, place, *_):
        return (0, jnp.bitwise_xor(place[0], s))

    def cache(s, place, *_):
        return (0, jnp.bitwise_xor(place[0], s), 0, 0)

    return pl.pallas_call(
        attend_kernel,
        grid_spec=pltpu.PrefetchScalarGridSpec(
            num_scalar_prefetch=3,
            grid=(kv,),
            in_specs=[
                pl.BlockSpec((requests, width), column),
                pl.BlockSpec((requests, dim), column),
                pl.BlockSpec((requests, dim), column),
                pl.BlockSpec((requests, 1, longest, dim), cache),
                pl.BlockSpec((requests, 1, longest, dim), cache),
            ],
            out_specs=[pl.BlockSpec((requests, width + LANES), lambda s, *_: (0, 0))] * kv,
        ),
        out_shape=[sds((requests, width + LANES))] * kv,
        compiler_params=params(1),
        cost_estimate=cost(2**28, 2 * keys.size * 2),
        name="attend",
    )(place, length, adapter, query, fresh_key, fresh_value, keys, values)


def route_kernel(place, x0, x1, x2, x3, rows_ref, pick_ref, c0, c1, c2, c3, held, *, local, cap):
    me, mine = place[0], place[1]
    count = x0.shape[0]
    for r, x in enumerate((x0, x1, x2, x3)):
        held[pl.ds(pl.multiple_of(jnp.bitwise_xor(me, r) * count, count), count), :] = x[
            ...
        ].astype(F32)
    every = held[...]
    packed = every.astype(BF16)
    rows, wide = every.shape
    width = wide - LANES
    rows_ref[...] = packed[:, :width]
    adapter = every[:, width:].astype(jnp.int32)
    lane = lax.broadcasted_iota(jnp.int32, (rows, LANES), 1)
    part, slot = lax.div(lane, cap), lax.rem(lane, cap)
    first = jnp.bitwise_xor(mine, part) * local
    held_there = (adapter >= first) & (adapter < first + local) & (part < 4)
    held_f = held_there.astype(F32)
    lower = lax.broadcasted_iota(jnp.int32, (rows, rows), 0) >= lax.broadcasted_iota(
        jnp.int32, (rows, rows), 1
    )
    place_in = jnp.dot(
        lower.astype(F32).astype(BF16), held_f.astype(BF16), preferred_element_type=F32
    )
    pick = jnp.where(held_there & (place_in == (slot + 1).astype(F32)), 1.0, 0.0).astype(BF16)
    pick_ref[...] = pick
    chosen = lax.dot_general(
        pick, packed, (((0,), (0,)), ((), ())), preferred_element_type=F32
    ).astype(BF16)
    for r, c in enumerate((c0, c1, c2, c3)):
        c[...] = chosen[r * cap : (r + 1) * cap]


def route(place, blocks, local, cap):
    count, wide = blocks[0].shape
    rows = count * len(blocks)
    smem = pl.BlockSpec(memory_space=pltpu.SMEM)
    vmem = pl.BlockSpec(memory_space=pltpu.VMEM)
    return pl.pallas_call(
        functools.partial(route_kernel, local=local, cap=cap),
        in_specs=[smem] + [vmem] * 4,
        out_specs=[vmem] * 6,
        out_shape=[sds((rows, wide - LANES)), sds((rows, LANES))] + [sds((cap, wide))] * 4,
        scratch_shapes=[pltpu.VMEM((rows, wide), F32)],
        compiler_params=params(),
        cost_estimate=cost(2**20, rows * wide * 8),
        name="route",
    )(place, *blocks)


def project_kernel(place, rows_ref, w_ref, *rest, add):
    step = pl.program_id(0)
    product = jnp.dot(rows_ref[...], w_ref[...], preferred_element_type=F32)
    if add:
        product = product + rest[0][...].astype(F32)
        rest = rest[1:]
    for i, out in enumerate(rest):

        @pl.when(step == i)
        def _(out=out):
            out[...] = product.astype(BF16)


def project(place, rows, weight, width, which, addend=None, tile=512):
    count, depth = rows.shape
    tiles = width // tile
    parts = len(which)

    def column(i, j, place):
        r = which[0] if parts == 1 else jnp.where(i == 0, which[0], which[1])
        return (0, jnp.bitwise_xor(place[0], r) * tiles + j)

    def target(k):
        return lambda i, j, place: (0, jnp.where(i < k, 0, jnp.where(i > k, tiles - 1, j)))

    in_specs = [
        pl.BlockSpec((count, depth), lambda i, j, place: (0, 0)),
        pl.BlockSpec((depth, tile), column),
    ]
    operands = [place, rows, weight]
    if addend is not None:
        in_specs.append(pl.BlockSpec((count, tile), lambda i, j, place: (0, j)))
        operands.append(addend)
    return pl.pallas_call(
        functools.partial(project_kernel, add=addend is not None),
        grid_spec=pltpu.PrefetchScalarGridSpec(
            num_scalar_prefetch=1,
            grid=(parts, tiles),
            in_specs=in_specs,
            out_specs=[pl.BlockSpec((count, tile), target(k)) for k in range(parts)],
        ),
        out_shape=[sds((count, width))] * parts,
        compiler_params=params(2),
        cost_estimate=cost(2 * count * depth * width * parts, depth * width * 2 * parts),
        name="project",
    )(*operands)


def down_kernel(place, c0, c1, c2, c3, down_ref, low_ref, slot_ref):
    local, width, rank = down_ref.shape
    chosen = jnp.concatenate([c[...] for c in (c0, c1, c2, c3)], axis=0)
    values = chosen[:, :width]
    slot = chosen[:, width:].astype(F32).astype(jnp.int32) - place[1] * local
    low = jnp.zeros((chosen.shape[0], rank), F32)
    for a in range(local):
        product = jnp.dot(values, down_ref[a], preferred_element_type=F32)
        low = jnp.where(slot == a, product, low)
    low_ref[...] = low.astype(BF16)
    slot_ref[...] = slot


def down(place, chosen, weight):
    local, width, rank = weight.shape
    rows = chosen[0].shape[0] * len(chosen)
    smem = pl.BlockSpec(memory_space=pltpu.SMEM)
    vmem = pl.BlockSpec(memory_space=pltpu.VMEM)
    return pl.pallas_call(
        down_kernel,
        in_specs=[smem] + [vmem] * 5,
        out_specs=[vmem] * 2,
        out_shape=[sds((rows, rank)), sds((rows, rank), jnp.int32)],
        compiler_params=params(),
        cost_estimate=cost(2 * rows * weight.size, weight.size * 2),
        name="down",
    )(place, *chosen, weight)


def up_kernel(place, ranks, l0, l1, l2, l3, slot_ref, up_ref, *outs):
    local = up_ref.shape[0]
    low = l0[...].astype(F32)
    for share in (l1, l2, l3):
        low = low + share[...].astype(F32)
    slot = slot_ref[...]
    lane = lax.broadcasted_iota(jnp.int32, low.shape, 1)
    total = None
    for a in range(local):
        rank = ranks[place[1] * local + a]
        factor = ADAPTER_SCALE / jnp.full(low.shape, rank, jnp.int32).astype(F32)
        kept = jnp.where((slot == a) & (lane < rank), low * factor, 0.0).astype(BF16)
        product = jnp.dot(kept, up_ref[a], preferred_element_type=F32)
        total = product if total is None else total + product
    adapted = total.astype(BF16)
    cap = outs[0].shape[0]
    for r, out in enumerate(outs):
        out[...] = adapted[r * cap : (r + 1) * cap]


def up(place, ranks, shares, slot, weight, parts, tile=512):
    local, rank, width = weight.shape
    rows = slot.shape[0]
    cap = rows // parts
    tiles = width // tile
    whole = pl.BlockSpec((rows, rank), lambda j, *_: (0, 0))
    return pl.pallas_call(
        up_kernel,
        grid_spec=pltpu.PrefetchScalarGridSpec(
            num_scalar_prefetch=2,
            grid=(tiles,),
            in_specs=[whole] * 5 + [pl.BlockSpec((local, rank, tile), lambda j, *_: (0, 0, j))],
            out_specs=[pl.BlockSpec((cap, tile), lambda j, *_: (0, j))] * parts,
        ),
        out_shape=[sds((cap, width))] * parts,
        compiler_params=params(1),
        cost_estimate=cost(2 * rows * weight.size, weight.size * 2),
        name="up",
    )(place, ranks, *shares, slot, weight)


def finish_kernel(pick_ref, y0, y1, y2, a0, a1, a2, a3, out):
    rows = jnp.concatenate([a[...] for a in (a0, a1, a2, a3)], axis=0)
    pick = pick_ref[...][:, : rows.shape[0]]
    adapted = jnp.dot(pick, rows, preferred_element_type=F32)
    base = y0[...].astype(F32) + y1[...].astype(F32) + y2[...].astype(F32)
    out[...] = (base + adapted).astype(BF16)


def finish(pick, shares, adapted):
    vmem = pl.BlockSpec(memory_space=pltpu.VMEM)
    return pl.pallas_call(
        finish_kernel,
        in_specs=[vmem] * 8,
        out_specs=vmem,
        out_shape=sds(shares[0].shape),
        compiler_params=params(),
        cost_estimate=cost(2**24, shares[0].size * 16),
        name="finish",
    )(pick, *shares, *adapted)


def across(value, axis, r):
    n = lax.axis_size(axis)
    return lax.ppermute(value, axis, [(i, i ^ r) for i in range(n)])


def per_device_four(
    query,
    fresh_key,
    fresh_value,
    stored_keys,
    stored_values,
    cached_length,
    request_adapter,
    rank_per_adapter,
    output_weight,
    adapter_down_weight,
    adapter_up_weight,
):
    tensor_count = lax.axis_size("tensor")
    batch_count = lax.axis_size("batch")
    local = adapter_down_weight.shape[0]
    width = adapter_up_weight.shape[2]
    requests = query.shape[0]
    cap = 2 * requests * tensor_count // batch_count
    place = jnp.stack([lax.axis_index("tensor"), lax.axis_index("batch")]).astype(jnp.int32)

    blocks = attend_blocks(
        place,
        cached_length,
        request_adapter,
        query,
        fresh_key,
        fresh_value,
        stored_keys,
        stored_values,
    )
    blocks = [blocks[0]] + [across(blocks[r], "tensor", r) for r in (1, 2, 3)]
    rows, pick, *chosen = route(place, blocks, local, cap)

    gathered = [chosen[0]] + [across(chosen[r], "batch", r) for r in (1, 2, 3)]
    far, near = project(place, rows, output_weight, width, (3, 1))
    far_in = across(far, "tensor", 1)
    near_in = across(near, "tensor", 1)

    low, slot = down(place, gathered, adapter_down_weight)
    shares = [low] + [across(low, "tensor", r) for r in (1, 2, 3)]
    (cross,) = project(place, rows, output_weight, width, (2,), addend=far_in)
    (mine,) = project(place, rows, output_weight, width, (0,))
    cross_in = across(cross, "tensor", 2)

    lifted = up(place, rank_per_adapter, shares, slot, adapter_up_weight, batch_count)
    lifted = [lifted[0]] + [across(lifted[r], "batch", r) for r in (1, 2, 3)]
    return finish(pick, (mine, near_in, cross_in), lifted)


def attend(query, fresh_key, fresh_value, stored_keys, stored_values, cached_length):
    requests = query.shape[0]
    kv_heads, longest, head_dim = stored_keys.shape[1:]
    group_size = query.shape[1] // (kv_heads * head_dim)
    queries = query.reshape(requests, kv_heads, group_size, head_dim)
    scaling = 1.0 / math.sqrt(head_dim)
    scores = (
        jnp.einsum("rkgd,rkld->rkgl", queries, stored_keys, preferred_element_type=F32) * scaling
    )
    own_score = (
        jnp.einsum(
            "rkgd,rkd->rkg",
            queries,
            fresh_key.reshape(requests, kv_heads, head_dim),
            preferred_element_type=F32,
        )
        * scaling
    )
    valid = (jnp.arange(longest, dtype=jnp.int32)[None, :] < cached_length[:, None])[
        :, None, None, :
    ]
    scores = jnp.where(valid, scores, -1e30)
    highest = jnp.maximum(jnp.max(scores, axis=-1), own_score)
    exponent = jnp.where(valid, jnp.exp(scores - highest[..., None]), 0.0)
    own_exp = jnp.exp(own_score - highest)
    sum_exp = jnp.sum(exponent, axis=-1) + own_exp
    weights = (exponent / sum_exp[..., None]).astype(BF16)
    own_weight = (own_exp / sum_exp).astype(BF16)
    result = jnp.einsum("rkgl,rkld->rkgd", weights, stored_values, preferred_element_type=F32)
    own_value = fresh_value.reshape(requests, kv_heads, 1, head_dim).astype(F32)
    result = result + own_weight.astype(F32)[..., None] * own_value
    return result.reshape(requests, -1).astype(BF16)


def per_device_any(
    query,
    fresh_key,
    fresh_value,
    stored_keys,
    stored_values,
    cached_length,
    request_adapter,
    rank_per_adapter,
    output_weight,
    adapter_down_weight,
    adapter_up_weight,
):
    attended = attend(query, fresh_key, fresh_value, stored_keys, stored_values, cached_length)
    batch_count = lax.axis_size("batch")
    local, _, rank_span = adapter_down_weight.shape
    head_rows = lax.all_to_all(attended, "tensor", split_axis=1, concat_axis=0, tiled=True)
    row_count = head_rows.shape[0]
    products = jnp.dot(head_rows, output_weight, preferred_element_type=F32)
    base = lax.psum_scatter(
        products.astype(BF16), "tensor", scatter_dimension=1, tiled=True
    ).astype(F32)
    all_rows = lax.all_gather(head_rows, "batch", axis=0, tiled=True)
    ids = lax.all_gather(request_adapter, ("batch", "tensor"), axis=0, tiled=True)
    slot = ids - lax.axis_index("batch") * local
    one_hot = slot[:, None] == jnp.arange(local, dtype=jnp.int32)[None, :]
    low_every = jnp.einsum("rk,skj->rsj", all_rows, adapter_down_weight, preferred_element_type=F32)
    low = jnp.sum(jnp.where(one_hot[:, :, None], low_every, 0.0), axis=1)
    low = lax.psum(low.astype(BF16), "tensor").astype(F32)
    adapter_count = rank_per_adapter.shape[0]
    picked = ids[:, None] == jnp.arange(adapter_count, dtype=jnp.int32)[None, :]
    row_rank = jnp.sum(jnp.where(picked, rank_per_adapter[None, :], 0), axis=1)[:, None]
    kept = jnp.arange(rank_span, dtype=jnp.int32)[None, :] < row_rank
    delta = jnp.where(kept, low * (ADAPTER_SCALE / row_rank.astype(F32)), 0.0).astype(BF16)
    widened = jnp.where(one_hot[:, :, None], delta[:, None, :], jnp.zeros((), BF16))
    adapted = jnp.dot(
        widened.reshape(ids.shape[0], local * rank_span),
        adapter_up_weight.reshape(local * rank_span, -1),
        preferred_element_type=F32,
    ).astype(BF16)
    adapted = lax.all_to_all(
        adapted.reshape(batch_count, row_count, -1), "batch", split_axis=0, concat_axis=0, tiled=True
    )
    adapted = jnp.sum(adapted.astype(F32), axis=0)
    return (base + adapted).astype(BF16)


def solution(mesh):
    in_specs = (
        P(("group", "batch", "tensor"), None),
        P(("group", "batch", "tensor"), None),
        P(("group", "batch", "tensor"), None),
        P(("group", "batch", "tensor"), None, None, None),
        P(("group", "batch", "tensor"), None, None, None),
        P(("group", "batch", "tensor")),
        P(("group", "batch", "tensor")),
        P(),
        P("tensor", None),
        P("batch", "tensor", None),
        P("batch", None, "tensor"),
    )
    out_specs = P(("group", "batch"), "tensor")

    def whole(*arrays):
        tensor_count, batch_count = mesh.shape["tensor"], mesh.shape["batch"]
        four = tensor_count == batch_count == arrays[3].shape[1] == 4
        body = per_device_four if four else per_device_any
        return jax.shard_map(
            body, mesh=mesh, in_specs=in_specs, out_specs=out_specs, check_vma=False
        )(*arrays)

    return whole
```

time: 120 us -> 56 us (0.47)
  waiting for transfers between devices: 48.7 us -> 13.2 us
  blocking collectives: 31.6 us -> 0 us
  matrix products: 22.6 us -> 0 us
  Pallas kernels: 0 us -> 15.3 us
  starting transfers between devices: 0.09 us -> 15.2 us
  between operations: 14.9 us -> 0.18 us
  local copies, waits for them, and re-layouts: 0.18 us -> 11.8 us
  other arithmetic: 1.87 us -> 0.08 us
    all_gather x2 -> x0, waiting for transfers between devices: 47.3 us -> none  [the longest x1 44.9 us: per_device(): lax.all_gather(adapter_up_weight, 'batch', axis=0, tiled=True)]
    dot_general x6 -> x0, matrix products: 22.6 us -> none  [the longest x1 9.69 us: per_device(): jnp.dot(head_rows, output_weight, preferred_element_type=jnp.float32)]
    all_to_all x2 -> x0, blocking collectives: 19.8 us -> none  [the longest x1 11.9 us: per_device(): lax.all_to_all(attention_result, 'tensor', split_axis=1, concat_axis=0, t...]
    pallas_call x0 -> x8, Pallas kernels: none -> 15.3 us  [the longest x3 8 us: project(): pl.pallas_call(functools.partial(project_kernel, add=addend is not None),...]
    ppermute x0 -> x15, starting transfers between devices: none -> 15.2 us  [across(): return lax.ppermute(value, axis, [(i, i ^ r) for i in range(n)])]
    ppermute x0 -> x15, waiting for transfers between devices: none -> 13.2 us  [across(): return lax.ppermute(value, axis, [(i, i ^ r) for i in range(n)])]
    psum x1 -> x0, blocking collectives: 11.8 us -> none  [per_device(): lax.psum(low_share.astype(jnp.bfloat16), 'tensor').astype(jnp.float32)]
    unnamed x6 -> x30, local copies, waits for them, and re-layouts: 0.01 us -> 11.8 us
  transfers between devices with their start and end apart: 3 -> 15, of which waited for: 2 -> 7; matrix products, arithmetic and copies ran while one was open for 16% -> 0% of each run, Pallas kernels for 0% -> 12%
where the time goes in v1:
time: 56 us; the launch traced here: 55.7 us
  Pallas kernels  15.3 us (27%)
  starting transfers between devices  15.2 us (27%)
  waiting for transfers between devices  13.2 us (24%)
  local copies, waits for them, and re-layouts  11.8 us (21%)
    ppermute x15, starting transfers between devices, across(): return lax.ppermute(value, axis, [(i, i ^ r) for i in range(n)])  15.2 us
    ppermute x15, waiting for transfers between devices, across(): return lax.ppermute(value, axis, [(i, i ^ r) for i in range(n)])  13.2 us
    unnamed x30, local copies, waits for them, and re-layouts  11.8 us
    pallas_call x3, Pallas kernels, project(): pl.pallas_call(functools.partial(project_kernel, add=addend is not None),...  8 us
    pallas_call x1, Pallas kernels, attend_blocks(): pl.pallas_call(attend_kernel, grid_spec=pltpu.PrefetchScalarGridSpec(num_...  2.97 us
    pallas_call x1, Pallas kernels, up(): pl.pallas_call(up_kernel, grid_spec=pltpu.PrefetchScalarGridSpec(num_scal...  1.68 us
  transfers between devices with their start and end apart: 15, of which 7 were waited for; matrix products, arithmetic and copies ran while one was open for 0% of the time, Pallas kernels for 12%

profile of v1, /device:TPU:0, one launch (start us, length us, event | category | flops | bytes accessed | tf_op | source)
XLA Modules:
  0.0 55.7 jit_solution(18044866255976601380)
XLA Ops:
  0.1 1.2 %copy-done.2 = bf16[8,4,128,128]{3,2,1,0:T(8,128)(2,1)S(1)} copy-done((bf16[8,4,128,128]{3,2,1,0:T(8,128)(2,1)S(1)}, bf16[8,4,128,128]{3,2,1,0:T(8,128)(2,1)}, u32[]{:S(2)}) %copy-start.2) | copy-done | bytes 1048600
  1.3 1.2 %copy-done.3 = bf16[8,4,128,128]{3,2,1,0:T(8,128)(2,1)S(1)} copy-done((bf16[8,4,128,128]{3,2,1,0:T(8,128)(2,1)S(1)}, bf16[8,4,128,128]{3,2,1,0:T(8,128)(2,1)}, u32[]{:S(2)}) %copy-start.3) | copy-done | bytes 1048600
  2.5 0.8 %copy-done.5 = bf16[8,4096]{1,0:T(8,128)(2,1)S(1)} copy-done((bf16[8,4096]{1,0:T(8,128)(2,1)S(1)}, bf16[8,4096]{1,0:T(8,128)(2,1)}, u32[]{:S(2)}) %copy-start.5) | copy-done | bytes 65560
  3.4 0.7 %copy-done.6 = bf16[8,512]{1,0:T(8,128)(2,1)S(1)} copy-done((bf16[8,512]{1,0:T(8,128)(2,1)S(1)}, bf16[8,512]{1,0:T(8,128)(2,1)}, u32[]{:S(2)}) %copy-start.6) | copy-done | bytes 8216
  6.1 3.0 %attend.1 = (bf16[8,1152]{1,0:T(8,128)(2,1)S(1)}, bf16[8,1152]{1,0:T(8,128)(2,1)S(1)}, bf16[8,1152]{1,0:T(8,128)(2,1)S(1)}, bf16[8,1152]{1,0:T(8,128)(2,1)S(1)}) custom-call(s32[2]{0:T(128)S(1)} %pad_add_fusion.place, s32[8]{0:T(128)S(1)} %copy-done.8, s32[8]{0:T(128)S(1)} %copy-done.9, bf16[8,4096]{1,0:T(8,128)(2,1)S(1)} %copy-done.5, ...), custom_call_target="tpu_custom_call" | custom-call | flops 268435456 | bytes 2097152 | tf_op jit(solution)/shard_map/attend/pallas_call | solution.py:95
  9.0 3.1 %collective-permute-start = (bf16[8,1152]{1,0:T(8,128)(2,1)S(1)}, bf16[8,1152]{1,0:T(8,128)(2,1)S(1)}, u32[]{:S(2)}, u32[]{:S(2)}) collective-permute-start(bf16[8,1152]{1,0:T(8,128)(2,1)S(1)} %get-tuple-element.24), channel_id=1, source_target_pairs={{0,1},{1,0},{2,3},{3,2},{4,5},{5,4},{6,7},{7,6},{8,9},{9,8},{10,11... | collective-permute-start | bytes 55304 | tf_op jit(solution)/shard_map/ppermute | solution.py:307
  12.1 2.6 %collective-permute-start.1 = (bf16[8,1152]{1,0:T(8,128)(2,1)S(1)}, bf16[8,1152]{1,0:T(8,128)(2,1)S(1)}, u32[]{:S(2)}, u32[]{:S(2)}) collective-permute-start(bf16[8,1152]{1,0:T(8,128)(2,1)S(1)} %get-tuple-element.25), channel_id=1, source_target_pairs={{0,2},{1,3},{2,0},{3,1},{4,6},{5,7},{6,4},{7,5},{8,10},{9,11},{10,... | collective-permute-start | bytes 55304 | tf_op jit(solution)/shard_map/ppermute | solution.py:307
  14.7 2.2 %collective-permute-done.1.x2 = bf16[8,1152]{1,0:T(8,128)(2,1)S(1)} collective-permute-done((bf16[8,1152]{1,0:T(8,128)(2,1)S(1)}, bf16[8,1152]{1,0:T(8,128)(2,1)S(1)}, u32[]{:S(2)}, u32[]{:S(2)}) %collective-permute-start.1) | collective-permute-done | bytes 18464 | tf_op jit(solution)/shard_map/ppermute | solution.py:307
  16.9 3.3 %collective-permute-done.2.x3 = bf16[8,1152]{1,0:T(8,128)(2,1)S(1)} collective-permute-done((bf16[8,1152]{1,0:T(8,128)(2,1)S(1)}, bf16[8,1152]{1,0:T(8,128)(2,1)S(1)}, u32[]{:S(2)}, u32[]{:S(2)}) %collective-permute-start.2) | collective-permute-done | bytes 18464 | tf_op jit(solution)/shard_map/ppermute | solution.py:307
  20.3 0.9 %route.1 = (bf16[32,1024]{1,0:T(8,128)(2,1)S(1)}, bf16[32,128]{1,0:T(8,128)(2,1)S(1)}, bf16[16,1152]{1,0:T(8,128)(2,1)S(1)}, bf16[16,1152]{1,0:T(8,128)(2,1)S(1)...) custom-call(s32[2]{0:T(128)S(1)} %pad_add_fusion.place, bf16[8,1152]{1,0:T(8,128)(2,1)S(1)} %get-tuple-element.23.x0, ...), custom_call_target="tpu_custom_call" | custom-call | flops 1048576 | bytes 294912 | tf_op jit(solution)/shard_map/route/pallas_call | solution.py:154
  21.3 5.8 %copy-done = bf16[1024,8192]{1,0:T(8,128)(2,1)S(1)} copy-done((bf16[1024,8192]{1,0:T(8,128)(2,1)S(1)}, bf16[1024,8192]{1,0:T(8,128)(2,1)}, u32[]{:S(2)}) %copy-start) | copy-done | bytes 16777240
  27.0 3.8 %project.4 = (bf16[32,2048]{1,0:T(8,128)(2,1)S(1)}, bf16[32,2048]{1,0:T(8,128)(2,1)S(1)}) custom-call(s32[2]{0:T(128)S(1)} %pad_add_fusion.place, bf16[32,1024]{1,0:T(8,128)(2,1)S(1)} %get-tuple-element.28.rows_ref, bf16[1024,8192]{1,0:T(8,128)(2,1)S(1)} %copy-done), custom_call_target="tpu_custom_call" | custom-call | flops 268435456 | bytes 8388608 | tf_op jit(solution)/shard_map/project/pallas_call | solution.py:199
  31.0 1.6 %collective-permute-start.7 = (bf16[16,1152]{1,0:T(8,128)(2,1)S(1)}, bf16[16,1152]{1,0:T(8,128)(2,1)S(1)}, u32[]{:S(2)}, u32[]{:S(2)}) collective-permute-start(bf16[16,1152]{1,0:T(8,128)(2,1)S(1)} %get-tuple-element.33), channel_id=1, source_target_pairs={{0,8},{4,12},{8,0},{12,4},{1,9},{5,13},{9,1},{13,5},{2,10},{6,14},... | collective-permute-start | bytes 110600 | tf_op jit(solution)/shard_map/ppermute | solution.py:307
  32.8 1.9 %collective-permute-start.3 = (bf16[32,2048]{1,0:T(8,128)(2,1)S(1)}, bf16[32,2048]{1,0:T(8,128)(2,1)S(1)}, u32[]{:S(2)}, u32[]{:S(2)}) collective-permute-start(bf16[32,2048]{1,0:T(8,128)(2,1)S(1)} %get-tuple-element.29), channel_id=1, source_target_pairs={{0,1},{1,0},{2,3},{3,2},{4,5},{5,4},{6,7},{7,6},{8,9},{9,8},{10,11... | collective-permute-start | bytes 393224 | tf_op jit(solution)/shard_map/ppermute | solution.py:307
  34.8 1.1 %collective-permute-done.4.rest_0_ = bf16[32,2048]{1,0:T(8,128)(2,1)S(1)} collective-permute-done((bf16[32,2048]{1,0:T(8,128)(2,1)S(1)}, bf16[32,2048]{1,0:T(8,128)(2,1)S(1)}, u32[]{:S(2)}, u32[]{:S(2)}) %collective-permute-start.4) | collective-permute-done | bytes 131104 | tf_op jit(solution)/shard_map/ppermute | solution.py:307
  35.8 2.2 %project.5 = bf16[32,2048]{1,0:T(8,128)(2,1)S(1)} custom-call(s32[2]{0:T(128)S(1)} %pad_add_fusion.place, bf16[32,1024]{1,0:T(8,128)(2,1)S(1)} %get-tuple-element.28.rows_ref, bf16[1024,8192]{1,0:T(8,128)(2,1)S(1)} %copy-done, bf16[32,2048]{1,0:T(8,128)(2,1)S(1)} %collective-permute-done.4.rest_0_), custom_call_target="tpu_custom_call" | custom-call | flops 134217728 | bytes 4194304 | tf_op jit(solution)/shard_map/project/pallas_call | solution.py:199
  38.1 0.8 %down.1 = (bf16[64,128]{1,0:T(8,128)(2,1)S(1)}, s32[64,128]{1,0:T(8,128)S(1)}) custom-call(s32[2]{0:T(128)S(1)} %pad_add_fusion.place, bf16[16,1152]{1,0:T(8,128)(2,1)S(1)} %get-tuple-element.31.c0, bf16[16,1152]{1,0:T(8,128)(2,1)S(1)} %collective-permute-done.6.c1, bf16[16,1152]{1,0:T(8,128)(2,1)S(1)} %collective-permute-done.7.c2, ...), custom_call_target="tpu_custom_call" | custom-call | flops 67108864 | bytes 1048576 | tf_op jit(solution)/shard_map/down/pallas_call | solution.py:232
  39.0 3.0 %collective-permute-start.10 = (bf16[64,128]{1,0:T(8,128)(2,1)S(1)}, bf16[64,128]{1,0:T(8,128)(2,1)S(1)}, u32[]{:S(2)}, u32[]{:S(2)}) collective-permute-start(bf16[64,128]{1,0:T(8,128)(2,1)S(1)} %get-tuple-element.35.l0), channel_id=1, source_target_pairs={{0,2},{1,3},{2,0},{3,1},{4,6},{5,7},{6,4},{7,5},{8,10},{9,11},{10,... | collective-permute-start | bytes 49160 | tf_op jit(solution)/shard_map/ppermute | solution.py:307
  42.6 4.3 %collective-permute-done.10.l2 = bf16[64,128]{1,0:T(8,128)(2,1)S(1)} collective-permute-done((bf16[64,128]{1,0:T(8,128)(2,1)S(1)}, bf16[64,128]{1,0:T(8,128)(2,1)S(1)}, u32[]{:S(2)}, u32[]{:S(2)}) %collective-permute-start.10) | collective-permute-done | bytes 16416 | tf_op jit(solution)/shard_map/ppermute | solution.py:307
  47.5 1.7 %up.1 = (bf16[16,2048]{1,0:T(8,128)(2,1)S(1)}, bf16[16,2048]{1,0:T(8,128)(2,1)S(1)}, bf16[16,2048]{1,0:T(8,128)(2,1)S(1)}, bf16[16,2048]{1,0:T(8,128)(2,1)S(1)}) custom-call(s32[2]{0:T(128)S(1)} %pad_add_fusion.place, s32[16]{0:T(128)S(1)} %copy-done.10, bf16[64,128]{1,0:T(8,128)(2,1)S(1)} %get-tuple-element.35.l0, ...), custom_call_target="tpu_custom_call" | custom-call | flops 134217728 | bytes 2097152 | tf_op jit(solution)/shard_map/up/pallas_call | solution.py:269
  49.2 1.6 %collective-permute-start.13 = (bf16[16,2048]{1,0:T(8,128)(2,1)S(1)}, bf16[16,2048]{1,0:T(8,128)(2,1)S(1)}, u32[]{:S(2)}, u32[]{:S(2)}) collective-permute-start(bf16[16,2048]{1,0:T(8,128)(2,1)S(1)} %get-tuple-element.39), channel_id=1, source_target_pairs={{0,8},{4,12},{8,0},{12,4},{1,9},{5,13},{9,1},{13,5},{2,10},{6,14},... | collective-permute-start | bytes 196616 | tf_op jit(solution)/shard_map/ppermute | solution.py:307
  51.1 2.1 %project.3.y0 = bf16[32,2048]{1,0:T(8,128)(2,1)S(1)} custom-call(s32[2]{0:T(128)S(1)} %pad_add_fusion.place, bf16[32,1024]{1,0:T(8,128)(2,1)S(1)} %get-tuple-element.28.rows_ref, bf16[1024,8192]{1,0:T(8,128)(2,1)S(1)} %bitcast.3), custom_call_target="tpu_custom_call" | custom-call | flops 134217728 | bytes 4194304 | tf_op jit(solution)/shard_map/project/pallas_call | solution.py:199
  53.7 1.1 %collective-permute-done.14.a3 = bf16[16,2048]{1,0:T(8,128)(2,1)S(1)} collective-permute-done((bf16[16,2048]{1,0:T(8,128)(2,1)S(1)}, bf16[16,2048]{1,0:T(8,128)(2,1)S(1)}, u32[]{:S(2)}, u32[]{:S(2)}) %collective-permute-start.14) | collective-permute-done | bytes 65568 | tf_op jit(solution)/shard_map/ppermute | solution.py:307
  54.8 0.8 %finish.1 = bf16[32,2048]{1,0:T(8,128)(2,1)} custom-call(bf16[32,128]{1,0:T(8,128)(2,1)S(1)} %get-tuple-element.27.pick_ref, bf16[32,2048]{1,0:T(8,128)(2,1)S(1)} %project.3.y0, bf16[32,2048]{1,0:T(8,128)(2,1)S(1)} %collective-permute-done.3.y1, bf16[32,2048]{1,0:T(8,128)(2,1)S(1)} %collective-permute-done.5.y2, bf16[16,2048]{1,0:T(8,128)(2,1)S(1)} %get-tuple-element.37.a0, ...), custom_call_target="tpu_custom_call" | custom-call | flops 16777216 | bytes 1048576 | tf_op jit(solution)/shard_map/finish/pallas_call | solution.py:294
  (46 shorter events, 4.8 us)
Async XLA Ops:
  0.1 1.2 %copy-start.2 = (bf16[8,4,128,128]{3,2,1,0:T(8,128)(2,1)S(1)}, bf16[8,4,128,128]{3,2,1,0:T(8,128)(2,1)}, u32[]{:S(2)}) copy-start(bf16[8,4,128,128]{3,2,1,0:T(8,128)(2,1)} %k_ref.1) | copy-start | bytes 3145732
  9.0 5.7 %collective-permute-start = (bf16[8,1152]{1,0:T(8,128)(2,1)S(1)}, bf16[8,1152]{1,0:T(8,128)(2,1)S(1)}, u32[]{:S(2)}, u32[]{:S(2)}) collective-permute-start(bf16[8,1152]{1,0:T(8,128)(2,1)S(1)} %get-tuple-element.24), channel_id=1, source_target_pairs={{0,1},{1,0},{2,3},{3,2},{4,5},{5,4},{6,7},{7,6},{8,9},{9,8},{10,11... | collective-permute-start | bytes 55304 | tf_op jit(solution)/shard_map/ppermute | solution.py:307
  12.1 4.8 %collective-permute-start.1 = (bf16[8,1152]{1,0:T(8,128)(2,1)S(1)}, bf16[8,1152]{1,0:T(8,128)(2,1)S(1)}, u32[]{:S(2)}, u32[]{:S(2)}) collective-permute-start(bf16[8,1152]{1,0:T(8,128)(2,1)S(1)} %get-tuple-element.25), channel_id=1, source_target_pairs={{0,2},{1,3},{2,0},{3,1},{4,6},{5,7},{6,4},{7,5},{8,10},{9,11},{10,... | collective-permute-start | bytes 55304 | tf_op jit(solution)/shard_map/ppermute | solution.py:307
  14.7 5.6 %collective-permute-start.2 = (bf16[8,1152]{1,0:T(8,128)(2,1)S(1)}, bf16[8,1152]{1,0:T(8,128)(2,1)S(1)}, u32[]{:S(2)}, u32[]{:S(2)}) collective-permute-start(bf16[8,1152]{1,0:T(8,128)(2,1)S(1)} %get-tuple-element.26), channel_id=1, source_target_pairs={{0,3},{1,2},{2,1},{3,0},{4,7},{5,6},{6,5},{7,4},{8,11},{9,10},{10,... | collective-permute-start | bytes 55304 | tf_op jit(solution)/shard_map/ppermute | solution.py:307
  21.2 5.8 %copy-start = (bf16[1024,8192]{1,0:T(8,128)(2,1)S(1)}, bf16[1024,8192]{1,0:T(8,128)(2,1)}, u32[]{:S(2)}) copy-start(bf16[1024,8192]{1,0:T(8,128)(2,1)} %w_ref.5) | copy-start | bytes 50331652
  27.0 11.1 %copy-start.4 = (bf16[4,1024,128]{2,1,0:T(8,128)(2,1)S(1)}, bf16[4,1024,128]{2,1,0:T(8,128)(2,1)}, u32[]{:S(2)}) copy-start(bf16[4,1024,128]{2,1,0:T(8,128)(2,1)} %down_ref.1) | copy-start | bytes 3145732
  27.0 20.5 %copy-start.1 = (bf16[4,128,2048]{2,1,0:T(8,128)(2,1)S(1)}, bf16[4,128,2048]{2,1,0:T(8,128)(2,1)}, u32[]{:S(2)}) copy-start(bf16[4,128,2048]{2,1,0:T(8,128)(2,1)} %up_ref.1) | copy-start | bytes 6291460
  27.0 20.5 %copy-start.10 = (s32[16]{0:T(128)S(1)}, s32[16]{0:T(128)}, u32[]{:S(2)}) copy-start(s32[16]{0:T(128)} %ranks.1) | copy-start | bytes 196
  27.0 24.1 %slice-start = ((s8[16777216]{0:T(1024)(128)(4,1)}), s8[4194304]{0:T(1024)(128)(4,1)S(1)}, s32[]{:S(2)}) async-start(s8[16777216]{0:T(1024)(128)(4,1)} %bitcast.2), calls=%async_computation | async-start | bytes 8388608
  27.0 24.1 %slice-start.1 = ((s8[16777216]{0:T(1024)(128)(4,1)}), s8[4194304]{0:T(1024)(128)(4,1)S(1)}, s32[]{:S(2)}) async-start(s8[16777216]{0:T(1024)(128)(4,1)} %bitcast.2), calls=%async_computation.1 | async-start | bytes 8388608
  30.8 5.0 %collective-permute-start.4 = (bf16[32,2048]{1,0:T(8,128)(2,1)S(1)}, bf16[32,2048]{1,0:T(8,128)(2,1)S(1)}, u32[]{:S(2)}, u32[]{:S(2)}) collective-permute-start(bf16[32,2048]{1,0:T(8,128)(2,1)S(1)} %get-tuple-element.30), channel_id=1, source_target_pairs={{0,1},{1,0},{2,3},{3,2},{4,5},{5,4},{6,7},{7,6},{8,9},{9,8},{10,11... | collective-permute-start | bytes 393224 | tf_op jit(solution)/shard_map/ppermute | solution.py:307
  30.9 7.2 %collective-permute-start.6 = (bf16[16,1152]{1,0:T(8,128)(2,1)S(1)}, bf16[16,1152]{1,0:T(8,128)(2,1)S(1)}, u32[]{:S(2)}, u32[]{:S(2)}) collective-permute-start(bf16[16,1152]{1,0:T(8,128)(2,1)S(1)} %get-tuple-element.32), channel_id=1, source_target_pairs={{0,4},{4,0},{8,12},{12,8},{1,5},{5,1},{9,13},{13,9},{2,6},{6,2},{1... | collective-permute-start | bytes 110600 | tf_op jit(solution)/shard_map/ppermute | solution.py:307
  31.0 7.1 %collective-permute-start.7 = (bf16[16,1152]{1,0:T(8,128)(2,1)S(1)}, bf16[16,1152]{1,0:T(8,128)(2,1)S(1)}, u32[]{:S(2)}, u32[]{:S(2)}) collective-permute-start(bf16[16,1152]{1,0:T(8,128)(2,1)S(1)} %get-tuple-element.33), channel_id=1, source_target_pairs={{0,8},{4,12},{8,0},{12,4},{1,9},{5,13},{9,1},{13,5},{2,10},{6,14},... | collective-permute-start | bytes 110600 | tf_op jit(solution)/shard_map/ppermute | solution.py:307
  32.5 5.6 %collective-permute-start.8 = (bf16[16,1152]{1,0:T(8,128)(2,1)S(1)}, bf16[16,1152]{1,0:T(8,128)(2,1)S(1)}, u32[]{:S(2)}, u32[]{:S(2)}) collective-permute-start(bf16[16,1152]{1,0:T(8,128)(2,1)S(1)} %get-tuple-element.34), channel_id=1, source_target_pairs={{0,12},{4,8},{8,4},{12,0},{1,13},{5,9},{9,5},{13,1},{2,14},{6,10},... | collective-permute-start | bytes 110600 | tf_op jit(solution)/shard_map/ppermute | solution.py:307
  32.8 18.3 %slice-start.2 = ((s8[16777216]{0:T(1024)(128)(4,1)}), s8[4194304]{0:T(1024)(128)(4,1)S(1)}, s32[]{:S(2)}) async-start(s8[16777216]{0:T(1024)(128)(4,1)} %bitcast.2), calls=%async_computation.2 | async-start | bytes 8388608
  32.8 18.3 %slice-start.3 = ((s8[16777216]{0:T(1024)(128)(4,1)}), s8[4194304]{0:T(1024)(128)(4,1)S(1)}, s32[]{:S(2)}) async-start(s8[16777216]{0:T(1024)(128)(4,1)} %bitcast.2), calls=%async_computation.3 | async-start | bytes 8388608
  32.8 22.0 %collective-permute-start.3 = (bf16[32,2048]{1,0:T(8,128)(2,1)S(1)}, bf16[32,2048]{1,0:T(8,128)(2,1)S(1)}, u32[]{:S(2)}, u32[]{:S(2)}) collective-permute-start(bf16[32,2048]{1,0:T(8,128)(2,1)S(1)} %get-tuple-element.29), channel_id=1, source_target_pairs={{0,1},{1,0},{2,3},{3,2},{4,5},{5,4},{6,7},{7,6},{8,9},{9,8},{10,11... | collective-permute-start | bytes 393224 | tf_op jit(solution)/shard_map/ppermute | solution.py:307
  38.0 16.8 %collective-permute-start.5 = (bf16[32,2048]{1,0:T(8,128)(2,1)S(1)}, bf16[32,2048]{1,0:T(8,128)(2,1)S(1)}, u32[]{:S(2)}, u32[]{:S(2)}) collective-permute-start(bf16[32,2048]{1,0:T(8,128)(2,1)S(1)} %project.5), channel_id=1, source_target_pairs={{0,2},{1,3},{2,0},{3,1},{4,6},{5,7},{6,4},{7,5},{8,10},{9,11},{10,... | collective-permute-start | bytes 393224 | tf_op jit(solution)/shard_map/ppermute | solution.py:307
  39.0 7.9 %collective-permute-start.10 = (bf16[64,128]{1,0:T(8,128)(2,1)S(1)}, bf16[64,128]{1,0:T(8,128)(2,1)S(1)}, u32[]{:S(2)}, u32[]{:S(2)}) collective-permute-start(bf16[64,128]{1,0:T(8,128)(2,1)S(1)} %get-tuple-element.35.l0), channel_id=1, source_target_pairs={{0,2},{1,3},{2,0},{3,1},{4,6},{5,7},{6,4},{7,5},{8,10},{9,11},{10,... | collective-permute-start | bytes 49160 | tf_op jit(solution)/shard_map/ppermute | solution.py:307
  41.9 5.5 %collective-permute-start.11 = (bf16[64,128]{1,0:T(8,128)(2,1)S(1)}, bf16[64,128]{1,0:T(8,128)(2,1)S(1)}, u32[]{:S(2)}, u32[]{:S(2)}) collective-permute-start(bf16[64,128]{1,0:T(8,128)(2,1)S(1)} %get-tuple-element.35.l0), channel_id=1, source_target_pairs={{0,3},{1,2},{2,1},{3,0},{4,7},{5,6},{6,5},{7,4},{8,11},{9,10},{10,... | collective-permute-start | bytes 49160 | tf_op jit(solution)/shard_map/ppermute | solution.py:307
  42.1 5.3 %collective-permute-start.9 = (bf16[64,128]{1,0:T(8,128)(2,1)S(1)}, bf16[64,128]{1,0:T(8,128)(2,1)S(1)}, u32[]{:S(2)}, u32[]{:S(2)}) collective-permute-start(bf16[64,128]{1,0:T(8,128)(2,1)S(1)} %get-tuple-element.35.l0), channel_id=1, source_target_pairs={{0,1},{1,0},{2,3},{3,2},{4,5},{5,4},{6,7},{7,6},{8,9},{9,8},{10,11... | collective-permute-start | bytes 49160 | tf_op jit(solution)/shard_map/ppermute | solution.py:307
  49.2 4.1 %collective-permute-start.12 = (bf16[16,2048]{1,0:T(8,128)(2,1)S(1)}, bf16[16,2048]{1,0:T(8,128)(2,1)S(1)}, u32[]{:S(2)}, u32[]{:S(2)}) collective-permute-start(bf16[16,2048]{1,0:T(8,128)(2,1)S(1)} %get-tuple-element.38), channel_id=1, source_target_pairs={{0,4},{4,0},{8,12},{12,8},{1,5},{5,1},{9,13},{13,9},{2,6},{6,2},{1... | collective-permute-start | bytes 196616 | tf_op jit(solution)/shard_map/ppermute | solution.py:307
  49.2 4.5 %collective-permute-start.13 = (bf16[16,2048]{1,0:T(8,128)(2,1)S(1)}, bf16[16,2048]{1,0:T(8,128)(2,1)S(1)}, u32[]{:S(2)}, u32[]{:S(2)}) collective-permute-start(bf16[16,2048]{1,0:T(8,128)(2,1)S(1)} %get-tuple-element.39), channel_id=1, source_target_pairs={{0,8},{4,12},{8,0},{12,4},{1,9},{5,13},{9,1},{13,5},{2,10},{6,14},... | collective-permute-start | bytes 196616 | tf_op jit(solution)/shard_map/ppermute | solution.py:307
  50.8 4.0 %collective-permute-start.14 = (bf16[16,2048]{1,0:T(8,128)(2,1)S(1)}, bf16[16,2048]{1,0:T(8,128)(2,1)S(1)}, u32[]{:S(2)}, u32[]{:S(2)}) collective-permute-start(bf16[16,2048]{1,0:T(8,128)(2,1)S(1)} %get-tuple-element.40), channel_id=1, source_target_pairs={{0,12},{4,8},{8,4},{12,0},{1,13},{5,9},{9,5},{13,1},{2,14},{6,10},... | collective-permute-start | bytes 196616 | tf_op jit(solution)/shard_map/ppermute | solution.py:307
  (6 other events, 4.8 us)

commit v2 on v1

--- a/solution.py
+++ b/solution.py
@@ -39,82 +39,115 @@
     return out
 
 
-def attend_kernel(place, length, adapter, q_ref, fk_ref, fv_ref, k_ref, v_ref, *outs):
-    step = pl.program_id(0)
-    requests, _, longest, dim = k_ref.shape
-    group = q_ref.shape[1] // dim
+def attend_kernel(*refs, kv):
+    length_hbm, adapter_hbm, q_hbm, fk_hbm, fv_hbm, k_hbm, v_hbm = refs[:7]
+    outs = refs[7 : 7 + kv]
+    length, adapter, q_buf, fk_buf, fv_buf, k_buf, v_buf, small, big = refs[7 + kv :]
+    requests, _, longest, dim = k_hbm.shape
+    width = q_hbm.shape[1] // kv
+    group = width // dim
     rows = group * requests
     scaling = 1.0 / math.sqrt(dim)
-    q32 = q_ref[...].astype(F32)
-    queries = jnp.concatenate([q32[:, h * dim : (h + 1) * dim] for h in range(group)], axis=0)
-    keys = k_ref[...].reshape(requests * longest, dim)
-    every = lax.dot_general(
-        queries.astype(BF16), keys, (((1,), (1,)), ((), ())), preferred_element_type=F32
-    )
+    me = lax.axis_index("tensor")
+    order = tuple(range(kv - 1, -1, -1))
+
+    ready = [
+        pltpu.make_async_copy(source, target, small.at[i])
+        for i, (source, target) in enumerate(
+            (
+                (q_hbm, q_buf),
+                (fk_hbm, fk_buf),
+                (fv_hbm, fv_buf),
+                (length_hbm, length),
+                (adapter_hbm, adapter),
+            )
+        )
+    ]
+    keys_in = {}
+    values_in = {}
+    for r in order:
+        head = jnp.bitwise_xor(me, r)
+        keys_in[r] = pltpu.make_async_copy(k_hbm.at[:, head], k_buf.at[r], big.at[0, r])
+        values_in[r] = pltpu.make_async_copy(v_hbm.at[:, head], v_buf.at[r], big.at[1, r])
+    for copy in ready:
+        copy.start()
+    for r in order:
+        keys_in[r].start()
+        values_in[r].start()
+    for copy in ready:
+        copy.wait()
+
     request = lax.rem(lax.broadcasted_iota(jnp.int32, (rows, longest), 0), requests)
-    scores = every[:, :longest]
-    for r in range(1, requests):
-        scores = jnp.where(request == r, every[:, r * longest : (r + 1) * longest], scores)
     lengths = jnp.concatenate([column_of(length, requests)] * group, axis=0)
     valid = lax.broadcasted_iota(jnp.int32, (rows, longest), 1) < lengths
-    scores = jnp.where(valid, scores * scaling, -1e30)
-    fresh_key = jnp.concatenate([fk_ref[...].astype(F32)] * group, axis=0)
-    fresh_value = jnp.concatenate([fv_ref[...].astype(F32)] * group, axis=0)
-    own = jnp.sum(queries * fresh_key, axis=1, keepdims=True) * scaling
-    highest = jnp.maximum(jnp.max(scores, axis=1, keepdims=True), own)
-    exponent = jnp.where(valid, jnp.exp(scores - highest), 0.0)
-    own_exp = jnp.exp(own - highest)
-    total = jnp.sum(exponent, axis=1, keepdims=True) + own_exp
-    weights = exponent / total
-    own_weight = (own_exp / total).astype(BF16).astype(F32)
-    spread = jnp.concatenate(
-        [jnp.where(request == r, weights, 0.0) for r in range(requests)], axis=1
-    ).astype(BF16)
-    values = v_ref[...].reshape(requests * longest, dim)
-    result = jnp.dot(spread, values, preferred_element_type=F32) + own_weight * fresh_value
-    pieces = [result[h * requests : (h + 1) * requests] for h in range(group)]
-    pieces.append(column_of(adapter, requests).astype(F32))
-    block = jnp.concatenate(pieces, axis=1).astype(BF16)
-    for i, out in enumerate(outs):
-
-        @pl.when(step == i)
-        def _(out=out):
-            out[...] = block
-
-
-def attend_blocks(place, length, adapter, query, fresh_key, fresh_value, keys, values):
+    ids = column_of(adapter, requests).astype(F32)
+    for r in order:
+        head = jnp.bitwise_xor(me, r)
+        mine = pl.ds(pl.multiple_of(head * dim, dim), dim)
+        q32 = q_buf[:, pl.ds(pl.multiple_of(head * width, width), width)].astype(F32)
+        queries = jnp.concatenate([q32[:, h * dim : (h + 1) * dim] for h in range(group)], axis=0)
+        fresh_key = jnp.concatenate([fk_buf[:, mine].astype(F32)] * group, axis=0)
+        fresh_value = jnp.concatenate([fv_buf[:, mine].astype(F32)] * group, axis=0)
+        own = jnp.sum(queries * fresh_key, axis=1, keepdims=True) * scaling
+        keys_in[r].wait()
+        every = lax.dot_general(
+            queries.astype(BF16),
+            k_buf[r].reshape(requests * longest, dim),
+            (((1,), (1,)), ((), ())),
+            preferred_element_type=F32,
+        )
+        scores = every[:, :longest]
+        for i in range(1, requests):
+            scores = jnp.where(request == i, every[:, i * longest : (i + 1) * longest], scores)
+        scores = jnp.where(valid, scores * scaling, -1e30)
+        highest = jnp.maximum(jnp.max(scores, axis=1, keepdims=True), own)
+        exponent = jnp.where(valid, jnp.exp(scores - highest), 0.0)
+        own_exp = jnp.exp(own - highest)
+        total = jnp.sum(exponent, axis=1, keepdims=True) + own_exp
+        weights = exponent / total
+        own_weight = (own_exp / total).astype(BF16).astype(F32)
+        spread = jnp.concatenate(
+            [jnp.where(request == i, weights, 0.0) for i in range(requests)], axis=1
+        ).astype(BF16)
+        values_in[r].wait()
+        result = (
+            jnp.dot(
+                spread, v_buf[r].reshape(requests * longest, dim), preferred_element_type=F32
+            )
+            + own_weight * fresh_value
+        )
+        pieces = [result[h * requests : (h + 1) * requests] for h in range(group)]
+        outs[r][...] = jnp.concatenate(pieces + [ids], axis=1).astype(BF16)
+
+
+def attend_blocks(length, adapter, query, fresh_key, fresh_value, keys, values):
     requests, kv, longest, dim = keys.shape
     width = query.shape[1] // kv
-
-    def column(s, place, *_):
-        return (0, jnp.bitwise_xor(place[0], s))
-
-    def cache(s, place, *_):
-        return (0, jnp.bitwise_xor(place[0], s), 0, 0)
-
+    hbm = pl.BlockSpec(memory_space=pltpu.HBM)
     return pl.pallas_call(
-        attend_kernel,
-        grid_spec=pltpu.PrefetchScalarGridSpec(
-            num_scalar_prefetch=3,
-            grid=(kv,),
-            in_specs=[
-                pl.BlockSpec((requests, width), column),
-                pl.BlockSpec((requests, dim), column),
-                pl.BlockSpec((requests, dim), column),
-                pl.BlockSpec((requests, 1, longest, dim), cache),
-                pl.BlockSpec((requests, 1, longest, dim), cache),
-            ],
-            out_specs=[pl.BlockSpec((requests, width + LANES), lambda s, *_: (0, 0))] * kv,
-        ),
+        functools.partial(attend_kernel, kv=kv),
+        in_specs=[hbm] * 7,
+        out_specs=[pl.BlockSpec(memory_space=pltpu.VMEM)] * kv,
         out_shape=[sds((requests, width + LANES))] * kv,
-        compiler_params=params(1),
-        cost_estimate=cost(2**28, 2 * keys.size * 2),
+        scratch_shapes=[
+            pltpu.SMEM(length.shape, jnp.int32),
+            pltpu.SMEM(adapter.shape, jnp.int32),
+            pltpu.VMEM(query.shape, BF16),
+            pltpu.VMEM(fresh_key.shape, BF16),
+            pltpu.VMEM(fresh_value.shape, BF16),
+            pltpu.VMEM((kv, requests, longest, dim), BF16),
+            pltpu.VMEM((kv, requests, longest, dim), BF16),
+            pltpu.SemaphoreType.DMA((5,)),
+            pltpu.SemaphoreType.DMA((2, kv)),
+        ],
+        compiler_params=params(),
+        cost_estimate=cost(2**31, 2 * keys.size * 2),
         name="attend",
-    )(place, length, adapter, query, fresh_key, fresh_value, keys, values)
-
-
-def route_kernel(place, x0, x1, x2, x3, rows_ref, pick_ref, c0, c1, c2, c3, held, *, local, cap):
-    me, mine = place[0], place[1]
+    )(*[pltpu.with_memory_space_constraint(x, pltpu.HBM) for x in (length, adapter, query, fresh_key, fresh_value, keys, values)])
+
+
+def route_kernel(x0, x1, x2, x3, rows_ref, pick_ref, c0, c1, c2, c3, held, *, local, cap):
+    me, mine = lax.axis_index("tensor"), lax.axis_index("batch")
     count = x0.shape[0]
     for r, x in enumerate((x0, x1, x2, x3)):
         held[pl.ds(pl.multiple_of(jnp.bitwise_xor(me, r) * count, count), count), :] = x[
@@ -146,76 +179,91 @@
         c[...] = chosen[r * cap : (r + 1) * cap]
 
 
-def route(place, blocks, local, cap):
+def route(blocks, local, cap):
     count, wide = blocks[0].shape
     rows = count * len(blocks)
-    smem = pl.BlockSpec(memory_space=pltpu.SMEM)
     vmem = pl.BlockSpec(memory_space=pltpu.VMEM)
     return pl.pallas_call(
         functools.partial(route_kernel, local=local, cap=cap),
-        in_specs=[smem] + [vmem] * 4,
+        in_specs=[vmem] * 4,
         out_specs=[vmem] * 6,
         out_shape=[sds((rows, wide - LANES)), sds((rows, LANES))] + [sds((cap, wide))] * 4,
         scratch_shapes=[pltpu.VMEM((rows, wide), F32)],
         compiler_params=params(),
         cost_estimate=cost(2**20, rows * wide * 8),
         name="route",
-    )(place, *blocks)
-
-
-def project_kernel(place, rows_ref, w_ref, *rest, add):
-    step = pl.program_id(0)
-    product = jnp.dot(rows_ref[...], w_ref[...], preferred_element_type=F32)
-    if add:
-        product = product + rest[0][...].astype(F32)
-        rest = rest[1:]
-    for i, out in enumerate(rest):
-
-        @pl.when(step == i)
-        def _(out=out):
-            out[...] = product.astype(BF16)
-
-
-def project(place, rows, weight, width, which, addend=None, tile=512):
+    )(*blocks)
+
+
+def project_kernel(*refs, which, tile, add, after):
+    rows_ref, w_hbm = refs[:2]
+    addend = refs[2] if add else None
+    skip = 2 + add + after
+    outs = refs[skip : skip + len(which)]
+    buf, sems = refs[skip + len(which) :]
+    width = outs[0].shape[1]
+    tiles = width // tile
+    me = lax.axis_index("tensor")
+    copies = []
+    for k, r in enumerate(which):
+        start = jnp.bitwise_xor(me, r) * width
+        for j in range(tiles):
+            at = pl.ds(pl.multiple_of(start + j * tile, tile), tile)
+            n = k * tiles + j
+            copies.append(pltpu.make_async_copy(w_hbm.at[:, at], buf.at[n], sems.at[n]))
+    for copy in copies:
+        copy.start()
+    rows = rows_ref[...]
+    for k, out in enumerate(outs):
+        for j in range(tiles):
+            n = k * tiles + j
+            copies[n].wait()
+            product = jnp.dot(rows, buf[n], preferred_element_type=F32)
+            span = slice(j * tile, (j + 1) * tile)
+            if add:
+                product = product + addend[:, span].astype(F32)
+            out[:, span] = product.astype(BF16)
+
+
+def project(rows, weight, width, which, addend=None, after=None, tile=512):
     count, depth = rows.shape
     tiles = width // tile
     parts = len(which)
-
-    def column(i, j, place):
-        r = which[0] if parts == 1 else jnp.where(i == 0, which[0], which[1])
-        return (0, jnp.bitwise_xor(place[0], r) * tiles + j)
-
-    def target(k):
-        return lambda i, j, place: (0, jnp.where(i < k, 0, jnp.where(i > k, tiles - 1, j)))
-
-    in_specs = [
-        pl.BlockSpec((count, depth), lambda i, j, place: (0, 0)),
-        pl.BlockSpec((depth, tile), column),
-    ]
-    operands = [place, rows, weight]
+    vmem = pl.BlockSpec(memory_space=pltpu.VMEM)
+    in_specs = [vmem, pl.BlockSpec(memory_space=pltpu.HBM)]
+    operands = [rows, pltpu.with_memory_space_constraint(weight, pltpu.HBM)]
     if addend is not None:
-        in_specs.append(pl.BlockSpec((count, tile), lambda i, j, place: (0, j)))
+        in_specs.append(vmem)
         operands.append(addend)
+    if after is not None:
+        in_specs.append(pl.BlockSpec(memory_space=pl.ANY))
+        operands.append(after)
     return pl.pallas_call(
-        functools.partial(project_kernel, add=addend is not None),
-        grid_spec=pltpu.PrefetchScalarGridSpec(
-            num_scalar_prefetch=1,
-            grid=(parts, tiles),
-            in_specs=in_specs,
-            out_specs=[pl.BlockSpec((count, tile), target(k)) for k in range(parts)],
+        functools.partial(
+            project_kernel,
+            which=which,
+            tile=tile,
+            add=addend is not None,
+            after=after is not None,
         ),
+        in_specs=in_specs,
+        out_specs=[vmem] * parts,
         out_shape=[sds((count, width))] * parts,
-        compiler_params=params(2),
+        scratch_shapes=[
+            pltpu.VMEM((parts * tiles, depth, tile), BF16),
+            pltpu.SemaphoreType.DMA((parts * tiles,)),
+        ],
+        compiler_params=params(),
         cost_estimate=cost(2 * count * depth * width * parts, depth * width * 2 * parts),
         name="project",
     )(*operands)
 
 
-def down_kernel(place, c0, c1, c2, c3, down_ref, low_ref, slot_ref):
+def down_kernel(c0, c1, c2, c3, down_ref, low_ref, slot_ref):
     local, width, rank = down_ref.shape
     chosen = jnp.concatenate([c[...] for c in (c0, c1, c2, c3)], axis=0)
     values = chosen[:, :width]
-    slot = chosen[:, width:].astype(F32).astype(jnp.int32) - place[1] * local
+    slot = chosen[:, width:].astype(F32).astype(jnp.int32) - lax.axis_index("batch") * local
     low = jnp.zeros((chosen.shape[0], rank), F32)
     for a in range(local):
         product = jnp.dot(values, down_ref[a], preferred_element_type=F32)
@@ -224,23 +272,22 @@
     slot_ref[...] = slot
 
 
-def down(place, chosen, weight):
+def down(chosen, weight):
     local, width, rank = weight.shape
     rows = chosen[0].shape[0] * len(chosen)
-    smem = pl.BlockSpec(memory_space=pltpu.SMEM)
     vmem = pl.BlockSpec(memory_space=pltpu.VMEM)
     return pl.pallas_call(
         down_kernel,
-        in_specs=[smem] + [vmem] * 5,
+        in_specs=[vmem] * 5,
         out_specs=[vmem] * 2,
         out_shape=[sds((rows, rank)), sds((rows, rank), jnp.int32)],
         compiler_params=params(),
-        cost_estimate=cost(2 * rows * weight.size, weight.size * 2),
+        cost_estimate=cost(2**34, weight.size * 2),
         name="down",
-    )(place, *chosen, weight)
-
-
-def up_kernel(place, ranks, l0, l1, l2, l3, slot_ref, up_ref, *outs):
+    )(*chosen, weight)
+
+
+def up_kernel(ranks, l0, l1, l2, l3, slot_ref, up_ref, *outs):
     local = up_ref.shape[0]
     low = l0[...].astype(F32)
     for share in (l1, l2, l3):
@@ -249,7 +296,7 @@
     lane = lax.broadcasted_iota(jnp.int32, low.shape, 1)
     total = None
     for a in range(local):
-        rank = ranks[place[1] * local + a]
+        rank = ranks[lax.axis_index("batch") * local + a]
         factor = ADAPTER_SCALE / jnp.full(low.shape, rank, jnp.int32).astype(F32)
         kept = jnp.where((slot == a) & (lane < rank), low * factor, 0.0).astype(BF16)
         product = jnp.dot(kept, up_ref[a], preferred_element_type=F32)
@@ -260,7 +307,7 @@
         out[...] = adapted[r * cap : (r + 1) * cap]
 
 
-def up(place, ranks, shares, slot, weight, parts, tile=512):
+def up(ranks, shares, slot, weight, parts, tile=512):
     local, rank, width = weight.shape
     rows = slot.shape[0]
     cap = rows // parts
@@ -269,16 +316,16 @@
     return pl.pallas_call(
         up_kernel,
         grid_spec=pltpu.PrefetchScalarGridSpec(
-            num_scalar_prefetch=2,
+            num_scalar_prefetch=1,
             grid=(tiles,),
             in_specs=[whole] * 5 + [pl.BlockSpec((local, rank, tile), lambda j, *_: (0, 0, j))],
             out_specs=[pl.BlockSpec((cap, tile), lambda j, *_: (0, j))] * parts,
         ),
         out_shape=[sds((cap, width))] * parts,
         compiler_params=params(1),
-        cost_estimate=cost(2 * rows * weight.size, weight.size * 2),
+        cost_estimate=cost(2**34, weight.size * 2),
         name="up",
-    )(place, ranks, *shares, slot, weight)
+    )(ranks, *shares, slot, weight)
 
 
 def finish_kernel(pick_ref, y0, y1, y2, a0, a1, a2, a3, out):
@@ -326,10 +373,7 @@
     width = adapter_up_weight.shape[2]
     requests = query.shape[0]
     cap = 2 * requests * tensor_count // batch_count
-    place = jnp.stack([lax.axis_index("tensor"), lax.axis_index("batch")]).astype(jnp.int32)
-
     blocks = attend_blocks(
-        place,
         cached_length,
         request_adapter,
         query,
@@ -339,20 +383,20 @@
         stored_values,
     )
     blocks = [blocks[0]] + [across(blocks[r], "tensor", r) for r in (1, 2, 3)]
-    rows, pick, *chosen = route(place, blocks, local, cap)
+    rows, pick, *chosen = route(blocks, local, cap)
 
     gathered = [chosen[0]] + [across(chosen[r], "batch", r) for r in (1, 2, 3)]
-    far, near = project(place, rows, output_weight, width, (3, 1))
+    far, near = project(rows, output_weight, width, (3, 1))
     far_in = across(far, "tensor", 1)
     near_in = across(near, "tensor", 1)
 
-    low, slot = down(place, gathered, adapter_down_weight)
+    low, slot = down(gathered, adapter_down_weight)
     shares = [low] + [across(low, "tensor", r) for r in (1, 2, 3)]
-    (cross,) = project(place, rows, output_weight, width, (2,), addend=far_in)
-    (mine,) = project(place, rows, output_weight, width, (0,))
+    (cross,) = project(rows, output_weight, width, (2,), addend=far_in)
+    (mine,) = project(rows, output_weight, width, (0,))
     cross_in = across(cross, "tensor", 2)
 
-    lifted = up(place, rank_per_adapter, shares, slot, adapter_up_weight, batch_count)
+    lifted = up(rank_per_adapter, shares, slot, adapter_up_weight, batch_count)
     lifted = [lifted[0]] + [across(lifted[r], "batch", r) for r in (1, 2, 3)]
     return finish(pick, (mine, near_in, cross_in), lifted)
 

time: 56 us -> 39.4 us (0.70)
  local copies, waits for them, and re-layouts: 11.8 us -> 0.02 us
  waiting for transfers between devices: 13.2 us -> 7.12 us
  starting transfers between devices: 15.2 us -> 16.1 us
    unnamed x30 -> x6, local copies, waits for them, and re-layouts: 11.8 us -> 0.02 us
    ppermute x15, waiting for transfers between devices: 13.2 us -> 7.12 us  [across(): return lax.ppermute(value, axis, [(i, i ^ r) for i in range(n)])]
    pallas_call x5, Pallas kernels: 11.8 us -> 12.9 us  [the longest x3 8.86 us: project(): pl.pallas_call(functools.partial(project_kernel, which=which, tile=tile,...]
    ppermute x15, starting transfers between devices: 15.2 us -> 16.1 us  [across(): return lax.ppermute(value, axis, [(i, i ^ r) for i in range(n)])]
  transfers between devices with their start and end apart: 15 -> 15, of which waited for: 7 -> 5; matrix products, arithmetic and copies ran while one was open for 0% -> 0% of each run, Pallas kernels for 12% -> 28%
where the time goes in v2:
time: 39.4 us; the launch traced here: 39.3 us
  starting transfers between devices  16.1 us (41%)
  Pallas kernels  15.8 us (40%)
  waiting for transfers between devices  7.12 us (18%)
    ppermute x15, starting transfers between devices, across(): return lax.ppermute(value, axis, [(i, i ^ r) for i in range(n)])  16.1 us
    pallas_call x3, Pallas kernels, project(): pl.pallas_call(functools.partial(project_kernel, which=which, tile=tile,...  8.86 us
    ppermute x15, waiting for transfers between devices, across(): return lax.ppermute(value, axis, [(i, i ^ r) for i in range(n)])  7.12 us
    pallas_call x1, Pallas kernels, attend_blocks(): pl.pallas_call(functools.partial(attend_kernel, kv=kv), in_specs=[hbm] *...  3.7 us
    pallas_call x1, Pallas kernels, up(): pl.pallas_call(up_kernel, grid_spec=pltpu.PrefetchScalarGridSpec(num_scal...  1.71 us
    pallas_call x1, Pallas kernels, finish(): pl.pallas_call(finish_kernel, in_specs=[vmem] * 8, out_specs=vmem, out_sh...  0.82 us
  transfers between devices with their start and end apart: 15, of which 5 were waited for; matrix products, arithmetic and copies ran while one was open for 0% of the time, Pallas kernels for 28%

profile of v2, /device:TPU:0, one launch (start us, length us, event | category | flops | bytes accessed | tf_op | source)
XLA Modules:
  0.0 39.3 jit_solution(405979130565966510)
XLA Ops:
  0.0 3.7 %attend.1 = (bf16[8,1152]{1,0:T(8,128)(2,1)S(1)}, bf16[8,1152]{1,0:T(8,128)(2,1)S(1)}, bf16[8,1152]{1,0:T(8,128)(2,1)S(1)}, bf16[8,1152]{1,0:T(8,128)(2,1)S(1)}) custom-call(s32[8]{0:T(128)} %refs_0_.1, s32[8]{0:T(128)} %refs_1_.4, bf16[8,4096]{1,0:T(8,128)(2,1)} %refs_2_.1, bf16[8,512]{1,0:T(8,128)(2,1)} %refs_3_.1, bf16[8,512]{1,0:T(8,128)(2,1)} %refs_4_.1, ...), custom_call_target="tpu_custom_call" | custom-call | flops 2147483648 | bytes 2097152 | tf_op jit(solution)/shard_map/attend/pallas_call | solution.py:127
  3.7 3.1 %collective-permute-start = (bf16[8,1152]{1,0:T(8,128)(2,1)S(1)}, bf16[8,1152]{1,0:T(8,128)(2,1)S(1)}, u32[]{:S(2)}, u32[]{:S(2)}) collective-permute-start(bf16[8,1152]{1,0:T(8,128)(2,1)S(1)} %get-tuple-element.24), channel_id=1, source_target_pairs={{0,1},{1,0},{2,3},{3,2},{4,5},{5,4},{6,7},{7,6},{8,9},{9,8},{10,11... | collective-permute-start | bytes 55304 | tf_op jit(solution)/shard_map/ppermute | solution.py:354
  6.8 2.6 %collective-permute-start.1 = (bf16[8,1152]{1,0:T(8,128)(2,1)S(1)}, bf16[8,1152]{1,0:T(8,128)(2,1)S(1)}, u32[]{:S(2)}, u32[]{:S(2)}) collective-permute-start(bf16[8,1152]{1,0:T(8,128)(2,1)S(1)} %get-tuple-element.25), channel_id=1, source_target_pairs={{0,2},{1,3},{2,0},{3,1},{4,6},{5,7},{6,4},{7,5},{8,10},{9,11},{10,... | collective-permute-start | bytes 55304 | tf_op jit(solution)/shard_map/ppermute | solution.py:354
  9.4 2.2 %collective-permute-done.1.x2 = bf16[8,1152]{1,0:T(8,128)(2,1)S(1)} collective-permute-done((bf16[8,1152]{1,0:T(8,128)(2,1)S(1)}, bf16[8,1152]{1,0:T(8,128)(2,1)S(1)}, u32[]{:S(2)}, u32[]{:S(2)}) %collective-permute-start.1) | collective-permute-done | bytes 18464 | tf_op jit(solution)/shard_map/ppermute | solution.py:354
  11.6 3.3 %collective-permute-done.2.x3 = bf16[8,1152]{1,0:T(8,128)(2,1)S(1)} collective-permute-done((bf16[8,1152]{1,0:T(8,128)(2,1)S(1)}, bf16[8,1152]{1,0:T(8,128)(2,1)S(1)}, u32[]{:S(2)}, u32[]{:S(2)}) %collective-permute-start.2) | collective-permute-done | bytes 18464 | tf_op jit(solution)/shard_map/ppermute | solution.py:354
  14.9 0.4 %route.1 = (bf16[32,1024]{1,0:T(8,128)(2,1)S(1)}, bf16[32,128]{1,0:T(8,128)(2,1)S(1)}, bf16[16,1152]{1,0:T(8,128)(2,1)S(1)}, bf16[16,1152]{1,0:T(8,128)(2,1)S(1)...) custom-call(bf16[8,1152]{1,0:T(8,128)(2,1)S(1)} %get-tuple-element.23.x0, ...), custom_call_target="tpu_custom_call" | custom-call | flops 1048576 | bytes 294912 | tf_op jit(solution)/shard_map/route/pallas_call | solution.py:186
  15.4 0.1 collective-permute-start.6
  15.4 1.6 %collective-permute-start.7 = (bf16[16,1152]{1,0:T(8,128)(2,1)S(1)}, bf16[16,1152]{1,0:T(8,128)(2,1)S(1)}, u32[]{:S(2)}, u32[]{:S(2)}) collective-permute-start(bf16[16,1152]{1,0:T(8,128)(2,1)S(1)} %get-tuple-element.33), channel_id=1, source_target_pairs={{0,8},{4,12},{8,0},{12,4},{1,9},{5,13},{9,1},{13,5},{2,10},{6,14},... | collective-permute-start | bytes 110600 | tf_op jit(solution)/shard_map/ppermute | solution.py:354
  17.0 0.3 collective-permute-start.8
  17.3 3.8 %project.4 = (bf16[32,2048]{1,0:T(8,128)(2,1)S(1)}, bf16[32,2048]{1,0:T(8,128)(2,1)S(1)}) custom-call(bf16[32,1024]{1,0:T(8,128)(2,1)S(1)} %get-tuple-element.28.refs_0_, bf16[1024,8192]{1,0:T(8,128)(2,1)} %refs_1_.7), custom_call_target="tpu_custom_call" | custom-call | flops 268435456 | bytes 8388608 | tf_op jit(solution)/shard_map/project/pallas_call | solution.py:241
  21.1 0.1 collective-permute-start.4
  21.2 0.3 down.1
  21.6 0.8 %collective-permute-start.10 = (bf16[64,128]{1,0:T(8,128)(2,1)S(1)}, bf16[64,128]{1,0:T(8,128)(2,1)S(1)}, u32[]{:S(2)}, u32[]{:S(2)}) collective-permute-start(bf16[64,128]{1,0:T(8,128)(2,1)S(1)} %get-tuple-element.35.l0), channel_id=1, source_target_pairs={{0,2},{1,3},{2,0},{3,1},{4,6},{5,7},{6,4},{7,5},{8,10},{9,11},{10,... | collective-permute-start | bytes 49160 | tf_op jit(solution)/shard_map/ppermute | solution.py:354
  22.4 3.6 %collective-permute-start.11 = (bf16[64,128]{1,0:T(8,128)(2,1)S(1)}, bf16[64,128]{1,0:T(8,128)(2,1)S(1)}, u32[]{:S(2)}, u32[]{:S(2)}) collective-permute-start(bf16[64,128]{1,0:T(8,128)(2,1)S(1)} %get-tuple-element.35.l0), channel_id=1, source_target_pairs={{0,3},{1,2},{2,1},{3,0},{4,7},{5,6},{6,5},{7,4},{8,11},{9,10},{10,... | collective-permute-start | bytes 49160 | tf_op jit(solution)/shard_map/ppermute | solution.py:354
  26.0 2.0 %collective-permute-start.3 = (bf16[32,2048]{1,0:T(8,128)(2,1)S(1)}, bf16[32,2048]{1,0:T(8,128)(2,1)S(1)}, u32[]{:S(2)}, u32[]{:S(2)}) collective-permute-start(bf16[32,2048]{1,0:T(8,128)(2,1)S(1)} %get-tuple-element.29), channel_id=1, source_target_pairs={{0,1},{1,0},{2,3},{3,2},{4,5},{5,4},{6,7},{7,6},{8,9},{9,8},{10,11... | collective-permute-start | bytes 393224 | tf_op jit(solution)/shard_map/ppermute | solution.py:354
  28.0 2.5 %project.5 = bf16[32,2048]{1,0:T(8,128)(2,1)S(1)} custom-call(bf16[32,1024]{1,0:T(8,128)(2,1)S(1)} %get-tuple-element.28.refs_0_, bf16[1024,8192]{1,0:T(8,128)(2,1)} %refs_1_.7, bf16[32,2048]{1,0:T(8,128)(2,1)S(1)} %collective-permute-done.4.refs_2_), custom_call_target="tpu_custom_call" | custom-call | flops 134217728 | bytes 4194304 | tf_op jit(solution)/shard_map/project/pallas_call | solution.py:241
  30.7 1.7 %up.1 = (bf16[16,2048]{1,0:T(8,128)(2,1)S(1)}, bf16[16,2048]{1,0:T(8,128)(2,1)S(1)}, bf16[16,2048]{1,0:T(8,128)(2,1)S(1)}, bf16[16,2048]{1,0:T(8,128)(2,1)S(1)}) custom-call(s32[16]{0:T(128)S(1)} %copy-done.2, bf16[64,128]{1,0:T(8,128)(2,1)S(1)} %get-tuple-element.35.l0, bf16[64,128]{1,0:T(8,128)(2,1)S(1)} %collective-permute-done.9.l1, ...), custom_call_target="tpu_custom_call" | custom-call | flops 17179869184 | bytes 2097152 | tf_op jit(solution)/shard_map/up/pallas_call | solution.py:316
  32.5 1.6 %collective-permute-start.13 = (bf16[16,2048]{1,0:T(8,128)(2,1)S(1)}, bf16[16,2048]{1,0:T(8,128)(2,1)S(1)}, u32[]{:S(2)}, u32[]{:S(2)}) collective-permute-start(bf16[16,2048]{1,0:T(8,128)(2,1)S(1)} %get-tuple-element.39), channel_id=1, source_target_pairs={{0,8},{4,12},{8,0},{12,4},{1,9},{5,13},{9,1},{13,5},{2,10},{6,14},... | collective-permute-start | bytes 196616 | tf_op jit(solution)/shard_map/ppermute | solution.py:354
  34.0 0.3 collective-permute-start.14
  34.3 2.5 %project.3.y0 = bf16[32,2048]{1,0:T(8,128)(2,1)S(1)} custom-call(bf16[32,1024]{1,0:T(8,128)(2,1)S(1)} %get-tuple-element.28.refs_0_, bf16[1024,8192]{1,0:T(8,128)(2,1)} %refs_1_.7), custom_call_target="tpu_custom_call" | custom-call | flops 134217728 | bytes 4194304 | tf_op jit(solution)/shard_map/project/pallas_call | solution.py:241
  36.9 0.1 collective-permute-done.13.a2
  37.0 1.1 %collective-permute-done.14.a3 = bf16[16,2048]{1,0:T(8,128)(2,1)S(1)} collective-permute-done((bf16[16,2048]{1,0:T(8,128)(2,1)S(1)}, bf16[16,2048]{1,0:T(8,128)(2,1)S(1)}, u32[]{:S(2)}, u32[]{:S(2)}) %collective-permute-start.14) | collective-permute-done | bytes 65568 | tf_op jit(solution)/shard_map/ppermute | solution.py:354
  38.1 0.3 collective-permute-done.5.y2
  38.4 0.8 %finish.1 = bf16[32,2048]{1,0:T(8,128)(2,1)} custom-call(bf16[32,128]{1,0:T(8,128)(2,1)S(1)} %get-tuple-element.27.pick_ref, bf16[32,2048]{1,0:T(8,128)(2,1)S(1)} %project.3.y0, bf16[32,2048]{1,0:T(8,128)(2,1)S(1)} %collective-permute-done.3.y1, bf16[32,2048]{1,0:T(8,128)(2,1)S(1)} %collective-permute-done.5.y2, bf16[16,2048]{1,0:T(8,128)(2,1)S(1)} %get-tuple-element.37.a0, ...), custom_call_target="tpu_custom_call" | custom-call | flops 16777216 | bytes 1048576 | tf_op jit(solution)/shard_map/finish/pallas_call | solution.py:341
  (20 shorter events, 0.2 us)
Async XLA Ops:
  0.0 21.2 %copy-start.1 = (bf16[4,1024,128]{2,1,0:T(8,128)(2,1)S(1)}, bf16[4,1024,128]{2,1,0:T(8,128)(2,1)}, u32[]{:S(2)}) copy-start(bf16[4,1024,128]{2,1,0:T(8,128)(2,1)} %down_ref.1) | copy-start | bytes 3145732
  3.7 5.7 %collective-permute-start = (bf16[8,1152]{1,0:T(8,128)(2,1)S(1)}, bf16[8,1152]{1,0:T(8,128)(2,1)S(1)}, u32[]{:S(2)}, u32[]{:S(2)}) collective-permute-start(bf16[8,1152]{1,0:T(8,128)(2,1)S(1)} %get-tuple-element.24), channel_id=1, source_target_pairs={{0,1},{1,0},{2,3},{3,2},{4,5},{5,4},{6,7},{7,6},{8,9},{9,8},{10,11... | collective-permute-start | bytes 55304 | tf_op jit(solution)/shard_map/ppermute | solution.py:354
  6.8 4.8 %collective-permute-start.1 = (bf16[8,1152]{1,0:T(8,128)(2,1)S(1)}, bf16[8,1152]{1,0:T(8,128)(2,1)S(1)}, u32[]{:S(2)}, u32[]{:S(2)}) collective-permute-start(bf16[8,1152]{1,0:T(8,128)(2,1)S(1)} %get-tuple-element.25), channel_id=1, source_target_pairs={{0,2},{1,3},{2,0},{3,1},{4,6},{5,7},{6,4},{7,5},{8,10},{9,11},{10,... | collective-permute-start | bytes 55304 | tf_op jit(solution)/shard_map/ppermute | solution.py:354
  9.4 5.6 %collective-permute-start.2 = (bf16[8,1152]{1,0:T(8,128)(2,1)S(1)}, bf16[8,1152]{1,0:T(8,128)(2,1)S(1)}, u32[]{:S(2)}, u32[]{:S(2)}) collective-permute-start(bf16[8,1152]{1,0:T(8,128)(2,1)S(1)} %get-tuple-element.26), channel_id=1, source_target_pairs={{0,3},{1,2},{2,1},{3,0},{4,7},{5,6},{6,5},{7,4},{8,11},{9,10},{10,... | collective-permute-start | bytes 55304 | tf_op jit(solution)/shard_map/ppermute | solution.py:354
  15.4 5.8 %collective-permute-start.6 = (bf16[16,1152]{1,0:T(8,128)(2,1)S(1)}, bf16[16,1152]{1,0:T(8,128)(2,1)S(1)}, u32[]{:S(2)}, u32[]{:S(2)}) collective-permute-start(bf16[16,1152]{1,0:T(8,128)(2,1)S(1)} %get-tuple-element.32), channel_id=1, source_target_pairs={{0,4},{4,0},{8,12},{12,8},{1,5},{5,1},{9,13},{13,9},{2,6},{6,2},{1... | collective-permute-start | bytes 110600 | tf_op jit(solution)/shard_map/ppermute | solution.py:354
  15.4 5.8 %collective-permute-start.7 = (bf16[16,1152]{1,0:T(8,128)(2,1)S(1)}, bf16[16,1152]{1,0:T(8,128)(2,1)S(1)}, u32[]{:S(2)}, u32[]{:S(2)}) collective-permute-start(bf16[16,1152]{1,0:T(8,128)(2,1)S(1)} %get-tuple-element.33), channel_id=1, source_target_pairs={{0,8},{4,12},{8,0},{12,4},{1,9},{5,13},{9,1},{13,5},{2,10},{6,14},... | collective-permute-start | bytes 110600 | tf_op jit(solution)/shard_map/ppermute | solution.py:354
  17.0 4.2 %collective-permute-start.8 = (bf16[16,1152]{1,0:T(8,128)(2,1)S(1)}, bf16[16,1152]{1,0:T(8,128)(2,1)S(1)}, u32[]{:S(2)}, u32[]{:S(2)}) collective-permute-start(bf16[16,1152]{1,0:T(8,128)(2,1)S(1)} %get-tuple-element.34), channel_id=1, source_target_pairs={{0,12},{4,8},{8,4},{12,0},{1,13},{5,9},{9,5},{13,1},{2,14},{6,10},... | collective-permute-start | bytes 110600 | tf_op jit(solution)/shard_map/ppermute | solution.py:354
  21.1 6.9 %collective-permute-start.4 = (bf16[32,2048]{1,0:T(8,128)(2,1)S(1)}, bf16[32,2048]{1,0:T(8,128)(2,1)S(1)}, u32[]{:S(2)}, u32[]{:S(2)}) collective-permute-start(bf16[32,2048]{1,0:T(8,128)(2,1)S(1)} %get-tuple-element.30), channel_id=1, source_target_pairs={{0,1},{1,0},{2,3},{3,2},{4,5},{5,4},{6,7},{7,6},{8,9},{9,8},{10,11... | collective-permute-start | bytes 393224 | tf_op jit(solution)/shard_map/ppermute | solution.py:354
  21.6 9.1 %copy-start = (bf16[4,128,2048]{2,1,0:T(8,128)(2,1)S(1)}, bf16[4,128,2048]{2,1,0:T(8,128)(2,1)}, u32[]{:S(2)}) copy-start(bf16[4,128,2048]{2,1,0:T(8,128)(2,1)} %up_ref.1) | copy-start | bytes 6291460
  21.6 9.1 %copy-start.2 = (s32[16]{0:T(128)S(1)}, s32[16]{0:T(128)}, u32[]{:S(2)}) copy-start(s32[16]{0:T(128)} %ranks.1) | copy-start | bytes 196
  21.6 9.1 %collective-permute-start.10 = (bf16[64,128]{1,0:T(8,128)(2,1)S(1)}, bf16[64,128]{1,0:T(8,128)(2,1)S(1)}, u32[]{:S(2)}, u32[]{:S(2)}) collective-permute-start(bf16[64,128]{1,0:T(8,128)(2,1)S(1)} %get-tuple-element.35.l0), channel_id=1, source_target_pairs={{0,2},{1,3},{2,0},{3,1},{4,6},{5,7},{6,4},{7,5},{8,10},{9,11},{10,... | collective-permute-start | bytes 49160 | tf_op jit(solution)/shard_map/ppermute | solution.py:354
  22.4 8.3 %collective-permute-start.11 = (bf16[64,128]{1,0:T(8,128)(2,1)S(1)}, bf16[64,128]{1,0:T(8,128)(2,1)S(1)}, u32[]{:S(2)}, u32[]{:S(2)}) collective-permute-start(bf16[64,128]{1,0:T(8,128)(2,1)S(1)} %get-tuple-element.35.l0), channel_id=1, source_target_pairs={{0,3},{1,2},{2,1},{3,0},{4,7},{5,6},{6,5},{7,4},{8,11},{9,10},{10,... | collective-permute-start | bytes 49160 | tf_op jit(solution)/shard_map/ppermute | solution.py:354
  26.0 4.7 %collective-permute-start.9 = (bf16[64,128]{1,0:T(8,128)(2,1)S(1)}, bf16[64,128]{1,0:T(8,128)(2,1)S(1)}, u32[]{:S(2)}, u32[]{:S(2)}) collective-permute-start(bf16[64,128]{1,0:T(8,128)(2,1)S(1)} %get-tuple-element.35.l0), channel_id=1, source_target_pairs={{0,1},{1,0},{2,3},{3,2},{4,5},{5,4},{6,7},{7,6},{8,9},{9,8},{10,11... | collective-permute-start | bytes 49160 | tf_op jit(solution)/shard_map/ppermute | solution.py:354
  26.0 12.1 %collective-permute-start.3 = (bf16[32,2048]{1,0:T(8,128)(2,1)S(1)}, bf16[32,2048]{1,0:T(8,128)(2,1)S(1)}, u32[]{:S(2)}, u32[]{:S(2)}) collective-permute-start(bf16[32,2048]{1,0:T(8,128)(2,1)S(1)} %get-tuple-element.29), channel_id=1, source_target_pairs={{0,1},{1,0},{2,3},{3,2},{4,5},{5,4},{6,7},{7,6},{8,9},{9,8},{10,11... | collective-permute-start | bytes 393224 | tf_op jit(solution)/shard_map/ppermute | solution.py:354
  30.6 7.9 %collective-permute-start.5 = (bf16[32,2048]{1,0:T(8,128)(2,1)S(1)}, bf16[32,2048]{1,0:T(8,128)(2,1)S(1)}, u32[]{:S(2)}, u32[]{:S(2)}) collective-permute-start(bf16[32,2048]{1,0:T(8,128)(2,1)S(1)} %project.5), channel_id=1, source_target_pairs={{0,2},{1,3},{2,0},{3,1},{4,6},{5,7},{6,4},{7,5},{8,10},{9,11},{10,... | collective-permute-start | bytes 393224 | tf_op jit(solution)/shard_map/ppermute | solution.py:354
  32.4 4.5 %collective-permute-start.12 = (bf16[16,2048]{1,0:T(8,128)(2,1)S(1)}, bf16[16,2048]{1,0:T(8,128)(2,1)S(1)}, u32[]{:S(2)}, u32[]{:S(2)}) collective-permute-start(bf16[16,2048]{1,0:T(8,128)(2,1)S(1)} %get-tuple-element.38), channel_id=1, source_target_pairs={{0,4},{4,0},{8,12},{12,8},{1,5},{5,1},{9,13},{13,9},{2,6},{6,2},{1... | collective-permute-start | bytes 196616 | tf_op jit(solution)/shard_map/ppermute | solution.py:354
  32.5 4.5 %collective-permute-start.13 = (bf16[16,2048]{1,0:T(8,128)(2,1)S(1)}, bf16[16,2048]{1,0:T(8,128)(2,1)S(1)}, u32[]{:S(2)}, u32[]{:S(2)}) collective-permute-start(bf16[16,2048]{1,0:T(8,128)(2,1)S(1)} %get-tuple-element.39), channel_id=1, source_target_pairs={{0,8},{4,12},{8,0},{12,4},{1,9},{5,13},{9,1},{13,5},{2,10},{6,14},... | collective-permute-start | bytes 196616 | tf_op jit(solution)/shard_map/ppermute | solution.py:354
  34.0 4.0 %collective-permute-start.14 = (bf16[16,2048]{1,0:T(8,128)(2,1)S(1)}, bf16[16,2048]{1,0:T(8,128)(2,1)S(1)}, u32[]{:S(2)}, u32[]{:S(2)}) collective-permute-start(bf16[16,2048]{1,0:T(8,128)(2,1)S(1)} %get-tuple-element.40), channel_id=1, source_target_pairs={{0,12},{4,8},{8,4},{12,0},{1,13},{5,9},{9,5},{13,1},{2,14},{6,10},... | collective-permute-start | bytes 196616 | tf_op jit(solution)/shard_map/ppermute | solution.py:354

commit v3 on v2

--- a/solution.py
+++ b/solution.py
@@ -81,40 +81,50 @@
     lengths = jnp.concatenate([column_of(length, requests)] * group, axis=0)
     valid = lax.broadcasted_iota(jnp.int32, (rows, longest), 1) < lengths
     ids = column_of(adapter, requests).astype(F32)
+    scores, own, fresh_value = {}, {}, {}
     for r in order:
         head = jnp.bitwise_xor(me, r)
         mine = pl.ds(pl.multiple_of(head * dim, dim), dim)
         q32 = q_buf[:, pl.ds(pl.multiple_of(head * width, width), width)].astype(F32)
         queries = jnp.concatenate([q32[:, h * dim : (h + 1) * dim] for h in range(group)], axis=0)
         fresh_key = jnp.concatenate([fk_buf[:, mine].astype(F32)] * group, axis=0)
-        fresh_value = jnp.concatenate([fv_buf[:, mine].astype(F32)] * group, axis=0)
-        own = jnp.sum(queries * fresh_key, axis=1, keepdims=True) * scaling
+        fresh_value[r] = jnp.concatenate([fv_buf[:, mine].astype(F32)] * group, axis=0)
+        own[r] = jnp.sum(queries * fresh_key, axis=1, keepdims=True) * scaling
+        scores[r] = queries.astype(BF16)
+    for r in order:
         keys_in[r].wait()
+    for r in order:
         every = lax.dot_general(
-            queries.astype(BF16),
+            scores[r],
             k_buf[r].reshape(requests * longest, dim),
             (((1,), (1,)), ((), ())),
             preferred_element_type=F32,
         )
-        scores = every[:, :longest]
+        picked = every[:, :longest]
         for i in range(1, requests):
-            scores = jnp.where(request == i, every[:, i * longest : (i + 1) * longest], scores)
-        scores = jnp.where(valid, scores * scaling, -1e30)
-        highest = jnp.maximum(jnp.max(scores, axis=1, keepdims=True), own)
-        exponent = jnp.where(valid, jnp.exp(scores - highest), 0.0)
-        own_exp = jnp.exp(own - highest)
-        total = jnp.sum(exponent, axis=1, keepdims=True) + own_exp
-        weights = exponent / total
-        own_weight = (own_exp / total).astype(BF16).astype(F32)
-        spread = jnp.concatenate(
+            picked = jnp.where(request == i, every[:, i * longest : (i + 1) * longest], picked)
+        scores[r] = jnp.where(valid, picked * scaling, -1e30)
+    highest = {r: jnp.maximum(jnp.max(scores[r], axis=1, keepdims=True), own[r]) for r in order}
+    exponent = {r: jnp.where(valid, jnp.exp(scores[r] - highest[r]), 0.0) for r in order}
+    own_exp = {r: jnp.exp(own[r] - highest[r]) for r in order}
+    inverse = {
+        r: 1.0 / (jnp.sum(exponent[r], axis=1, keepdims=True) + own_exp[r]) for r in order
+    }
+    spread = {}
+    for r in order:
+        weights = exponent[r] * inverse[r]
+        spread[r] = jnp.concatenate(
             [jnp.where(request == i, weights, 0.0) for i in range(requests)], axis=1
         ).astype(BF16)
+    for r in order:
         values_in[r].wait()
+    for r in order:
+        own_weight = (own_exp[r] * inverse[r]).astype(BF16).astype(F32)
         result = (
             jnp.dot(
-                spread, v_buf[r].reshape(requests * longest, dim), preferred_element_type=F32
+                spread[r], v_buf[r].reshape(requests * longest, dim), preferred_element_type=F32
             )
-            + own_weight * fresh_value
+            + own_weight * fresh_value[r]
         )
         pieces = [result[h * requests : (h + 1) * requests] for h in range(group)]
         outs[r][...] = jnp.concatenate(pieces + [ids], axis=1).astype(BF16)
@@ -287,42 +297,40 @@
     )(*chosen, weight)
 
 
-def up_kernel(ranks, l0, l1, l2, l3, slot_ref, up_ref, *outs):
-    local = up_ref.shape[0]
+def up_kernel(ranks, l0, l1, l2, l3, slot_ref, up_ref, *outs, tile):
+    local, _, width = up_ref.shape
     low = l0[...].astype(F32)
     for share in (l1, l2, l3):
         low = low + share[...].astype(F32)
     slot = slot_ref[...]
     lane = lax.broadcasted_iota(jnp.int32, low.shape, 1)
-    total = None
+    kept = []
     for a in range(local):
         rank = ranks[lax.axis_index("batch") * local + a]
         factor = ADAPTER_SCALE / jnp.full(low.shape, rank, jnp.int32).astype(F32)
-        kept = jnp.where((slot == a) & (lane < rank), low * factor, 0.0).astype(BF16)
-        product = jnp.dot(kept, up_ref[a], preferred_element_type=F32)
-        total = product if total is None else total + product
-    adapted = total.astype(BF16)
+        kept.append(jnp.where((slot == a) & (lane < rank), low * factor, 0.0).astype(BF16))
     cap = outs[0].shape[0]
-    for r, out in enumerate(outs):
-        out[...] = adapted[r * cap : (r + 1) * cap]
+    for start in range(0, width, tile):
+        span = slice(start, start + tile)
+        total = jnp.dot(kept[0], up_ref[0, :, span], preferred_element_type=F32)
+        for a in range(1, local):
+            total = total + jnp.dot(kept[a], up_ref[a, :, span], preferred_element_type=F32)
+        adapted = total.astype(BF16)
+        for r, out in enumerate(outs):
+            out[:, span] = adapted[r * cap : (r + 1) * cap]
 
 
 def up(ranks, shares, slot, weight, parts, tile=512):
     local, rank, width = weight.shape
     rows = slot.shape[0]
     cap = rows // parts
-    tiles = width // tile
-    whole = pl.BlockSpec((rows, rank), lambda j, *_: (0, 0))
+    vmem = pl.BlockSpec(memory_space=pltpu.VMEM)
     return pl.pallas_call(
-        up_kernel,
-        grid_spec=pltpu.PrefetchScalarGridSpec(
-            num_scalar_prefetch=1,
-            grid=(tiles,),
-            in_specs=[whole] * 5 + [pl.BlockSpec((local, rank, tile), lambda j, *_: (0, 0, j))],
-            out_specs=[pl.BlockSpec((cap, tile), lambda j, *_: (0, j))] * parts,
-        ),
+        functools.partial(up_kernel, tile=tile),
+        in_specs=[pl.BlockSpec(memory_space=pltpu.SMEM)] + [vmem] * 6,
+        out_specs=[vmem] * parts,
         out_shape=[sds((cap, width))] * parts,
-        compiler_params=params(1),
+        compiler_params=params(),
         cost_estimate=cost(2**34, weight.size * 2),
         name="up",
     )(ranks, *shares, slot, weight)

time: 39.4 us -> 38.3 us (0.972)
  Pallas kernels: 15.8 us -> 14 us
  waiting for transfers between devices: 7.12 us -> 7.84 us
    pallas_call x1, Pallas kernels: 3.7 us -> 2.63 us  [attend_blocks(): pl.pallas_call(functools.partial(attend_kernel, kv=kv), in_specs=[hbm] *...]
    pallas_call x1, Pallas kernels: 1.71 us -> 0.99 us  [up(): pl.pallas_call(functools.partial(up_kernel, tile=tile), in_specs=[pl.Bloc...]
    ppermute x15, waiting for transfers between devices: 7.12 us -> 7.84 us  [across(): return lax.ppermute(value, axis, [(i, i ^ r) for i in range(n)])]
  transfers between devices with their start and end apart: 15 -> 15, of which waited for: 5 -> 5; matrix products, arithmetic and copies ran while one was open for 0% -> 0% of each run, Pallas kernels for 28% -> 27%
where the time goes in v3:
time: 38.3 us; the launch traced here: 38.2 us
  starting transfers between devices  16.1 us (42%)
  Pallas kernels  14 us (37%)
  waiting for transfers between devices  7.84 us (20%)
    ppermute x15, starting transfers between devices, across(): return lax.ppermute(value, axis, [(i, i ^ r) for i in range(n)])  16.1 us
    pallas_call x3, Pallas kernels, project(): pl.pallas_call(functools.partial(project_kernel, which=which, tile=tile,...  8.86 us
    ppermute x15, waiting for transfers between devices, across(): return lax.ppermute(value, axis, [(i, i ^ r) for i in range(n)])  7.84 us
    pallas_call x1, Pallas kernels, attend_blocks(): pl.pallas_call(functools.partial(attend_kernel, kv=kv), in_specs=[hbm] *...  2.63 us
    pallas_call x1, Pallas kernels, up(): pl.pallas_call(functools.partial(up_kernel, tile=tile), in_specs=[pl.Bloc...  0.99 us
    pallas_call x1, Pallas kernels, finish(): pl.pallas_call(finish_kernel, in_specs=[vmem] * 8, out_specs=vmem, out_sh...  0.82 us
  transfers between devices with their start and end apart: 15, of which 5 were waited for; matrix products, arithmetic and copies ran while one was open for 0% of the time, Pallas kernels for 27%

profile of v3, /device:TPU:0, one launch (start us, length us, event | category | flops | bytes accessed | tf_op | source)
XLA Modules:
  0.0 38.2 jit_solution(5380160569592759700)
XLA Ops:
  0.0 2.6 %attend.1 = (bf16[8,1152]{1,0:T(8,128)(2,1)S(1)}, bf16[8,1152]{1,0:T(8,128)(2,1)S(1)}, bf16[8,1152]{1,0:T(8,128)(2,1)S(1)}, bf16[8,1152]{1,0:T(8,128)(2,1)S(1)}) custom-call(s32[8]{0:T(128)} %refs_0_.1, s32[8]{0:T(128)} %refs_1_.4, bf16[8,4096]{1,0:T(8,128)(2,1)} %refs_2_.1, bf16[8,512]{1,0:T(8,128)(2,1)} %refs_3_.1, bf16[8,512]{1,0:T(8,128)(2,1)} %refs_4_.1, ...), custom_call_target="tpu_custom_call" | custom-call | flops 2147483648 | bytes 2097152 | tf_op jit(solution)/shard_map/attend/pallas_call | solution.py:137
  2.6 3.1 %collective-permute-start = (bf16[8,1152]{1,0:T(8,128)(2,1)S(1)}, bf16[8,1152]{1,0:T(8,128)(2,1)S(1)}, u32[]{:S(2)}, u32[]{:S(2)}) collective-permute-start(bf16[8,1152]{1,0:T(8,128)(2,1)S(1)} %get-tuple-element.24), channel_id=1, source_target_pairs={{0,1},{1,0},{2,3},{3,2},{4,5},{5,4},{6,7},{7,6},{8,9},{9,8},{10,11... | collective-permute-start | bytes 55304 | tf_op jit(solution)/shard_map/ppermute | solution.py:362
  5.7 2.6 %collective-permute-start.1 = (bf16[8,1152]{1,0:T(8,128)(2,1)S(1)}, bf16[8,1152]{1,0:T(8,128)(2,1)S(1)}, u32[]{:S(2)}, u32[]{:S(2)}) collective-permute-start(bf16[8,1152]{1,0:T(8,128)(2,1)S(1)} %get-tuple-element.25), channel_id=1, source_target_pairs={{0,2},{1,3},{2,0},{3,1},{4,6},{5,7},{6,4},{7,5},{8,10},{9,11},{10,... | collective-permute-start | bytes 55304 | tf_op jit(solution)/shard_map/ppermute | solution.py:362
  8.3 2.2 %collective-permute-done.1.x2 = bf16[8,1152]{1,0:T(8,128)(2,1)S(1)} collective-permute-done((bf16[8,1152]{1,0:T(8,128)(2,1)S(1)}, bf16[8,1152]{1,0:T(8,128)(2,1)S(1)}, u32[]{:S(2)}, u32[]{:S(2)}) %collective-permute-start.1) | collective-permute-done | bytes 18464 | tf_op jit(solution)/shard_map/ppermute | solution.py:362
  10.5 3.3 %collective-permute-done.2.x3 = bf16[8,1152]{1,0:T(8,128)(2,1)S(1)} collective-permute-done((bf16[8,1152]{1,0:T(8,128)(2,1)S(1)}, bf16[8,1152]{1,0:T(8,128)(2,1)S(1)}, u32[]{:S(2)}, u32[]{:S(2)}) %collective-permute-start.2) | collective-permute-done | bytes 18464 | tf_op jit(solution)/shard_map/ppermute | solution.py:362
  13.9 0.4 %route.1 = (bf16[32,1024]{1,0:T(8,128)(2,1)S(1)}, bf16[32,128]{1,0:T(8,128)(2,1)S(1)}, bf16[16,1152]{1,0:T(8,128)(2,1)S(1)}, bf16[16,1152]{1,0:T(8,128)(2,1)S(1)...) custom-call(bf16[8,1152]{1,0:T(8,128)(2,1)S(1)} %get-tuple-element.23.x0, ...), custom_call_target="tpu_custom_call" | custom-call | flops 1048576 | bytes 294912 | tf_op jit(solution)/shard_map/route/pallas_call | solution.py:196
  14.3 0.1 collective-permute-start.6
  14.4 1.6 %collective-permute-start.7 = (bf16[16,1152]{1,0:T(8,128)(2,1)S(1)}, bf16[16,1152]{1,0:T(8,128)(2,1)S(1)}, u32[]{:S(2)}, u32[]{:S(2)}) collective-permute-start(bf16[16,1152]{1,0:T(8,128)(2,1)S(1)} %get-tuple-element.33), channel_id=1, source_target_pairs={{0,8},{4,12},{8,0},{12,4},{1,9},{5,13},{9,1},{13,5},{2,10},{6,14},... | collective-permute-start | bytes 110600 | tf_op jit(solution)/shard_map/ppermute | solution.py:362
  15.9 0.3 collective-permute-start.8
  16.2 3.8 %project.4 = (bf16[32,2048]{1,0:T(8,128)(2,1)S(1)}, bf16[32,2048]{1,0:T(8,128)(2,1)S(1)}) custom-call(bf16[32,1024]{1,0:T(8,128)(2,1)S(1)} %get-tuple-element.28.refs_0_, bf16[1024,8192]{1,0:T(8,128)(2,1)} %refs_1_.7), custom_call_target="tpu_custom_call" | custom-call | flops 268435456 | bytes 8388608 | tf_op jit(solution)/shard_map/project/pallas_call | solution.py:251
  20.1 0.1 collective-permute-start.4
  20.2 0.3 down.1
  20.5 0.8 %collective-permute-start.10 = (bf16[64,128]{1,0:T(8,128)(2,1)S(1)}, bf16[64,128]{1,0:T(8,128)(2,1)S(1)}, u32[]{:S(2)}, u32[]{:S(2)}) collective-permute-start(bf16[64,128]{1,0:T(8,128)(2,1)S(1)} %get-tuple-element.35.l0), channel_id=1, source_target_pairs={{0,2},{1,3},{2,0},{3,1},{4,6},{5,7},{6,4},{7,5},{8,10},{9,11},{10,... | collective-permute-start | bytes 49160 | tf_op jit(solution)/shard_map/ppermute | solution.py:362
  21.3 3.6 %collective-permute-start.11 = (bf16[64,128]{1,0:T(8,128)(2,1)S(1)}, bf16[64,128]{1,0:T(8,128)(2,1)S(1)}, u32[]{:S(2)}, u32[]{:S(2)}) collective-permute-start(bf16[64,128]{1,0:T(8,128)(2,1)S(1)} %get-tuple-element.35.l0), channel_id=1, source_target_pairs={{0,3},{1,2},{2,1},{3,0},{4,7},{5,6},{6,5},{7,4},{8,11},{9,10},{10,... | collective-permute-start | bytes 49160 | tf_op jit(solution)/shard_map/ppermute | solution.py:362
  24.9 2.0 %collective-permute-start.3 = (bf16[32,2048]{1,0:T(8,128)(2,1)S(1)}, bf16[32,2048]{1,0:T(8,128)(2,1)S(1)}, u32[]{:S(2)}, u32[]{:S(2)}) collective-permute-start(bf16[32,2048]{1,0:T(8,128)(2,1)S(1)} %get-tuple-element.29), channel_id=1, source_target_pairs={{0,1},{1,0},{2,3},{3,2},{4,5},{5,4},{6,7},{7,6},{8,9},{9,8},{10,11... | collective-permute-start | bytes 393224 | tf_op jit(solution)/shard_map/ppermute | solution.py:362
  27.0 2.5 %project.5 = bf16[32,2048]{1,0:T(8,128)(2,1)S(1)} custom-call(bf16[32,1024]{1,0:T(8,128)(2,1)S(1)} %get-tuple-element.28.refs_0_, bf16[1024,8192]{1,0:T(8,128)(2,1)} %refs_1_.7, bf16[32,2048]{1,0:T(8,128)(2,1)S(1)} %collective-permute-done.4.refs_2_), custom_call_target="tpu_custom_call" | custom-call | flops 134217728 | bytes 4194304 | tf_op jit(solution)/shard_map/project/pallas_call | solution.py:251
  29.6 1.0 %up.1 = (bf16[16,2048]{1,0:T(8,128)(2,1)S(1)}, bf16[16,2048]{1,0:T(8,128)(2,1)S(1)}, bf16[16,2048]{1,0:T(8,128)(2,1)S(1)}, bf16[16,2048]{1,0:T(8,128)(2,1)S(1)}) custom-call(s32[16]{0:T(128)S(1)} %copy-done.2, bf16[64,128]{1,0:T(8,128)(2,1)S(1)} %get-tuple-element.35.l0, bf16[64,128]{1,0:T(8,128)(2,1)S(1)} %collective-permute-done.9.l1, ...), custom_call_target="tpu_custom_call" | custom-call | flops 17179869184 | bytes 2097152 | tf_op jit(solution)/shard_map/up/pallas_call | solution.py:328
  30.7 1.6 %collective-permute-start.13 = (bf16[16,2048]{1,0:T(8,128)(2,1)S(1)}, bf16[16,2048]{1,0:T(8,128)(2,1)S(1)}, u32[]{:S(2)}, u32[]{:S(2)}) collective-permute-start(bf16[16,2048]{1,0:T(8,128)(2,1)S(1)} %get-tuple-element.39), channel_id=1, source_target_pairs={{0,8},{4,12},{8,0},{12,4},{1,9},{5,13},{9,1},{13,5},{2,10},{6,14},... | collective-permute-start | bytes 196616 | tf_op jit(solution)/shard_map/ppermute | solution.py:362
  32.3 0.3 collective-permute-start.14
  32.6 2.5 %project.3.y0 = bf16[32,2048]{1,0:T(8,128)(2,1)S(1)} custom-call(bf16[32,1024]{1,0:T(8,128)(2,1)S(1)} %get-tuple-element.28.refs_0_, bf16[1024,8192]{1,0:T(8,128)(2,1)} %refs_1_.7), custom_call_target="tpu_custom_call" | custom-call | flops 134217728 | bytes 4194304 | tf_op jit(solution)/shard_map/project/pallas_call | solution.py:251
  35.1 0.1 collective-permute-done.13.a2
  35.2 1.1 %collective-permute-done.14.a3 = bf16[16,2048]{1,0:T(8,128)(2,1)S(1)} collective-permute-done((bf16[16,2048]{1,0:T(8,128)(2,1)S(1)}, bf16[16,2048]{1,0:T(8,128)(2,1)S(1)}, u32[]{:S(2)}, u32[]{:S(2)}) %collective-permute-start.14) | collective-permute-done | bytes 65568 | tf_op jit(solution)/shard_map/ppermute | solution.py:362
  36.3 1.1 %collective-permute-done.5.y2 = bf16[32,2048]{1,0:T(8,128)(2,1)S(1)} collective-permute-done((bf16[32,2048]{1,0:T(8,128)(2,1)S(1)}, bf16[32,2048]{1,0:T(8,128)(2,1)S(1)}, u32[]{:S(2)}, u32[]{:S(2)}) %collective-permute-start.5) | collective-permute-done | bytes 131104 | tf_op jit(solution)/shard_map/ppermute | solution.py:362
  37.4 0.8 %finish.1 = bf16[32,2048]{1,0:T(8,128)(2,1)} custom-call(bf16[32,128]{1,0:T(8,128)(2,1)S(1)} %get-tuple-element.27.pick_ref, bf16[32,2048]{1,0:T(8,128)(2,1)S(1)} %project.3.y0, bf16[32,2048]{1,0:T(8,128)(2,1)S(1)} %collective-permute-done.3.y1, bf16[32,2048]{1,0:T(8,128)(2,1)S(1)} %collective-permute-done.5.y2, bf16[16,2048]{1,0:T(8,128)(2,1)S(1)} %get-tuple-element.37.a0, ...), custom_call_target="tpu_custom_call" | custom-call | flops 16777216 | bytes 1048576 | tf_op jit(solution)/shard_map/finish/pallas_call | solution.py:349
  (20 shorter events, 0.2 us)
Async XLA Ops:
  0.0 20.2 %copy-start.1 = (bf16[4,1024,128]{2,1,0:T(8,128)(2,1)S(1)}, bf16[4,1024,128]{2,1,0:T(8,128)(2,1)}, u32[]{:S(2)}) copy-start(bf16[4,1024,128]{2,1,0:T(8,128)(2,1)} %down_ref.1) | copy-start | bytes 3145732
  2.6 5.7 %collective-permute-start = (bf16[8,1152]{1,0:T(8,128)(2,1)S(1)}, bf16[8,1152]{1,0:T(8,128)(2,1)S(1)}, u32[]{:S(2)}, u32[]{:S(2)}) collective-permute-start(bf16[8,1152]{1,0:T(8,128)(2,1)S(1)} %get-tuple-element.24), channel_id=1, source_target_pairs={{0,1},{1,0},{2,3},{3,2},{4,5},{5,4},{6,7},{7,6},{8,9},{9,8},{10,11... | collective-permute-start | bytes 55304 | tf_op jit(solution)/shard_map/ppermute | solution.py:362
  5.7 4.8 %collective-permute-start.1 = (bf16[8,1152]{1,0:T(8,128)(2,1)S(1)}, bf16[8,1152]{1,0:T(8,128)(2,1)S(1)}, u32[]{:S(2)}, u32[]{:S(2)}) collective-permute-start(bf16[8,1152]{1,0:T(8,128)(2,1)S(1)} %get-tuple-element.25), channel_id=1, source_target_pairs={{0,2},{1,3},{2,0},{3,1},{4,6},{5,7},{6,4},{7,5},{8,10},{9,11},{10,... | collective-permute-start | bytes 55304 | tf_op jit(solution)/shard_map/ppermute | solution.py:362
  8.3 5.6 %collective-permute-start.2 = (bf16[8,1152]{1,0:T(8,128)(2,1)S(1)}, bf16[8,1152]{1,0:T(8,128)(2,1)S(1)}, u32[]{:S(2)}, u32[]{:S(2)}) collective-permute-start(bf16[8,1152]{1,0:T(8,128)(2,1)S(1)} %get-tuple-element.26), channel_id=1, source_target_pairs={{0,3},{1,2},{2,1},{3,0},{4,7},{5,6},{6,5},{7,4},{8,11},{9,10},{10,... | collective-permute-start | bytes 55304 | tf_op jit(solution)/shard_map/ppermute | solution.py:362
  14.3 5.8 %collective-permute-start.6 = (bf16[16,1152]{1,0:T(8,128)(2,1)S(1)}, bf16[16,1152]{1,0:T(8,128)(2,1)S(1)}, u32[]{:S(2)}, u32[]{:S(2)}) collective-permute-start(bf16[16,1152]{1,0:T(8,128)(2,1)S(1)} %get-tuple-element.32), channel_id=1, source_target_pairs={{0,4},{4,0},{8,12},{12,8},{1,5},{5,1},{9,13},{13,9},{2,6},{6,2},{1... | collective-permute-start | bytes 110600 | tf_op jit(solution)/shard_map/ppermute | solution.py:362
  14.4 5.8 %collective-permute-start.7 = (bf16[16,1152]{1,0:T(8,128)(2,1)S(1)}, bf16[16,1152]{1,0:T(8,128)(2,1)S(1)}, u32[]{:S(2)}, u32[]{:S(2)}) collective-permute-start(bf16[16,1152]{1,0:T(8,128)(2,1)S(1)} %get-tuple-element.33), channel_id=1, source_target_pairs={{0,8},{4,12},{8,0},{12,4},{1,9},{5,13},{9,1},{13,5},{2,10},{6,14},... | collective-permute-start | bytes 110600 | tf_op jit(solution)/shard_map/ppermute | solution.py:362
  15.9 4.2 %collective-permute-start.8 = (bf16[16,1152]{1,0:T(8,128)(2,1)S(1)}, bf16[16,1152]{1,0:T(8,128)(2,1)S(1)}, u32[]{:S(2)}, u32[]{:S(2)}) collective-permute-start(bf16[16,1152]{1,0:T(8,128)(2,1)S(1)} %get-tuple-element.34), channel_id=1, source_target_pairs={{0,12},{4,8},{8,4},{12,0},{1,13},{5,9},{9,5},{13,1},{2,14},{6,10},... | collective-permute-start | bytes 110600 | tf_op jit(solution)/shard_map/ppermute | solution.py:362
  20.1 6.9 %collective-permute-start.4 = (bf16[32,2048]{1,0:T(8,128)(2,1)S(1)}, bf16[32,2048]{1,0:T(8,128)(2,1)S(1)}, u32[]{:S(2)}, u32[]{:S(2)}) collective-permute-start(bf16[32,2048]{1,0:T(8,128)(2,1)S(1)} %get-tuple-element.30), channel_id=1, source_target_pairs={{0,1},{1,0},{2,3},{3,2},{4,5},{5,4},{6,7},{7,6},{8,9},{9,8},{10,11... | collective-permute-start | bytes 393224 | tf_op jit(solution)/shard_map/ppermute | solution.py:362
  20.5 9.1 %copy-start = (bf16[4,128,2048]{2,1,0:T(8,128)(2,1)S(1)}, bf16[4,128,2048]{2,1,0:T(8,128)(2,1)}, u32[]{:S(2)}) copy-start(bf16[4,128,2048]{2,1,0:T(8,128)(2,1)} %up_ref.1) | copy-start | bytes 6291460
  20.5 9.1 %copy-start.2 = (s32[16]{0:T(128)S(1)}, s32[16]{0:T(128)}, u32[]{:S(2)}) copy-start(s32[16]{0:T(128)} %ranks.1) | copy-start | bytes 196
  20.5 9.1 %collective-permute-start.10 = (bf16[64,128]{1,0:T(8,128)(2,1)S(1)}, bf16[64,128]{1,0:T(8,128)(2,1)S(1)}, u32[]{:S(2)}, u32[]{:S(2)}) collective-permute-start(bf16[64,128]{1,0:T(8,128)(2,1)S(1)} %get-tuple-element.35.l0), channel_id=1, source_target_pairs={{0,2},{1,3},{2,0},{3,1},{4,6},{5,7},{6,4},{7,5},{8,10},{9,11},{10,... | collective-permute-start | bytes 49160 | tf_op jit(solution)/shard_map/ppermute | solution.py:362
  21.3 8.3 %collective-permute-start.11 = (bf16[64,128]{1,0:T(8,128)(2,1)S(1)}, bf16[64,128]{1,0:T(8,128)(2,1)S(1)}, u32[]{:S(2)}, u32[]{:S(2)}) collective-permute-start(bf16[64,128]{1,0:T(8,128)(2,1)S(1)} %get-tuple-element.35.l0), channel_id=1, source_target_pairs={{0,3},{1,2},{2,1},{3,0},{4,7},{5,6},{6,5},{7,4},{8,11},{9,10},{10,... | collective-permute-start | bytes 49160 | tf_op jit(solution)/shard_map/ppermute | solution.py:362
  24.9 4.7 %collective-permute-start.9 = (bf16[64,128]{1,0:T(8,128)(2,1)S(1)}, bf16[64,128]{1,0:T(8,128)(2,1)S(1)}, u32[]{:S(2)}, u32[]{:S(2)}) collective-permute-start(bf16[64,128]{1,0:T(8,128)(2,1)S(1)} %get-tuple-element.35.l0), channel_id=1, source_target_pairs={{0,1},{1,0},{2,3},{3,2},{4,5},{5,4},{6,7},{7,6},{8,9},{9,8},{10,11... | collective-permute-start | bytes 49160 | tf_op jit(solution)/shard_map/ppermute | solution.py:362
  24.9 11.4 %collective-permute-start.3 = (bf16[32,2048]{1,0:T(8,128)(2,1)S(1)}, bf16[32,2048]{1,0:T(8,128)(2,1)S(1)}, u32[]{:S(2)}, u32[]{:S(2)}) collective-permute-start(bf16[32,2048]{1,0:T(8,128)(2,1)S(1)} %get-tuple-element.29), channel_id=1, source_target_pairs={{0,1},{1,0},{2,3},{3,2},{4,5},{5,4},{6,7},{7,6},{8,9},{9,8},{10,11... | collective-permute-start | bytes 393224 | tf_op jit(solution)/shard_map/ppermute | solution.py:362
  29.5 7.9 %collective-permute-start.5 = (bf16[32,2048]{1,0:T(8,128)(2,1)S(1)}, bf16[32,2048]{1,0:T(8,128)(2,1)S(1)}, u32[]{:S(2)}, u32[]{:S(2)}) collective-permute-start(bf16[32,2048]{1,0:T(8,128)(2,1)S(1)} %project.5), channel_id=1, source_target_pairs={{0,2},{1,3},{2,0},{3,1},{4,6},{5,7},{6,4},{7,5},{8,10},{9,11},{10,... | collective-permute-start | bytes 393224 | tf_op jit(solution)/shard_map/ppermute | solution.py:362
  30.6 4.5 %collective-permute-start.12 = (bf16[16,2048]{1,0:T(8,128)(2,1)S(1)}, bf16[16,2048]{1,0:T(8,128)(2,1)S(1)}, u32[]{:S(2)}, u32[]{:S(2)}) collective-permute-start(bf16[16,2048]{1,0:T(8,128)(2,1)S(1)} %get-tuple-element.38), channel_id=1, source_target_pairs={{0,4},{4,0},{8,12},{12,8},{1,5},{5,1},{9,13},{13,9},{2,6},{6,2},{1... | collective-permute-start | bytes 196616 | tf_op jit(solution)/shard_map/ppermute | solution.py:362
  30.7 4.5 %collective-permute-start.13 = (bf16[16,2048]{1,0:T(8,128)(2,1)S(1)}, bf16[16,2048]{1,0:T(8,128)(2,1)S(1)}, u32[]{:S(2)}, u32[]{:S(2)}) collective-permute-start(bf16[16,2048]{1,0:T(8,128)(2,1)S(1)} %get-tuple-element.39), channel_id=1, source_target_pairs={{0,8},{4,12},{8,0},{12,4},{1,9},{5,13},{9,1},{13,5},{2,10},{6,14},... | collective-permute-start | bytes 196616 | tf_op jit(solution)/shard_map/ppermute | solution.py:362
  32.3 4.0 %collective-permute-start.14 = (bf16[16,2048]{1,0:T(8,128)(2,1)S(1)}, bf16[16,2048]{1,0:T(8,128)(2,1)S(1)}, u32[]{:S(2)}, u32[]{:S(2)}) collective-permute-start(bf16[16,2048]{1,0:T(8,128)(2,1)S(1)} %get-tuple-element.40), channel_id=1, source_target_pairs={{0,12},{4,8},{8,4},{12,0},{1,13},{5,9},{9,5},{13,1},{2,14},{6,10},... | collective-permute-start | bytes 196616 | tf_op jit(solution)/shard_map/ppermute | solution.py:362

commit v4 on v3

--- a/solution.py
+++ b/solution.py
@@ -127,7 +127,7 @@
             + own_weight * fresh_value[r]
         )
         pieces = [result[h * requests : (h + 1) * requests] for h in range(group)]
-        outs[r][...] = jnp.concatenate(pieces + [ids], axis=1).astype(BF16)
+        outs[kv - 1 - r][...] = jnp.concatenate(pieces + [ids], axis=1).astype(BF16)
 
 
 def attend_blocks(length, adapter, query, fresh_key, fresh_value, keys, values):
@@ -159,7 +159,7 @@
 def route_kernel(x0, x1, x2, x3, rows_ref, pick_ref, c0, c1, c2, c3, held, *, local, cap):
     me, mine = lax.axis_index("tensor"), lax.axis_index("batch")
     count = x0.shape[0]
-    for r, x in enumerate((x0, x1, x2, x3)):
+    for r, x in zip((3, 2, 1, 0), (x0, x1, x2, x3)):
         held[pl.ds(pl.multiple_of(jnp.bitwise_xor(me, r) * count, count), count), :] = x[
             ...
         ].astype(F32)
@@ -390,7 +390,7 @@
         stored_keys,
         stored_values,
     )
-    blocks = [blocks[0]] + [across(blocks[r], "tensor", r) for r in (1, 2, 3)]
+    blocks = [across(blocks[3 - r], "tensor", r) for r in (3, 2, 1)] + [blocks[3]]
     rows, pick, *chosen = route(blocks, local, cap)
 
     gathered = [chosen[0]] + [across(chosen[r], "batch", r) for r in (1, 2, 3)]

time: 38.3 us -> 37.1 us (0.969)
  waiting for transfers between devices: 7.84 us -> 5.24 us
  starting transfers between devices: 16.1 us -> 17.5 us
    ppermute x15, waiting for transfers between devices: 7.84 us -> 5.24 us  [across(): return lax.ppermute(value, axis, [(i, i ^ r) for i in range(n)])]
    ppermute x15, starting transfers between devices: 16.1 us -> 17.5 us  [across(): return lax.ppermute(value, axis, [(i, i ^ r) for i in range(n)])]
  transfers between devices with their start and end apart: 15 -> 15, of which waited for: 5 -> 4; matrix products, arithmetic and copies ran while one was open for 0% -> 0% of each run, Pallas kernels for 27% -> 28%
where the time goes in v4:
time: 37.1 us; the launch traced here: 36.9 us
  starting transfers between devices  17.5 us (47%)
  Pallas kernels  14 us (38%)
  waiting for transfers between devices  5.24 us (14%)
    ppermute x15, starting transfers between devices, across(): return lax.ppermute(value, axis, [(i, i ^ r) for i in range(n)])  17.5 us
    pallas_call x3, Pallas kernels, project(): pl.pallas_call(functools.partial(project_kernel, which=which, tile=tile,...  8.86 us
    ppermute x15, waiting for transfers between devices, across(): return lax.ppermute(value, axis, [(i, i ^ r) for i in range(n)])  5.24 us
    pallas_call x1, Pallas kernels, attend_blocks(): pl.pallas_call(functools.partial(attend_kernel, kv=kv), in_specs=[hbm] *...  2.63 us
    pallas_call x1, Pallas kernels, up(): pl.pallas_call(functools.partial(up_kernel, tile=tile), in_specs=[pl.Bloc...  0.98 us
    pallas_call x1, Pallas kernels, finish(): pl.pallas_call(finish_kernel, in_specs=[vmem] * 8, out_specs=vmem, out_sh...  0.83 us
  transfers between devices with their start and end apart: 15, of which 4 were waited for; matrix products, arithmetic and copies ran while one was open for 0% of the time, Pallas kernels for 28%

profile of v4, /device:TPU:0, one launch (start us, length us, event | category | flops | bytes accessed | tf_op | source)
XLA Modules:
  0.0 36.9 jit_solution(109722436730926931)
XLA Ops:
  0.0 2.6 %attend.1 = (bf16[8,1152]{1,0:T(8,128)(2,1)S(1)}, bf16[8,1152]{1,0:T(8,128)(2,1)S(1)}, bf16[8,1152]{1,0:T(8,128)(2,1)S(1)}, bf16[8,1152]{1,0:T(8,128)(2,1)S(1)}) custom-call(s32[8]{0:T(128)} %refs_0_.1, s32[8]{0:T(128)} %refs_1_.4, bf16[8,4096]{1,0:T(8,128)(2,1)} %refs_2_.1, bf16[8,512]{1,0:T(8,128)(2,1)} %refs_3_.1, bf16[8,512]{1,0:T(8,128)(2,1)} %refs_4_.1, ...), custom_call_target="tpu_custom_call" | custom-call | flops 2147483648 | bytes 2097152 | tf_op jit(solution)/shard_map/attend/pallas_call | solution.py:137
  2.6 5.1 %collective-permute-start = (bf16[8,1152]{1,0:T(8,128)(2,1)S(1)}, bf16[8,1152]{1,0:T(8,128)(2,1)S(1)}, u32[]{:S(2)}, u32[]{:S(2)}) collective-permute-start(bf16[8,1152]{1,0:T(8,128)(2,1)S(1)} %get-tuple-element.23), channel_id=1, source_target_pairs={{0,3},{1,2},{2,1},{3,0},{4,7},{5,6},{6,5},{7,4},{8,11},{9,10},{10,... | collective-permute-start | bytes 55304 | tf_op jit(solution)/shard_map/ppermute | solution.py:362
  7.8 0.6 %collective-permute-start.2 = (bf16[8,1152]{1,0:T(8,128)(2,1)S(1)}, bf16[8,1152]{1,0:T(8,128)(2,1)S(1)}, u32[]{:S(2)}, u32[]{:S(2)}) collective-permute-start(bf16[8,1152]{1,0:T(8,128)(2,1)S(1)} %get-tuple-element.25), channel_id=1, source_target_pairs={{0,1},{1,0},{2,3},{3,2},{4,5},{5,4},{6,7},{7,6},{8,9},{9,8},{10,11... | collective-permute-start | bytes 55304 | tf_op jit(solution)/shard_map/ppermute | solution.py:362
  8.4 1.1 %collective-permute-done.x0 = bf16[8,1152]{1,0:T(8,128)(2,1)S(1)} collective-permute-done((bf16[8,1152]{1,0:T(8,128)(2,1)S(1)}, bf16[8,1152]{1,0:T(8,128)(2,1)S(1)}, u32[]{:S(2)}, u32[]{:S(2)}) %collective-permute-start) | collective-permute-done | bytes 18464 | tf_op jit(solution)/shard_map/ppermute | solution.py:362
  9.5 2.9 %collective-permute-done.1.x1 = bf16[8,1152]{1,0:T(8,128)(2,1)S(1)} collective-permute-done((bf16[8,1152]{1,0:T(8,128)(2,1)S(1)}, bf16[8,1152]{1,0:T(8,128)(2,1)S(1)}, u32[]{:S(2)}, u32[]{:S(2)}) %collective-permute-start.1) | collective-permute-done | bytes 18464 | tf_op jit(solution)/shard_map/ppermute | solution.py:362
  12.4 0.4 %route.1 = (bf16[32,1024]{1,0:T(8,128)(2,1)S(1)}, bf16[32,128]{1,0:T(8,128)(2,1)S(1)}, bf16[16,1152]{1,0:T(8,128)(2,1)S(1)}, bf16[16,1152]{1,0:T(8,128)(2,1)S(1)...) custom-call(bf16[8,1152]{1,0:T(8,128)(2,1)S(1)} %collective-permute-done.x0, ...), custom_call_target="tpu_custom_call" | custom-call | flops 1048576 | bytes 294912 | tf_op jit(solution)/shard_map/route/pallas_call | solution.py:196
  12.8 0.1 collective-permute-start.6
  12.9 1.6 %collective-permute-start.7 = (bf16[16,1152]{1,0:T(8,128)(2,1)S(1)}, bf16[16,1152]{1,0:T(8,128)(2,1)S(1)}, u32[]{:S(2)}, u32[]{:S(2)}) collective-permute-start(bf16[16,1152]{1,0:T(8,128)(2,1)S(1)} %get-tuple-element.33), channel_id=1, source_target_pairs={{0,8},{4,12},{8,0},{12,4},{1,9},{5,13},{9,1},{13,5},{2,10},{6,14},... | collective-permute-start | bytes 110600 | tf_op jit(solution)/shard_map/ppermute | solution.py:362
  14.5 0.3 collective-permute-start.8
  14.8 3.8 %project.4 = (bf16[32,2048]{1,0:T(8,128)(2,1)S(1)}, bf16[32,2048]{1,0:T(8,128)(2,1)S(1)}) custom-call(bf16[32,1024]{1,0:T(8,128)(2,1)S(1)} %get-tuple-element.28.refs_0_, bf16[1024,8192]{1,0:T(8,128)(2,1)} %refs_1_.7), custom_call_target="tpu_custom_call" | custom-call | flops 268435456 | bytes 8388608 | tf_op jit(solution)/shard_map/project/pallas_call | solution.py:251
  18.6 0.1 collective-permute-start.4
  18.7 0.3 down.1
  19.1 2.1 %collective-permute-start.10 = (bf16[64,128]{1,0:T(8,128)(2,1)S(1)}, bf16[64,128]{1,0:T(8,128)(2,1)S(1)}, u32[]{:S(2)}, u32[]{:S(2)}) collective-permute-start(bf16[64,128]{1,0:T(8,128)(2,1)S(1)} %get-tuple-element.35.l0), channel_id=1, source_target_pairs={{0,2},{1,3},{2,0},{3,1},{4,6},{5,7},{6,4},{7,5},{8,10},{9,11},{10,... | collective-permute-start | bytes 49160 | tf_op jit(solution)/shard_map/ppermute | solution.py:362
  21.2 2.3 %collective-permute-start.11 = (bf16[64,128]{1,0:T(8,128)(2,1)S(1)}, bf16[64,128]{1,0:T(8,128)(2,1)S(1)}, u32[]{:S(2)}, u32[]{:S(2)}) collective-permute-start(bf16[64,128]{1,0:T(8,128)(2,1)S(1)} %get-tuple-element.35.l0), channel_id=1, source_target_pairs={{0,3},{1,2},{2,1},{3,0},{4,7},{5,6},{6,5},{7,4},{8,11},{9,10},{10,... | collective-permute-start | bytes 49160 | tf_op jit(solution)/shard_map/ppermute | solution.py:362
  23.5 2.0 %collective-permute-start.3 = (bf16[32,2048]{1,0:T(8,128)(2,1)S(1)}, bf16[32,2048]{1,0:T(8,128)(2,1)S(1)}, u32[]{:S(2)}, u32[]{:S(2)}) collective-permute-start(bf16[32,2048]{1,0:T(8,128)(2,1)S(1)} %get-tuple-element.29), channel_id=1, source_target_pairs={{0,1},{1,0},{2,3},{3,2},{4,5},{5,4},{6,7},{7,6},{8,9},{9,8},{10,11... | collective-permute-start | bytes 393224 | tf_op jit(solution)/shard_map/ppermute | solution.py:362
  25.5 2.5 %project.5 = bf16[32,2048]{1,0:T(8,128)(2,1)S(1)} custom-call(bf16[32,1024]{1,0:T(8,128)(2,1)S(1)} %get-tuple-element.28.refs_0_, bf16[1024,8192]{1,0:T(8,128)(2,1)} %refs_1_.7, bf16[32,2048]{1,0:T(8,128)(2,1)S(1)} %collective-permute-done.4.refs_2_), custom_call_target="tpu_custom_call" | custom-call | flops 134217728 | bytes 4194304 | tf_op jit(solution)/shard_map/project/pallas_call | solution.py:251
  28.0 1.4 %collective-permute-start.5 = (bf16[32,2048]{1,0:T(8,128)(2,1)S(1)}, bf16[32,2048]{1,0:T(8,128)(2,1)S(1)}, u32[]{:S(2)}, u32[]{:S(2)}) collective-permute-start(bf16[32,2048]{1,0:T(8,128)(2,1)S(1)} %project.5), channel_id=1, source_target_pairs={{0,2},{1,3},{2,0},{3,1},{4,6},{5,7},{6,4},{7,5},{8,10},{9,11},{10,... | collective-permute-start | bytes 393224 | tf_op jit(solution)/shard_map/ppermute | solution.py:362
  29.4 1.0 %up.1 = (bf16[16,2048]{1,0:T(8,128)(2,1)S(1)}, bf16[16,2048]{1,0:T(8,128)(2,1)S(1)}, bf16[16,2048]{1,0:T(8,128)(2,1)S(1)}, bf16[16,2048]{1,0:T(8,128)(2,1)S(1)}) custom-call(s32[16]{0:T(128)S(1)} %copy-done.2, bf16[64,128]{1,0:T(8,128)(2,1)S(1)} %get-tuple-element.35.l0, bf16[64,128]{1,0:T(8,128)(2,1)S(1)} %collective-permute-done.9.l1, ...), custom_call_target="tpu_custom_call" | custom-call | flops 17179869184 | bytes 2097152 | tf_op jit(solution)/shard_map/up/pallas_call | solution.py:328
  30.5 1.6 %collective-permute-start.13 = (bf16[16,2048]{1,0:T(8,128)(2,1)S(1)}, bf16[16,2048]{1,0:T(8,128)(2,1)S(1)}, u32[]{:S(2)}, u32[]{:S(2)}) collective-permute-start(bf16[16,2048]{1,0:T(8,128)(2,1)S(1)} %get-tuple-element.39), channel_id=1, source_target_pairs={{0,8},{4,12},{8,0},{12,4},{1,9},{5,13},{9,1},{13,5},{2,10},{6,14},... | collective-permute-start | bytes 196616 | tf_op jit(solution)/shard_map/ppermute | solution.py:362
  32.1 0.3 collective-permute-start.14
  32.4 2.5 %project.3.y0 = bf16[32,2048]{1,0:T(8,128)(2,1)S(1)} custom-call(bf16[32,1024]{1,0:T(8,128)(2,1)S(1)} %get-tuple-element.28.refs_0_, bf16[1024,8192]{1,0:T(8,128)(2,1)} %refs_1_.7), custom_call_target="tpu_custom_call" | custom-call | flops 134217728 | bytes 4194304 | tf_op jit(solution)/shard_map/project/pallas_call | solution.py:251
  34.9 0.1 collective-permute-done.13.a2
  35.0 1.1 %collective-permute-done.14.a3 = bf16[16,2048]{1,0:T(8,128)(2,1)S(1)} collective-permute-done((bf16[16,2048]{1,0:T(8,128)(2,1)S(1)}, bf16[16,2048]{1,0:T(8,128)(2,1)S(1)}, u32[]{:S(2)}, u32[]{:S(2)}) %collective-permute-start.14) | collective-permute-done | bytes 65568 | tf_op jit(solution)/shard_map/ppermute | solution.py:362
  36.1 0.8 %finish.1 = bf16[32,2048]{1,0:T(8,128)(2,1)} custom-call(bf16[32,128]{1,0:T(8,128)(2,1)S(1)} %get-tuple-element.27.pick_ref, bf16[32,2048]{1,0:T(8,128)(2,1)S(1)} %project.3.y0, bf16[32,2048]{1,0:T(8,128)(2,1)S(1)} %collective-permute-done.3.y1, bf16[32,2048]{1,0:T(8,128)(2,1)S(1)} %collective-permute-done.5.y2, bf16[16,2048]{1,0:T(8,128)(2,1)S(1)} %get-tuple-element.37.a0, ...), custom_call_target="tpu_custom_call" | custom-call | flops 16777216 | bytes 1048576 | tf_op jit(solution)/shard_map/finish/pallas_call | solution.py:349
  (20 shorter events, 0.1 us)
Async XLA Ops:
  0.0 18.7 %copy-start.1 = (bf16[4,1024,128]{2,1,0:T(8,128)(2,1)S(1)}, bf16[4,1024,128]{2,1,0:T(8,128)(2,1)}, u32[]{:S(2)}) copy-start(bf16[4,1024,128]{2,1,0:T(8,128)(2,1)} %down_ref.1) | copy-start | bytes 3145732
  2.6 6.9 %collective-permute-start = (bf16[8,1152]{1,0:T(8,128)(2,1)S(1)}, bf16[8,1152]{1,0:T(8,128)(2,1)S(1)}, u32[]{:S(2)}, u32[]{:S(2)}) collective-permute-start(bf16[8,1152]{1,0:T(8,128)(2,1)S(1)} %get-tuple-element.23), channel_id=1, source_target_pairs={{0,3},{1,2},{2,1},{3,0},{4,7},{5,6},{6,5},{7,4},{8,11},{9,10},{10,... | collective-permute-start | bytes 55304 | tf_op jit(solution)/shard_map/ppermute | solution.py:362
  7.8 4.7 %collective-permute-start.1 = (bf16[8,1152]{1,0:T(8,128)(2,1)S(1)}, bf16[8,1152]{1,0:T(8,128)(2,1)S(1)}, u32[]{:S(2)}, u32[]{:S(2)}) collective-permute-start(bf16[8,1152]{1,0:T(8,128)(2,1)S(1)} %get-tuple-element.24), channel_id=1, source_target_pairs={{0,2},{1,3},{2,0},{3,1},{4,6},{5,7},{6,4},{7,5},{8,10},{9,11},{10,... | collective-permute-start | bytes 55304 | tf_op jit(solution)/shard_map/ppermute | solution.py:362
  7.8 4.7 %collective-permute-start.2 = (bf16[8,1152]{1,0:T(8,128)(2,1)S(1)}, bf16[8,1152]{1,0:T(8,128)(2,1)S(1)}, u32[]{:S(2)}, u32[]{:S(2)}) collective-permute-start(bf16[8,1152]{1,0:T(8,128)(2,1)S(1)} %get-tuple-element.25), channel_id=1, source_target_pairs={{0,1},{1,0},{2,3},{3,2},{4,5},{5,4},{6,7},{7,6},{8,9},{9,8},{10,11... | collective-permute-start | bytes 55304 | tf_op jit(solution)/shard_map/ppermute | solution.py:362
  12.8 5.9 %collective-permute-start.6 = (bf16[16,1152]{1,0:T(8,128)(2,1)S(1)}, bf16[16,1152]{1,0:T(8,128)(2,1)S(1)}, u32[]{:S(2)}, u32[]{:S(2)}) collective-permute-start(bf16[16,1152]{1,0:T(8,128)(2,1)S(1)} %get-tuple-element.32), channel_id=1, source_target_pairs={{0,4},{4,0},{8,12},{12,8},{1,5},{5,1},{9,13},{13,9},{2,6},{6,2},{1... | collective-permute-start | bytes 110600 | tf_op jit(solution)/shard_map/ppermute | solution.py:362
  12.9 5.8 %collective-permute-start.7 = (bf16[16,1152]{1,0:T(8,128)(2,1)S(1)}, bf16[16,1152]{1,0:T(8,128)(2,1)S(1)}, u32[]{:S(2)}, u32[]{:S(2)}) collective-permute-start(bf16[16,1152]{1,0:T(8,128)(2,1)S(1)} %get-tuple-element.33), channel_id=1, source_target_pairs={{0,8},{4,12},{8,0},{12,4},{1,9},{5,13},{9,1},{13,5},{2,10},{6,14},... | collective-permute-start | bytes 110600 | tf_op jit(solution)/shard_map/ppermute | solution.py:362
  14.5 4.2 %collective-permute-start.8 = (bf16[16,1152]{1,0:T(8,128)(2,1)S(1)}, bf16[16,1152]{1,0:T(8,128)(2,1)S(1)}, u32[]{:S(2)}, u32[]{:S(2)}) collective-permute-start(bf16[16,1152]{1,0:T(8,128)(2,1)S(1)} %get-tuple-element.34), channel_id=1, source_target_pairs={{0,12},{4,8},{8,4},{12,0},{1,13},{5,9},{9,5},{13,1},{2,14},{6,10},... | collective-permute-start | bytes 110600 | tf_op jit(solution)/shard_map/ppermute | solution.py:362
  18.6 6.9 %collective-permute-start.4 = (bf16[32,2048]{1,0:T(8,128)(2,1)S(1)}, bf16[32,2048]{1,0:T(8,128)(2,1)S(1)}, u32[]{:S(2)}, u32[]{:S(2)}) collective-permute-start(bf16[32,2048]{1,0:T(8,128)(2,1)S(1)} %get-tuple-element.30), channel_id=1, source_target_pairs={{0,1},{1,0},{2,3},{3,2},{4,5},{5,4},{6,7},{7,6},{8,9},{9,8},{10,11... | collective-permute-start | bytes 393224 | tf_op jit(solution)/shard_map/ppermute | solution.py:362
  19.0 10.4 %copy-start = (bf16[4,128,2048]{2,1,0:T(8,128)(2,1)S(1)}, bf16[4,128,2048]{2,1,0:T(8,128)(2,1)}, u32[]{:S(2)}) copy-start(bf16[4,128,2048]{2,1,0:T(8,128)(2,1)} %up_ref.1) | copy-start | bytes 6291460
  19.0 10.4 %copy-start.2 = (s32[16]{0:T(128)S(1)}, s32[16]{0:T(128)}, u32[]{:S(2)}) copy-start(s32[16]{0:T(128)} %ranks.1) | copy-start | bytes 196
  19.1 10.4 %collective-permute-start.10 = (bf16[64,128]{1,0:T(8,128)(2,1)S(1)}, bf16[64,128]{1,0:T(8,128)(2,1)S(1)}, u32[]{:S(2)}, u32[]{:S(2)}) collective-permute-start(bf16[64,128]{1,0:T(8,128)(2,1)S(1)} %get-tuple-element.35.l0), channel_id=1, source_target_pairs={{0,2},{1,3},{2,0},{3,1},{4,6},{5,7},{6,4},{7,5},{8,10},{9,11},{10,... | collective-permute-start | bytes 49160 | tf_op jit(solution)/shard_map/ppermute | solution.py:362
  21.2 8.3 %collective-permute-start.11 = (bf16[64,128]{1,0:T(8,128)(2,1)S(1)}, bf16[64,128]{1,0:T(8,128)(2,1)S(1)}, u32[]{:S(2)}, u32[]{:S(2)}) collective-permute-start(bf16[64,128]{1,0:T(8,128)(2,1)S(1)} %get-tuple-element.35.l0), channel_id=1, source_target_pairs={{0,3},{1,2},{2,1},{3,0},{4,7},{5,6},{6,5},{7,4},{8,11},{9,10},{10,... | collective-permute-start | bytes 49160 | tf_op jit(solution)/shard_map/ppermute | solution.py:362
  23.5 5.9 %collective-permute-start.9 = (bf16[64,128]{1,0:T(8,128)(2,1)S(1)}, bf16[64,128]{1,0:T(8,128)(2,1)S(1)}, u32[]{:S(2)}, u32[]{:S(2)}) collective-permute-start(bf16[64,128]{1,0:T(8,128)(2,1)S(1)} %get-tuple-element.35.l0), channel_id=1, source_target_pairs={{0,1},{1,0},{2,3},{3,2},{4,5},{5,4},{6,7},{7,6},{8,9},{9,8},{10,11... | collective-permute-start | bytes 49160 | tf_op jit(solution)/shard_map/ppermute | solution.py:362
  23.5 12.6 %collective-permute-start.3 = (bf16[32,2048]{1,0:T(8,128)(2,1)S(1)}, bf16[32,2048]{1,0:T(8,128)(2,1)S(1)}, u32[]{:S(2)}, u32[]{:S(2)}) collective-permute-start(bf16[32,2048]{1,0:T(8,128)(2,1)S(1)} %get-tuple-element.29), channel_id=1, source_target_pairs={{0,1},{1,0},{2,3},{3,2},{4,5},{5,4},{6,7},{7,6},{8,9},{9,8},{10,11... | collective-permute-start | bytes 393224 | tf_op jit(solution)/shard_map/ppermute | solution.py:362
  28.0 8.1 %collective-permute-start.5 = (bf16[32,2048]{1,0:T(8,128)(2,1)S(1)}, bf16[32,2048]{1,0:T(8,128)(2,1)S(1)}, u32[]{:S(2)}, u32[]{:S(2)}) collective-permute-start(bf16[32,2048]{1,0:T(8,128)(2,1)S(1)} %project.5), channel_id=1, source_target_pairs={{0,2},{1,3},{2,0},{3,1},{4,6},{5,7},{6,4},{7,5},{8,10},{9,11},{10,... | collective-permute-start | bytes 393224 | tf_op jit(solution)/shard_map/ppermute | solution.py:362
  30.4 4.5 %collective-permute-start.12 = (bf16[16,2048]{1,0:T(8,128)(2,1)S(1)}, bf16[16,2048]{1,0:T(8,128)(2,1)S(1)}, u32[]{:S(2)}, u32[]{:S(2)}) collective-permute-start(bf16[16,2048]{1,0:T(8,128)(2,1)S(1)} %get-tuple-element.38), channel_id=1, source_target_pairs={{0,4},{4,0},{8,12},{12,8},{1,5},{5,1},{9,13},{13,9},{2,6},{6,2},{1... | collective-permute-start | bytes 196616 | tf_op jit(solution)/shard_map/ppermute | solution.py:362
  30.5 4.5 %collective-permute-start.13 = (bf16[16,2048]{1,0:T(8,128)(2,1)S(1)}, bf16[16,2048]{1,0:T(8,128)(2,1)S(1)}, u32[]{:S(2)}, u32[]{:S(2)}) collective-permute-start(bf16[16,2048]{1,0:T(8,128)(2,1)S(1)} %get-tuple-element.39), channel_id=1, source_target_pairs={{0,8},{4,12},{8,0},{12,4},{1,9},{5,13},{9,1},{13,5},{2,10},{6,14},... | collective-permute-start | bytes 196616 | tf_op jit(solution)/shard_map/ppermute | solution.py:362
  32.1 4.0 %collective-permute-start.14 = (bf16[16,2048]{1,0:T(8,128)(2,1)S(1)}, bf16[16,2048]{1,0:T(8,128)(2,1)S(1)}, u32[]{:S(2)}, u32[]{:S(2)}) collective-permute-start(bf16[16,2048]{1,0:T(8,128)(2,1)S(1)} %get-tuple-element.40), channel_id=1, source_target_pairs={{0,12},{4,8},{8,4},{12,0},{1,13},{5,9},{9,5},{13,1},{2,14},{6,10},... | collective-permute-start | bytes 196616 | tf_op jit(solution)/shard_map/ppermute | solution.py:362

commit v5 on v4

--- a/solution.py
+++ b/solution.py
@@ -40,9 +40,10 @@
 
 
 def attend_kernel(*refs, kv):
-    length_hbm, adapter_hbm, q_hbm, fk_hbm, fv_hbm, k_hbm, v_hbm = refs[:7]
-    outs = refs[7 : 7 + kv]
-    length, adapter, q_buf, fk_buf, fv_buf, k_buf, v_buf, small, big = refs[7 + kv :]
+    length_hbm, adapter_hbm, q_hbm, fk_hbm, fv_hbm, k_hbm, v_hbm, w_hbm = refs[:8]
+    outs = refs[8 : 8 + kv]
+    far, cross = refs[8 + kv : 10 + kv]
+    length, adapter, q_buf, fk_buf, fv_buf, k_buf, v_buf, small, big, ahead = refs[10 + kv :]
     requests, _, longest, dim = k_hbm.shape
     width = q_hbm.shape[1] // kv
     group = width // dim
@@ -73,7 +74,17 @@
         copy.start()
     for r in order:
         keys_in[r].start()
+    for r in order:
         values_in[r].start()
+    half = lax.rem(lax.axis_index("batch"), 2)
+    part = w_hbm.shape[1] // (2 * kv)
+    ahead_in = []
+    for i, (r, target) in enumerate(((3, far), (2, cross))):
+        at = pl.multiple_of((jnp.bitwise_xor(me, r) * 2 + half) * part, part)
+        source = w_hbm.at[:, pl.ds(at, target.shape[1])]
+        ahead_in.append(pltpu.make_async_copy(source, target, ahead.at[i]))
+    for copy in ahead_in:
+        copy.start()
     for copy in ready:
         copy.wait()
 
@@ -128,17 +139,20 @@
         )
         pieces = [result[h * requests : (h + 1) * requests] for h in range(group)]
         outs[kv - 1 - r][...] = jnp.concatenate(pieces + [ids], axis=1).astype(BF16)
-
-
-def attend_blocks(length, adapter, query, fresh_key, fresh_value, keys, values):
+    for copy in ahead_in:
+        copy.wait()
+
+
+def attend_blocks(length, adapter, query, fresh_key, fresh_value, keys, values, weight):
     requests, kv, longest, dim = keys.shape
     width = query.shape[1] // kv
     hbm = pl.BlockSpec(memory_space=pltpu.HBM)
     return pl.pallas_call(
         functools.partial(attend_kernel, kv=kv),
-        in_specs=[hbm] * 7,
-        out_specs=[pl.BlockSpec(memory_space=pltpu.VMEM)] * kv,
-        out_shape=[sds((requests, width + LANES))] * kv,
+        in_specs=[hbm] * 8,
+        out_specs=[pl.BlockSpec(memory_space=pltpu.VMEM)] * (kv + 2),
+        out_shape=[sds((requests, width + LANES))] * kv
+        + [sds((weight.shape[0], weight.shape[1] // n)) for n in (4 * kv, 2 * kv)],
         scratch_shapes=[
             pltpu.SMEM(length.shape, jnp.int32),
             pltpu.SMEM(adapter.shape, jnp.int32),
@@ -149,14 +163,15 @@
             pltpu.VMEM((kv, requests, longest, dim), BF16),
             pltpu.SemaphoreType.DMA((5,)),
             pltpu.SemaphoreType.DMA((2, kv)),
+            pltpu.SemaphoreType.DMA((2,)),
         ],
         compiler_params=params(),
         cost_estimate=cost(2**31, 2 * keys.size * 2),
         name="attend",
-    )(*[pltpu.with_memory_space_constraint(x, pltpu.HBM) for x in (length, adapter, query, fresh_key, fresh_value, keys, values)])
-
-
-def route_kernel(x0, x1, x2, x3, rows_ref, pick_ref, c0, c1, c2, c3, held, *, local, cap):
+    )(*[pltpu.with_memory_space_constraint(x, pltpu.HBM) for x in (length, adapter, query, fresh_key, fresh_value, keys, values, weight)])
+
+
+def route_kernel(x0, x1, x2, x3, near_ref, pick_ref, c0, c2, c3, held, *, local, cap):
     me, mine = lax.axis_index("tensor"), lax.axis_index("batch")
     count = x0.shape[0]
     for r, x in zip((3, 2, 1, 0), (x0, x1, x2, x3)):
@@ -167,7 +182,7 @@
     packed = every.astype(BF16)
     rows, wide = every.shape
     width = wide - LANES
-    rows_ref[...] = packed[:, :width]
+    near_ref[:rows] = packed
     adapter = every[:, width:].astype(jnp.int32)
     lane = lax.broadcasted_iota(jnp.int32, (rows, LANES), 1)
     part, slot = lax.div(lane, cap), lax.rem(lane, cap)
@@ -185,8 +200,9 @@
     chosen = lax.dot_general(
         pick, packed, (((0,), (0,)), ((), ())), preferred_element_type=F32
     ).astype(BF16)
-    for r, c in enumerate((c0, c1, c2, c3)):
+    for r, c in ((0, c0), (2, c2), (3, c3)):
         c[...] = chosen[r * cap : (r + 1) * cap]
+    near_ref[rows:] = chosen[cap : 2 * cap]
 
 
 def route(blocks, local, cap):
@@ -196,8 +212,8 @@
     return pl.pallas_call(
         functools.partial(route_kernel, local=local, cap=cap),
         in_specs=[vmem] * 4,
-        out_specs=[vmem] * 6,
-        out_shape=[sds((rows, wide - LANES)), sds((rows, LANES))] + [sds((cap, wide))] * 4,
+        out_specs=[vmem] * 5,
+        out_shape=[sds((rows + cap, wide)), sds((rows, LANES))] + [sds((cap, wide))] * 3,
         scratch_shapes=[pltpu.VMEM((rows, wide), F32)],
         compiler_params=params(),
         cost_estimate=cost(2**20, rows * wide * 8),
@@ -205,73 +221,76 @@
     )(*blocks)
 
 
-def project_kernel(*refs, which, tile, add, after):
-    rows_ref, w_hbm = refs[:2]
-    addend = refs[2] if add else None
-    skip = 2 + add + after
-    outs = refs[skip : skip + len(which)]
-    buf, sems = refs[skip + len(which) :]
-    width = outs[0].shape[1]
-    tiles = width // tile
-    me = lax.axis_index("tensor")
-    copies = []
+def project_kernel(*refs, which, tile, leads, add, count):
+    mine_ref, other_ref, w_hbm = refs[:3]
+    refs = refs[3:]
+    addend, refs = (refs[0], refs[1:]) if add else (None, refs)
+    ready, refs = refs[0], refs[1:]
+    outs, (buf, sems) = refs[: len(which)], refs[len(which) :]
+    depth, width = w_hbm.shape[0], outs[0].shape[1]
+    me, half = lax.axis_index("tensor"), lax.rem(lax.axis_index("batch"), 2)
+    copies = {}
     for k, r in enumerate(which):
-        start = jnp.bitwise_xor(me, r) * width
-        for j in range(tiles):
-            at = pl.ds(pl.multiple_of(start + j * tile, tile), tile)
-            n = k * tiles + j
-            copies.append(pltpu.make_async_copy(w_hbm.at[:, at], buf.at[n], sems.at[n]))
-    for copy in copies:
+        start = (jnp.bitwise_xor(me, r) * 2 + half) * width
+        for low in range(leads[k], width, tile):
+            n = len(copies)
+            at = pl.ds(pl.multiple_of(start + low, tile), tile)
+            copies[k, low] = n, pltpu.make_async_copy(w_hbm.at[:, at], buf.at[n], sems.at[n])
+    for _, copy in copies.values():
         copy.start()
-    rows = rows_ref[...]
-    for k, out in enumerate(outs):
-        for j in range(tiles):
-            n = k * tiles + j
-            copies[n].wait()
-            product = jnp.dot(rows, buf[n], preferred_element_type=F32)
-            span = slice(j * tile, (j + 1) * tile)
+    rows = jnp.concatenate([mine_ref[:count, :depth], other_ref[:count, :depth]], axis=0)
+    for k in range(len(which)):
+        for low in range(0, width, tile):
+            span = slice(low, low + tile)
+            if low < leads[k]:
+                block = ready[:, span]
+            else:
+                n, copy = copies[k, low]
+                copy.wait()
+                block = buf[n]
+            product = jnp.dot(rows, block, preferred_element_type=F32)
             if add:
                 product = product + addend[:, span].astype(F32)
-            out[:, span] = product.astype(BF16)
-
-
-def project(rows, weight, width, which, addend=None, after=None, tile=512):
-    count, depth = rows.shape
-    tiles = width // tile
+            outs[k][:, span] = product.astype(BF16)
+
+
+def project(mine, other, count, weight, width, which, ready, addend=None, tile=512):
+    depth = weight.shape[0]
     parts = len(which)
+    leads = (ready.shape[1],) + (0,) * (parts - 1)
+    pieces = max(1, (parts * width - sum(leads)) // tile)
     vmem = pl.BlockSpec(memory_space=pltpu.VMEM)
-    in_specs = [vmem, pl.BlockSpec(memory_space=pltpu.HBM)]
-    operands = [rows, pltpu.with_memory_space_constraint(weight, pltpu.HBM)]
+    in_specs = [vmem, vmem, pl.BlockSpec(memory_space=pltpu.HBM)]
+    operands = [mine, other, pltpu.with_memory_space_constraint(weight, pltpu.HBM)]
     if addend is not None:
         in_specs.append(vmem)
         operands.append(addend)
-    if after is not None:
-        in_specs.append(pl.BlockSpec(memory_space=pl.ANY))
-        operands.append(after)
     return pl.pallas_call(
         functools.partial(
             project_kernel,
             which=which,
             tile=tile,
+            leads=leads,
             add=addend is not None,
-            after=after is not None,
+            count=count,
         ),
-        in_specs=in_specs,
+        in_specs=in_specs + [vmem],
         out_specs=[vmem] * parts,
-        out_shape=[sds((count, width))] * parts,
+        out_shape=[sds((2 * count, width))] * parts,
         scratch_shapes=[
-            pltpu.VMEM((parts * tiles, depth, tile), BF16),
-            pltpu.SemaphoreType.DMA((parts * tiles,)),
+            pltpu.VMEM((pieces, depth, tile), BF16),
+            pltpu.SemaphoreType.DMA((pieces,)),
         ],
         compiler_params=params(),
-        cost_estimate=cost(2 * count * depth * width * parts, depth * width * 2 * parts),
+        cost_estimate=cost(4 * count * depth * width * parts, depth * width * 2 * parts),
         name="project",
-    )(*operands)
+    )(*operands, ready)
 
 
 def down_kernel(c0, c1, c2, c3, down_ref, low_ref, slot_ref):
     local, width, rank = down_ref.shape
-    chosen = jnp.concatenate([c[...] for c in (c0, c1, c2, c3)], axis=0)
+    cap = c0.shape[0]
+    chosen = jnp.concatenate([c0[...], c1[c1.shape[0] - cap :], c2[...], c3[...]], axis=0)
     values = chosen[:, :width]
     slot = chosen[:, width:].astype(F32).astype(jnp.int32) - lax.axis_index("batch") * local
     low = jnp.zeros((chosen.shape[0], rank), F32)
@@ -336,21 +355,47 @@
     )(ranks, *shares, slot, weight)
 
 
-def finish_kernel(pick_ref, y0, y1, y2, a0, a1, a2, a3, out):
-    rows = jnp.concatenate([a[...] for a in (a0, a1, a2, a3)], axis=0)
-    pick = pick_ref[...][:, : rows.shape[0]]
-    adapted = jnp.dot(pick, rows, preferred_element_type=F32)
-    base = y0[...].astype(F32) + y1[...].astype(F32) + y2[...].astype(F32)
-    out[...] = (base + adapted).astype(BF16)
+def gather_kernel(y0, y1, y2, _, mine, theirs):
+    count = mine.shape[0]
+    total = y0[...].astype(F32) + y1[...].astype(F32) + y2[...].astype(F32)
+    mine[...] = total[:count]
+    theirs[...] = total[count:].astype(BF16)
+
+
+def gather_base(shares, after):
+    vmem = pl.BlockSpec(memory_space=pltpu.VMEM)
+    count, width = shares[0].shape
+    return pl.pallas_call(
+        gather_kernel,
+        in_specs=[vmem] * 3 + [pl.BlockSpec(memory_space=pl.ANY)],
+        out_specs=[vmem] * 2,
+        out_shape=[sds((count // 2, width), F32), sds((count // 2, width))],
+        compiler_params=params(),
+        cost_estimate=cost(2**20, shares[0].size * 12),
+        name="gather_base",
+    )(*shares, after)
+
+
+def finish_kernel(pick_ref, m0, m1, a0, a1, a2, a3, out):
+    width = m0.shape[1]
+    half = lax.rem(lax.axis_index("batch"), 2)
+    pick = pick_ref[...][:, : 4 * a0.shape[0]]
+    for k, base in enumerate((m0, m1)):
+        at = jnp.bitwise_xor(half, k) * width
+        span = pl.ds(pl.multiple_of(at, width), width)
+        rows = jnp.concatenate([a[:, span] for a in (a0, a1, a2, a3)], axis=0)
+        adapted = jnp.dot(pick, rows, preferred_element_type=F32)
+        out[:, span] = (base[...].astype(F32) + adapted).astype(BF16)
 
 
 def finish(pick, shares, adapted):
     vmem = pl.BlockSpec(memory_space=pltpu.VMEM)
+    count, width = shares[0].shape
     return pl.pallas_call(
         finish_kernel,
-        in_specs=[vmem] * 8,
+        in_specs=[vmem] * 7,
         out_specs=vmem,
-        out_shape=sds(shares[0].shape),
+        out_shape=sds((count, 2 * width)),
         compiler_params=params(),
         cost_estimate=cost(2**24, shares[0].size * 16),
         name="finish",
@@ -381,7 +426,7 @@
     width = adapter_up_weight.shape[2]
     requests = query.shape[0]
     cap = 2 * requests * tensor_count // batch_count
-    blocks = attend_blocks(
+    *blocks, w_far, w_cross = attend_blocks(
         cached_length,
         request_adapter,
         query,
@@ -389,24 +434,26 @@
         fresh_value,
         stored_keys,
         stored_values,
+        output_weight,
     )
     blocks = [across(blocks[3 - r], "tensor", r) for r in (3, 2, 1)] + [blocks[3]]
-    rows, pick, *chosen = route(blocks, local, cap)
-
-    gathered = [chosen[0]] + [across(chosen[r], "batch", r) for r in (1, 2, 3)]
-    far, near = project(rows, output_weight, width, (3, 1))
+    near_rows, pick, *chosen = route(blocks, local, cap)
+    count = requests * tensor_count
+    other = across(near_rows, "batch", 1)
+    gathered = [chosen[0], other] + [across(c, "batch", r) for c, r in zip(chosen[1:], (2, 3))]
+    both = (near_rows, other, count, output_weight, width // 2)
+    far, near, mine = project(*both, (3, 1, 0), w_far)
     far_in = across(far, "tensor", 1)
     near_in = across(near, "tensor", 1)
 
     low, slot = down(gathered, adapter_down_weight)
     shares = [low] + [across(low, "tensor", r) for r in (1, 2, 3)]
-    (cross,) = project(rows, output_weight, width, (2,), addend=far_in)
-    (mine,) = project(rows, output_weight, width, (0,))
+    (cross,) = project(*both, (2,), w_cross, addend=far_in)
     cross_in = across(cross, "tensor", 2)
-
     lifted = up(rank_per_adapter, shares, slot, adapter_up_weight, batch_count)
     lifted = [lifted[0]] + [across(lifted[r], "batch", r) for r in (1, 2, 3)]
-    return finish(pick, (mine, near_in, cross_in), lifted)
+    mine, theirs = gather_base((mine, near_in, cross_in), lifted[0])
+    return finish(pick, (mine, across(theirs, "batch", 1)), lifted)
 
 
 def attend(query, fresh_key, fresh_value, stored_keys, stored_values, cached_length):

time: 37.1 us -> 35.4 us (0.954)
  Pallas kernels: 14 us -> 8.94 us
  waiting for transfers between devices: 5.24 us -> 7.85 us
  starting transfers between devices: 17.5 us -> 18.3 us
    pallas_call x3 -> x2, Pallas kernels: 8.86 us -> 3.6 us  [project(): pl.pallas_call(functools.partial(project_kernel, which=which, tile=tile,...]
    ppermute x15 -> x16, waiting for transfers between devices: 5.24 us -> 7.85 us  [across(): return lax.ppermute(value, axis, [(i, i ^ r) for i in range(n)])]
    ppermute x15 -> x16, starting transfers between devices: 17.5 us -> 18.3 us  [across(): return lax.ppermute(value, axis, [(i, i ^ r) for i in range(n)])]
    pallas_call x1 -> x2, Pallas kernels: 0.83 us -> 0.88 us  [the longest x1 0.83 us: finish(): pl.pallas_call(finish_kernel, in_specs=[vmem] * 7, out_specs=vmem, out_sh...]
  transfers between devices with their start and end apart: 15 -> 16, of which waited for: 4 -> 5; matrix products, arithmetic and copies ran while one was open for 0% -> 0% of each run, Pallas kernels for 28% -> 14%
where the time goes in v5:
time: 35.4 us; the launch traced here: 35.3 us
  starting transfers between devices  18.3 us (52%)
  Pallas kernels  8.94 us (25%)
  waiting for transfers between devices  7.85 us (22%)
    ppermute x16, starting transfers between devices, across(): return lax.ppermute(value, axis, [(i, i ^ r) for i in range(n)])  18.3 us
    ppermute x16, waiting for transfers between devices, across(): return lax.ppermute(value, axis, [(i, i ^ r) for i in range(n)])  7.85 us
    pallas_call x2, Pallas kernels, project(): pl.pallas_call(functools.partial(project_kernel, which=which, tile=tile,...  3.6 us
    pallas_call x1, Pallas kernels, attend_blocks(): pl.pallas_call(functools.partial(attend_kernel, kv=kv), in_specs=[hbm] *...  2.75 us
    pallas_call x1, Pallas kernels, up(): pl.pallas_call(functools.partial(up_kernel, tile=tile), in_specs=[pl.Bloc...  0.98 us
    pallas_call x1, Pallas kernels, finish(): pl.pallas_call(finish_kernel, in_specs=[vmem] * 7, out_specs=vmem, out_sh...  0.83 us
  transfers between devices with their start and end apart: 16, of which 5 were waited for; matrix products, arithmetic and copies ran while one was open for 0% of the time, Pallas kernels for 14%

profile of v5, /device:TPU:0, one launch (start us, length us, event | category | flops | bytes accessed | tf_op | source)
XLA Modules:
  0.0 35.3 jit_solution(1342854180113411013)
XLA Ops:
  0.0 2.8 %attend.1 = (bf16[8,1152]{1,0:T(8,128)(2,1)S(1)}, bf16[8,1152]{1,0:T(8,128)(2,1)S(1)}, bf16[8,1152]{1,0:T(8,128)(2,1)S(1)}, bf16[8,1152]{1,0:T(8,128)(2,1)S(1)},...) custom-call(s32[8]{0:T(128)} %refs_0_.1, s32[8]{0:T(128)} %refs_1_.1, bf16[8,4096]{1,0:T(8,128)(2,1)} %refs_2_.3, ...), custom_call_target="tpu_custom_call" | custom-call | flops 2147483648 | bytes 2097152 | tf_op jit(solution)/shard_map/attend/pallas_call | solution.py:150
  2.8 5.1 %collective-permute-start = (bf16[8,1152]{1,0:T(8,128)(2,1)S(1)}, bf16[8,1152]{1,0:T(8,128)(2,1)S(1)}, u32[]{:S(2)}, u32[]{:S(2)}) collective-permute-start(bf16[8,1152]{1,0:T(8,128)(2,1)S(1)} %get-tuple-element.27), channel_id=1, source_target_pairs={{0,3},{1,2},{2,1},{3,0},{4,7},{5,6},{6,5},{7,4},{8,11},{9,10},{10,... | collective-permute-start | bytes 55304 | tf_op jit(solution)/shard_map/ppermute | solution.py:407
  7.9 0.6 %collective-permute-start.2 = (bf16[8,1152]{1,0:T(8,128)(2,1)S(1)}, bf16[8,1152]{1,0:T(8,128)(2,1)S(1)}, u32[]{:S(2)}, u32[]{:S(2)}) collective-permute-start(bf16[8,1152]{1,0:T(8,128)(2,1)S(1)} %get-tuple-element.29), channel_id=1, source_target_pairs={{0,1},{1,0},{2,3},{3,2},{4,5},{5,4},{6,7},{7,6},{8,9},{9,8},{10,11... | collective-permute-start | bytes 55304 | tf_op jit(solution)/shard_map/ppermute | solution.py:407
  8.5 1.1 %collective-permute-done.x0 = bf16[8,1152]{1,0:T(8,128)(2,1)S(1)} collective-permute-done((bf16[8,1152]{1,0:T(8,128)(2,1)S(1)}, bf16[8,1152]{1,0:T(8,128)(2,1)S(1)}, u32[]{:S(2)}, u32[]{:S(2)}) %collective-permute-start) | collective-permute-done | bytes 18464 | tf_op jit(solution)/shard_map/ppermute | solution.py:407
  9.6 2.9 %collective-permute-done.1.x1 = bf16[8,1152]{1,0:T(8,128)(2,1)S(1)} collective-permute-done((bf16[8,1152]{1,0:T(8,128)(2,1)S(1)}, bf16[8,1152]{1,0:T(8,128)(2,1)S(1)}, u32[]{:S(2)}, u32[]{:S(2)}) %collective-permute-start.1) | collective-permute-done | bytes 18464 | tf_op jit(solution)/shard_map/ppermute | solution.py:407
  12.5 0.4 %route.1 = (bf16[48,1152]{1,0:T(8,128)(2,1)S(1)}, bf16[32,128]{1,0:T(8,128)(2,1)S(1)}, bf16[16,1152]{1,0:T(8,128)(2,1)S(1)}, bf16[16,1152]{1,0:T(8,128)(2,1)S(1)}, bf16[16,1152]{1,0:T(8,128)(2,1)S(1)}) custom-call(bf16[8,1152]{1,0:T(8,128)(2,1)S(1)} %collective-permute-done.x0, bf16[8,1152]{1,0:T(8,128)(2,1)S(1)} %collective-permute-done.1.x1, ...), custom_call_target="tpu_custom_call" | custom-call | flops 1048576 | bytes 294912 | tf_op jit(solution)/shard_map/route/pallas_call | solution.py:212
  13.0 0.1 collective-permute-start.3
  13.0 1.6 %collective-permute-start.7 = (bf16[16,1152]{1,0:T(8,128)(2,1)S(1)}, bf16[16,1152]{1,0:T(8,128)(2,1)S(1)}, u32[]{:S(2)}, u32[]{:S(2)}) collective-permute-start(bf16[16,1152]{1,0:T(8,128)(2,1)S(1)} %get-tuple-element.39), channel_id=1, source_target_pairs={{0,8},{4,12},{8,0},{12,4},{1,9},{5,13},{9,1},{13,5},{2,10},{6,14},... | collective-permute-start | bytes 110600 | tf_op jit(solution)/shard_map/ppermute | solution.py:407
  14.6 0.3 collective-permute-start.8
  14.9 3.1 %project.2 = (bf16[64,1024]{1,0:T(8,128)(2,1)S(1)}, bf16[64,1024]{1,0:T(8,128)(2,1)S(1)}, bf16[64,1024]{1,0:T(8,128)(2,1)S(1)}) custom-call(bf16[48,1152]{1,0:T(8,128)(2,1)S(1)} %get-tuple-element.32.refs_0_, bf16[48,1152]{1,0:T(8,128)(2,1)S(1)} %collective-permute-done.3.refs_1_.c1, bf16[1024,8192]{1,0:T(8,128)(2,1)} %refs_2_.5, ...), custom_call_target="tpu_custom_call" | custom-call | flops 402653184 | bytes 6291456 | tf_op jit(solution)/shard_map/project/pallas_call | solution.py:268
  18.0 0.1 collective-permute-start.5
  18.1 0.3 down.1
  18.5 3.5 %collective-permute-start.11 = (bf16[64,128]{1,0:T(8,128)(2,1)S(1)}, bf16[64,128]{1,0:T(8,128)(2,1)S(1)}, u32[]{:S(2)}, u32[]{:S(2)}) collective-permute-start(bf16[64,128]{1,0:T(8,128)(2,1)S(1)} %get-tuple-element.41.l0), channel_id=1, source_target_pairs={{0,3},{1,2},{2,1},{3,0},{4,7},{5,6},{6,5},{7,4},{8,11},{9,10},{10,... | collective-permute-start | bytes 49160 | tf_op jit(solution)/shard_map/ppermute | solution.py:407
  22.0 0.9 %collective-permute-start.9 = (bf16[64,128]{1,0:T(8,128)(2,1)S(1)}, bf16[64,128]{1,0:T(8,128)(2,1)S(1)}, u32[]{:S(2)}, u32[]{:S(2)}) collective-permute-start(bf16[64,128]{1,0:T(8,128)(2,1)S(1)} %get-tuple-element.41.l0), channel_id=1, source_target_pairs={{0,1},{1,0},{2,3},{3,2},{4,5},{5,4},{6,7},{7,6},{8,9},{9,8},{10,11... | collective-permute-start | bytes 49160 | tf_op jit(solution)/shard_map/ppermute | solution.py:407
  22.9 1.1 %collective-permute-start.4 = (bf16[64,1024]{1,0:T(8,128)(2,1)S(1)}, bf16[64,1024]{1,0:T(8,128)(2,1)S(1)}, u32[]{:S(2)}, u32[]{:S(2)}) collective-permute-start(bf16[64,1024]{1,0:T(8,128)(2,1)S(1)} %get-tuple-element.35), channel_id=1, source_target_pairs={{0,1},{1,0},{2,3},{3,2},{4,5},{5,4},{6,7},{7,6},{8,9},{9,8},{10,11... | collective-permute-start | bytes 393224 | tf_op jit(solution)/shard_map/ppermute | solution.py:407
  24.0 0.5 %project.3 = bf16[64,1024]{1,0:T(8,128)(2,1)S(1)} custom-call(bf16[48,1152]{1,0:T(8,128)(2,1)S(1)} %get-tuple-element.32.refs_0_, bf16[48,1152]{1,0:T(8,128)(2,1)S(1)} %collective-permute-done.3.refs_1_.c1, bf16[1024,8192]{1,0:T(8,128)(2,1)} %refs_2_.5, bf16[64,1024]{1,0:T(8,128)(2,1)S(1)} %collective-permute-done.5.refs_3_, ...), custom_call_target="tpu_custom_call" | custom-call | flops 134217728 | bytes 2097152 | tf_op jit(solution)/shard_map/project/pallas_call | solution.py:268
  24.5 3.0 %collective-permute-start.6 = (bf16[64,1024]{1,0:T(8,128)(2,1)S(1)}, bf16[64,1024]{1,0:T(8,128)(2,1)S(1)}, u32[]{:S(2)}, u32[]{:S(2)}) collective-permute-start(bf16[64,1024]{1,0:T(8,128)(2,1)S(1)} %project.3), channel_id=1, source_target_pairs={{0,2},{1,3},{2,0},{3,1},{4,6},{5,7},{6,4},{7,5},{8,10},{9,11},{10,... | collective-permute-start | bytes 393224 | tf_op jit(solution)/shard_map/ppermute | solution.py:407
  27.5 1.0 %up.1 = (bf16[16,2048]{1,0:T(8,128)(2,1)S(1)}, bf16[16,2048]{1,0:T(8,128)(2,1)S(1)}, bf16[16,2048]{1,0:T(8,128)(2,1)S(1)}, bf16[16,2048]{1,0:T(8,128)(2,1)S(1)}) custom-call(s32[16]{0:T(128)S(1)} %copy-done.2, bf16[64,128]{1,0:T(8,128)(2,1)S(1)} %get-tuple-element.41.l0, bf16[64,128]{1,0:T(8,128)(2,1)S(1)} %collective-permute-done.9.l1, ...), custom_call_target="tpu_custom_call" | custom-call | flops 17179869184 | bytes 2097152 | tf_op jit(solution)/shard_map/up/pallas_call | solution.py:347
  28.6 1.6 %collective-permute-start.14 = (bf16[16,2048]{1,0:T(8,128)(2,1)S(1)}, bf16[16,2048]{1,0:T(8,128)(2,1)S(1)}, u32[]{:S(2)}, u32[]{:S(2)}) collective-permute-start(bf16[16,2048]{1,0:T(8,128)(2,1)S(1)} %get-tuple-element.47), channel_id=1, source_target_pairs={{0,8},{4,12},{8,0},{12,4},{1,9},{5,13},{9,1},{13,5},{2,10},{6,14},... | collective-permute-start | bytes 196616 | tf_op jit(solution)/shard_map/ppermute | solution.py:407
  30.2 0.3 collective-permute-start.15
  30.5 2.6 %collective-permute-done.6.y2 = bf16[64,1024]{1,0:T(8,128)(2,1)S(1)} collective-permute-done((bf16[64,1024]{1,0:T(8,128)(2,1)S(1)}, bf16[64,1024]{1,0:T(8,128)(2,1)S(1)}, u32[]{:S(2)}, u32[]{:S(2)}) %collective-permute-start.6) | collective-permute-done | bytes 131104 | tf_op jit(solution)/shard_map/ppermute | solution.py:407
  33.2 1.0 %collective-permute-done.15.a3 = bf16[16,2048]{1,0:T(8,128)(2,1)S(1)} collective-permute-done((bf16[16,2048]{1,0:T(8,128)(2,1)S(1)}, bf16[16,2048]{1,0:T(8,128)(2,1)S(1)}, u32[]{:S(2)}, u32[]{:S(2)}) %collective-permute-start.15) | collective-permute-done | bytes 65568 | tf_op jit(solution)/shard_map/ppermute | solution.py:407
  34.2 0.2 collective-permute-done.12.m1
  34.4 0.8 %finish.1 = bf16[32,2048]{1,0:T(8,128)(2,1)} custom-call(bf16[32,128]{1,0:T(8,128)(2,1)S(1)} %get-tuple-element.31.pick_ref, f32[32,1024]{1,0:T(8,128)S(1)} %get-tuple-element.44.m0, bf16[32,1024]{1,0:T(8,128)(2,1)S(1)} %collective-permute-done.12.m1, bf16[16,2048]{1,0:T(8,128)(2,1)S(1)} %get-tuple-element.43._.a0, ...), custom_call_target="tpu_custom_call" | custom-call | flops 16777216 | bytes 524288 | tf_op jit(solution)/shard_map/finish/pallas_call | solution.py:394
  (22 shorter events, 0.2 us)
Async XLA Ops:
  2.8 6.9 %collective-permute-start = (bf16[8,1152]{1,0:T(8,128)(2,1)S(1)}, bf16[8,1152]{1,0:T(8,128)(2,1)S(1)}, u32[]{:S(2)}, u32[]{:S(2)}) collective-permute-start(bf16[8,1152]{1,0:T(8,128)(2,1)S(1)} %get-tuple-element.27), channel_id=1, source_target_pairs={{0,3},{1,2},{2,1},{3,0},{4,7},{5,6},{6,5},{7,4},{8,11},{9,10},{10,... | collective-permute-start | bytes 55304 | tf_op jit(solution)/shard_map/ppermute | solution.py:407
  7.9 4.7 %collective-permute-start.1 = (bf16[8,1152]{1,0:T(8,128)(2,1)S(1)}, bf16[8,1152]{1,0:T(8,128)(2,1)S(1)}, u32[]{:S(2)}, u32[]{:S(2)}) collective-permute-start(bf16[8,1152]{1,0:T(8,128)(2,1)S(1)} %get-tuple-element.28), channel_id=1, source_target_pairs={{0,2},{1,3},{2,0},{3,1},{4,6},{5,7},{6,4},{7,5},{8,10},{9,11},{10,... | collective-permute-start | bytes 55304 | tf_op jit(solution)/shard_map/ppermute | solution.py:407
  7.9 4.7 %collective-permute-start.2 = (bf16[8,1152]{1,0:T(8,128)(2,1)S(1)}, bf16[8,1152]{1,0:T(8,128)(2,1)S(1)}, u32[]{:S(2)}, u32[]{:S(2)}) collective-permute-start(bf16[8,1152]{1,0:T(8,128)(2,1)S(1)} %get-tuple-element.29), channel_id=1, source_target_pairs={{0,1},{1,0},{2,3},{3,2},{4,5},{5,4},{6,7},{7,6},{8,9},{9,8},{10,11... | collective-permute-start | bytes 55304 | tf_op jit(solution)/shard_map/ppermute | solution.py:407
  13.0 1.9 %collective-permute-start.3 = (bf16[48,1152]{1,0:T(8,128)(2,1)S(1)}, bf16[48,1152]{1,0:T(8,128)(2,1)S(1)}, u32[]{:S(2)}, u32[]{:S(2)}) collective-permute-start(bf16[48,1152]{1,0:T(8,128)(2,1)S(1)} %get-tuple-element.32.refs_0_), channel_id=1, source_target_pairs={{0,4},{4,0},{8,12},{12,8},{1,5},{5,1},{9,13},{13,9},{2,6},{6,2},{1... | collective-permute-start | bytes 331784 | tf_op jit(solution)/shard_map/ppermute | solution.py:407
  13.0 5.1 %collective-permute-start.7 = (bf16[16,1152]{1,0:T(8,128)(2,1)S(1)}, bf16[16,1152]{1,0:T(8,128)(2,1)S(1)}, u32[]{:S(2)}, u32[]{:S(2)}) collective-permute-start(bf16[16,1152]{1,0:T(8,128)(2,1)S(1)} %get-tuple-element.39), channel_id=1, source_target_pairs={{0,8},{4,12},{8,0},{12,4},{1,9},{5,13},{9,1},{13,5},{2,10},{6,14},... | collective-permute-start | bytes 110600 | tf_op jit(solution)/shard_map/ppermute | solution.py:407
  14.6 3.5 %collective-permute-start.8 = (bf16[16,1152]{1,0:T(8,128)(2,1)S(1)}, bf16[16,1152]{1,0:T(8,128)(2,1)S(1)}, u32[]{:S(2)}, u32[]{:S(2)}) collective-permute-start(bf16[16,1152]{1,0:T(8,128)(2,1)S(1)} %get-tuple-element.40), channel_id=1, source_target_pairs={{0,12},{4,8},{8,4},{12,0},{1,13},{5,9},{9,5},{13,1},{2,14},{6,10},... | collective-permute-start | bytes 110600 | tf_op jit(solution)/shard_map/ppermute | solution.py:407
  14.9 3.2 %copy-start.1 = (bf16[4,1024,128]{2,1,0:T(8,128)(2,1)S(1)}, bf16[4,1024,128]{2,1,0:T(8,128)(2,1)}, u32[]{:S(2)}) copy-start(bf16[4,1024,128]{2,1,0:T(8,128)(2,1)} %down_ref.1) | copy-start | bytes 3145732
  18.0 6.0 %collective-permute-start.5 = (bf16[64,1024]{1,0:T(8,128)(2,1)S(1)}, bf16[64,1024]{1,0:T(8,128)(2,1)S(1)}, u32[]{:S(2)}, u32[]{:S(2)}) collective-permute-start(bf16[64,1024]{1,0:T(8,128)(2,1)S(1)} %get-tuple-element.36), channel_id=1, source_target_pairs={{0,1},{1,0},{2,3},{3,2},{4,5},{5,4},{6,7},{7,6},{8,9},{9,8},{10,11... | collective-permute-start | bytes 393224 | tf_op jit(solution)/shard_map/ppermute | solution.py:407
  18.5 9.0 %collective-permute-start.11 = (bf16[64,128]{1,0:T(8,128)(2,1)S(1)}, bf16[64,128]{1,0:T(8,128)(2,1)S(1)}, u32[]{:S(2)}, u32[]{:S(2)}) collective-permute-start(bf16[64,128]{1,0:T(8,128)(2,1)S(1)} %get-tuple-element.41.l0), channel_id=1, source_target_pairs={{0,3},{1,2},{2,1},{3,0},{4,7},{5,6},{6,5},{7,4},{8,11},{9,10},{10,... | collective-permute-start | bytes 49160 | tf_op jit(solution)/shard_map/ppermute | solution.py:407
  22.0 5.5 %collective-permute-start.10 = (bf16[64,128]{1,0:T(8,128)(2,1)S(1)}, bf16[64,128]{1,0:T(8,128)(2,1)S(1)}, u32[]{:S(2)}, u32[]{:S(2)}) collective-permute-start(bf16[64,128]{1,0:T(8,128)(2,1)S(1)} %get-tuple-element.41.l0), channel_id=1, source_target_pairs={{0,2},{1,3},{2,0},{3,1},{4,6},{5,7},{6,4},{7,5},{8,10},{9,11},{10,... | collective-permute-start | bytes 49160 | tf_op jit(solution)/shard_map/ppermute | solution.py:407
  22.0 5.5 %collective-permute-start.9 = (bf16[64,128]{1,0:T(8,128)(2,1)S(1)}, bf16[64,128]{1,0:T(8,128)(2,1)S(1)}, u32[]{:S(2)}, u32[]{:S(2)}) collective-permute-start(bf16[64,128]{1,0:T(8,128)(2,1)S(1)} %get-tuple-element.41.l0), channel_id=1, source_target_pairs={{0,1},{1,0},{2,3},{3,2},{4,5},{5,4},{6,7},{7,6},{8,9},{9,8},{10,11... | collective-permute-start | bytes 49160 | tf_op jit(solution)/shard_map/ppermute | solution.py:407
  22.9 7.6 %collective-permute-start.4 = (bf16[64,1024]{1,0:T(8,128)(2,1)S(1)}, bf16[64,1024]{1,0:T(8,128)(2,1)S(1)}, u32[]{:S(2)}, u32[]{:S(2)}) collective-permute-start(bf16[64,1024]{1,0:T(8,128)(2,1)S(1)} %get-tuple-element.35), channel_id=1, source_target_pairs={{0,1},{1,0},{2,3},{3,2},{4,5},{5,4},{6,7},{7,6},{8,9},{9,8},{10,11... | collective-permute-start | bytes 393224 | tf_op jit(solution)/shard_map/ppermute | solution.py:407
  24.0 3.5 %copy-start = (bf16[4,128,2048]{2,1,0:T(8,128)(2,1)S(1)}, bf16[4,128,2048]{2,1,0:T(8,128)(2,1)}, u32[]{:S(2)}) copy-start(bf16[4,128,2048]{2,1,0:T(8,128)(2,1)} %up_ref.1) | copy-start | bytes 6291460
  24.0 3.5 %copy-start.2 = (s32[16]{0:T(128)S(1)}, s32[16]{0:T(128)}, u32[]{:S(2)}) copy-start(s32[16]{0:T(128)} %ranks.1) | copy-start | bytes 196
  24.5 8.5 %collective-permute-start.6 = (bf16[64,1024]{1,0:T(8,128)(2,1)S(1)}, bf16[64,1024]{1,0:T(8,128)(2,1)S(1)}, u32[]{:S(2)}, u32[]{:S(2)}) collective-permute-start(bf16[64,1024]{1,0:T(8,128)(2,1)S(1)} %project.3), channel_id=1, source_target_pairs={{0,2},{1,3},{2,0},{3,1},{4,6},{5,7},{6,4},{7,5},{8,10},{9,11},{10,... | collective-permute-start | bytes 393224 | tf_op jit(solution)/shard_map/ppermute | solution.py:407
  28.5 4.7 %collective-permute-start.13 = (bf16[16,2048]{1,0:T(8,128)(2,1)S(1)}, bf16[16,2048]{1,0:T(8,128)(2,1)S(1)}, u32[]{:S(2)}, u32[]{:S(2)}) collective-permute-start(bf16[16,2048]{1,0:T(8,128)(2,1)S(1)} %get-tuple-element.46), channel_id=1, source_target_pairs={{0,4},{4,0},{8,12},{12,8},{1,5},{5,1},{9,13},{13,9},{2,6},{6,2},{1... | collective-permute-start | bytes 196616 | tf_op jit(solution)/shard_map/ppermute | solution.py:407
  28.6 4.6 %collective-permute-start.14 = (bf16[16,2048]{1,0:T(8,128)(2,1)S(1)}, bf16[16,2048]{1,0:T(8,128)(2,1)S(1)}, u32[]{:S(2)}, u32[]{:S(2)}) collective-permute-start(bf16[16,2048]{1,0:T(8,128)(2,1)S(1)} %get-tuple-element.47), channel_id=1, source_target_pairs={{0,8},{4,12},{8,0},{12,4},{1,9},{5,13},{9,1},{13,5},{2,10},{6,14},... | collective-permute-start | bytes 196616 | tf_op jit(solution)/shard_map/ppermute | solution.py:407
  30.2 4.0 %collective-permute-start.15 = (bf16[16,2048]{1,0:T(8,128)(2,1)S(1)}, bf16[16,2048]{1,0:T(8,128)(2,1)S(1)}, u32[]{:S(2)}, u32[]{:S(2)}) collective-permute-start(bf16[16,2048]{1,0:T(8,128)(2,1)S(1)} %get-tuple-element.48), channel_id=1, source_target_pairs={{0,12},{4,8},{8,4},{12,0},{1,13},{5,9},{9,5},{13,1},{2,14},{6,10},... | collective-permute-start | bytes 196616 | tf_op jit(solution)/shard_map/ppermute | solution.py:407
  33.1 1.3 %collective-permute-start.12 = (bf16[32,1024]{1,0:T(8,128)(2,1)S(1)}, bf16[32,1024]{1,0:T(8,128)(2,1)S(1)}, u32[]{:S(2)}, u32[]{:S(2)}) collective-permute-start(bf16[32,1024]{1,0:T(8,128)(2,1)S(1)} %get-tuple-element.45), channel_id=1, source_target_pairs={{0,4},{4,0},{8,12},{12,8},{1,5},{5,1},{9,13},{13,9},{2,6},{6,2},{1... | collective-permute-start | bytes 196616 | tf_op jit(solution)/shard_map/ppermute | solution.py:407

commit v6 on v5

--- a/solution.py
+++ b/solution.py
@@ -40,10 +40,9 @@
 
 
 def attend_kernel(*refs, kv):
-    length_hbm, adapter_hbm, q_hbm, fk_hbm, fv_hbm, k_hbm, v_hbm, w_hbm = refs[:8]
-    outs = refs[8 : 8 + kv]
-    far, cross = refs[8 + kv : 10 + kv]
-    length, adapter, q_buf, fk_buf, fv_buf, k_buf, v_buf, small, big, ahead = refs[10 + kv :]
+    length_hbm, adapter_hbm, q_hbm, fk_hbm, fv_hbm, k_hbm, v_hbm = refs[:7]
+    outs = refs[7 : 7 + kv]
+    length, adapter, q_buf, fk_buf, fv_buf, k_buf, v_buf, small, big = refs[7 + kv :]
     requests, _, longest, dim = k_hbm.shape
     width = q_hbm.shape[1] // kv
     group = width // dim
@@ -76,15 +75,6 @@
         keys_in[r].start()
     for r in order:
         values_in[r].start()
-    half = lax.rem(lax.axis_index("batch"), 2)
-    part = w_hbm.shape[1] // (2 * kv)
-    ahead_in = []
-    for i, (r, target) in enumerate(((3, far), (2, cross))):
-        at = pl.multiple_of((jnp.bitwise_xor(me, r) * 2 + half) * part, part)
-        source = w_hbm.at[:, pl.ds(at, target.shape[1])]
-        ahead_in.append(pltpu.make_async_copy(source, target, ahead.at[i]))
-    for copy in ahead_in:
-        copy.start()
     for copy in ready:
         copy.wait()
 
@@ -139,20 +129,17 @@
         )
         pieces = [result[h * requests : (h + 1) * requests] for h in range(group)]
         outs[kv - 1 - r][...] = jnp.concatenate(pieces + [ids], axis=1).astype(BF16)
-    for copy in ahead_in:
-        copy.wait()
-
-
-def attend_blocks(length, adapter, query, fresh_key, fresh_value, keys, values, weight):
+
+
+def attend_blocks(length, adapter, query, fresh_key, fresh_value, keys, values):
     requests, kv, longest, dim = keys.shape
     width = query.shape[1] // kv
     hbm = pl.BlockSpec(memory_space=pltpu.HBM)
     return pl.pallas_call(
         functools.partial(attend_kernel, kv=kv),
-        in_specs=[hbm] * 8,
-        out_specs=[pl.BlockSpec(memory_space=pltpu.VMEM)] * (kv + 2),
-        out_shape=[sds((requests, width + LANES))] * kv
-        + [sds((weight.shape[0], weight.shape[1] // n)) for n in (4 * kv, 2 * kv)],
+        in_specs=[hbm] * 7,
+        out_specs=[pl.BlockSpec(memory_space=pltpu.VMEM)] * kv,
+        out_shape=[sds((requests, width + LANES))] * kv,
         scratch_shapes=[
             pltpu.SMEM(length.shape, jnp.int32),
             pltpu.SMEM(adapter.shape, jnp.int32),
@@ -163,12 +150,11 @@
             pltpu.VMEM((kv, requests, longest, dim), BF16),
             pltpu.SemaphoreType.DMA((5,)),
             pltpu.SemaphoreType.DMA((2, kv)),
-            pltpu.SemaphoreType.DMA((2,)),
         ],
         compiler_params=params(),
-        cost_estimate=cost(2**31, 2 * keys.size * 2),
+        cost_estimate=cost(2**35, 2 * keys.size * 2),
         name="attend",
-    )(*[pltpu.with_memory_space_constraint(x, pltpu.HBM) for x in (length, adapter, query, fresh_key, fresh_value, keys, values, weight)])
+    )(*[pltpu.with_memory_space_constraint(x, pltpu.HBM) for x in (length, adapter, query, fresh_key, fresh_value, keys, values)])
 
 
 def route_kernel(x0, x1, x2, x3, near_ref, pick_ref, c0, c2, c3, held, *, local, cap):
@@ -221,70 +207,38 @@
     )(*blocks)
 
 
-def project_kernel(*refs, which, tile, leads, add, count):
-    mine_ref, other_ref, w_hbm = refs[:3]
-    refs = refs[3:]
-    addend, refs = (refs[0], refs[1:]) if add else (None, refs)
-    ready, refs = refs[0], refs[1:]
-    outs, (buf, sems) = refs[: len(which)], refs[len(which) :]
-    depth, width = w_hbm.shape[0], outs[0].shape[1]
+def project_kernel(mine_ref, other_ref, w_ref, *refs, which, tile, add, count):
+    addend, outs = (refs[0], refs[1:]) if add else (None, refs)
+    depth, width = w_ref.shape[0], outs[0].shape[1]
     me, half = lax.axis_index("tensor"), lax.rem(lax.axis_index("batch"), 2)
-    copies = {}
+    rows = jnp.concatenate([mine_ref[:count, :depth], other_ref[:count, :depth]], axis=0)
     for k, r in enumerate(which):
         start = (jnp.bitwise_xor(me, r) * 2 + half) * width
-        for low in range(leads[k], width, tile):
-            n = len(copies)
+        for low in range(0, width, tile):
             at = pl.ds(pl.multiple_of(start + low, tile), tile)
-            copies[k, low] = n, pltpu.make_async_copy(w_hbm.at[:, at], buf.at[n], sems.at[n])
-    for _, copy in copies.values():
-        copy.start()
-    rows = jnp.concatenate([mine_ref[:count, :depth], other_ref[:count, :depth]], axis=0)
-    for k in range(len(which)):
-        for low in range(0, width, tile):
+            product = jnp.dot(rows, w_ref[:, at], preferred_element_type=F32)
             span = slice(low, low + tile)
-            if low < leads[k]:
-                block = ready[:, span]
-            else:
-                n, copy = copies[k, low]
-                copy.wait()
-                block = buf[n]
-            product = jnp.dot(rows, block, preferred_element_type=F32)
             if add:
                 product = product + addend[:, span].astype(F32)
             outs[k][:, span] = product.astype(BF16)
 
 
-def project(mine, other, count, weight, width, which, ready, addend=None, tile=512):
+def project(mine, other, count, weight, width, which, addend=None, tile=512):
     depth = weight.shape[0]
     parts = len(which)
-    leads = (ready.shape[1],) + (0,) * (parts - 1)
-    pieces = max(1, (parts * width - sum(leads)) // tile)
     vmem = pl.BlockSpec(memory_space=pltpu.VMEM)
-    in_specs = [vmem, vmem, pl.BlockSpec(memory_space=pltpu.HBM)]
-    operands = [mine, other, pltpu.with_memory_space_constraint(weight, pltpu.HBM)]
-    if addend is not None:
-        in_specs.append(vmem)
-        operands.append(addend)
+    operands = [mine, other, weight] + ([] if addend is None else [addend])
     return pl.pallas_call(
         functools.partial(
-            project_kernel,
-            which=which,
-            tile=tile,
-            leads=leads,
-            add=addend is not None,
-            count=count,
+            project_kernel, which=which, tile=tile, add=addend is not None, count=count
         ),
-        in_specs=in_specs + [vmem],
+        in_specs=[vmem] * len(operands),
         out_specs=[vmem] * parts,
         out_shape=[sds((2 * count, width))] * parts,
-        scratch_shapes=[
-            pltpu.VMEM((pieces, depth, tile), BF16),
-            pltpu.SemaphoreType.DMA((pieces,)),
-        ],
         compiler_params=params(),
         cost_estimate=cost(4 * count * depth * width * parts, depth * width * 2 * parts),
         name="project",
-    )(*operands, ready)
+    )(*operands)
 
 
 def down_kernel(c0, c1, c2, c3, down_ref, low_ref, slot_ref):
@@ -426,7 +380,7 @@
     width = adapter_up_weight.shape[2]
     requests = query.shape[0]
     cap = 2 * requests * tensor_count // batch_count
-    *blocks, w_far, w_cross = attend_blocks(
+    blocks = attend_blocks(
         cached_length,
         request_adapter,
         query,
@@ -434,7 +388,6 @@
         fresh_value,
         stored_keys,
         stored_values,
-        output_weight,
     )
     blocks = [across(blocks[3 - r], "tensor", r) for r in (3, 2, 1)] + [blocks[3]]
     near_rows, pick, *chosen = route(blocks, local, cap)
@@ -442,13 +395,13 @@
     other = across(near_rows, "batch", 1)
     gathered = [chosen[0], other] + [across(c, "batch", r) for c, r in zip(chosen[1:], (2, 3))]
     both = (near_rows, other, count, output_weight, width // 2)
-    far, near, mine = project(*both, (3, 1, 0), w_far)
+    far, near, mine = project(*both, (3, 1, 0))
     far_in = across(far, "tensor", 1)
     near_in = across(near, "tensor", 1)
 
     low, slot = down(gathered, adapter_down_weight)
     shares = [low] + [across(low, "tensor", r) for r in (1, 2, 3)]
-    (cross,) = project(*both, (2,), w_cross, addend=far_in)
+    (cross,) = project(*both, (2,), addend=far_in)
     cross_in = across(cross, "tensor", 2)
     lifted = up(rank_per_adapter, shares, slot, adapter_up_weight, batch_count)
     lifted = [lifted[0]] + [across(lifted[r], "batch", r) for r in (1, 2, 3)]

time: 35.4 us -> 34 us (0.960)
  waiting for transfers between devices: 7.85 us -> 10.4 us
  Pallas kernels: 8.94 us -> 6.76 us
  starting transfers between devices: 18.3 us -> 16.5 us
    ppermute x16, waiting for transfers between devices: 7.85 us -> 10.4 us  [across(): return lax.ppermute(value, axis, [(i, i ^ r) for i in range(n)])]
    pallas_call x2, Pallas kernels: 3.6 us -> 1.69 us  [project(): pl.pallas_call(functools.partial(project_kernel, which=which, tile=tile,...]
    ppermute x16, starting transfers between devices: 18.3 us -> 16.5 us  [across(): return lax.ppermute(value, axis, [(i, i ^ r) for i in range(n)])]
  transfers between devices with their start and end apart: 16 -> 16, of which waited for: 5 -> 9; matrix products, arithmetic and copies ran while one was open for 0% -> 0% of each run, Pallas kernels for 14% -> 9%
where the time goes in v6:
time: 34 us; the launch traced here: 33.8 us
  starting transfers between devices  16.5 us (49%)
  waiting for transfers between devices  10.4 us (31%)
  Pallas kernels  6.76 us (20%)
    ppermute x16, starting transfers between devices, across(): return lax.ppermute(value, axis, [(i, i ^ r) for i in range(n)])  16.5 us
    ppermute x16, waiting for transfers between devices, across(): return lax.ppermute(value, axis, [(i, i ^ r) for i in range(n)])  10.4 us
    pallas_call x1, Pallas kernels, attend_blocks(): pl.pallas_call(functools.partial(attend_kernel, kv=kv), in_specs=[hbm] *...  2.49 us
    pallas_call x2, Pallas kernels, project(): pl.pallas_call(functools.partial(project_kernel, which=which, tile=tile,...  1.69 us
    pallas_call x1, Pallas kernels, up(): pl.pallas_call(functools.partial(up_kernel, tile=tile), in_specs=[pl.Bloc...  0.98 us
    pallas_call x1, Pallas kernels, finish(): pl.pallas_call(finish_kernel, in_specs=[vmem] * 7, out_specs=vmem, out_sh...  0.83 us
  transfers between devices with their start and end apart: 16, of which 9 were waited for; matrix products, arithmetic and copies ran while one was open for 0% of the time, Pallas kernels for 9%

profile of v6, /device:TPU:0, one launch (start us, length us, event | category | flops | bytes accessed | tf_op | source)
XLA Modules:
  0.0 33.8 jit_solution(8443687334133152861)
XLA Ops:
  0.0 2.5 %attend.1 = (bf16[8,1152]{1,0:T(8,128)(2,1)S(1)}, bf16[8,1152]{1,0:T(8,128)(2,1)S(1)}, bf16[8,1152]{1,0:T(8,128)(2,1)S(1)}, bf16[8,1152]{1,0:T(8,128)(2,1)S(1)}) custom-call(s32[8]{0:T(128)} %refs_0_.1, s32[8]{0:T(128)} %refs_1_.1, bf16[8,4096]{1,0:T(8,128)(2,1)} %refs_2_.1, bf16[8,512]{1,0:T(8,128)(2,1)} %refs_3_.1, bf16[8,512]{1,0:T(8,128)(2,1)} %refs_4_.1, ...), custom_call_target="tpu_custom_call" | custom-call | flops 34359738368 | bytes 2097152 | tf_op jit(solution)/shard_map/attend/pallas_call | solution.py:138
  2.5 5.1 %collective-permute-start = (bf16[8,1152]{1,0:T(8,128)(2,1)S(1)}, bf16[8,1152]{1,0:T(8,128)(2,1)S(1)}, u32[]{:S(2)}, u32[]{:S(2)}) collective-permute-start(bf16[8,1152]{1,0:T(8,128)(2,1)S(1)} %get-tuple-element.25), channel_id=1, source_target_pairs={{0,3},{1,2},{2,1},{3,0},{4,7},{5,6},{6,5},{7,4},{8,11},{9,10},{10,... | collective-permute-start | bytes 55304 | tf_op jit(solution)/shard_map/ppermute | solution.py:361
  7.6 0.6 %collective-permute-start.2 = (bf16[8,1152]{1,0:T(8,128)(2,1)S(1)}, bf16[8,1152]{1,0:T(8,128)(2,1)S(1)}, u32[]{:S(2)}, u32[]{:S(2)}) collective-permute-start(bf16[8,1152]{1,0:T(8,128)(2,1)S(1)} %get-tuple-element.27), channel_id=1, source_target_pairs={{0,1},{1,0},{2,3},{3,2},{4,5},{5,4},{6,7},{7,6},{8,9},{9,8},{10,11... | collective-permute-start | bytes 55304 | tf_op jit(solution)/shard_map/ppermute | solution.py:361
  8.3 1.1 %collective-permute-done.x0 = bf16[8,1152]{1,0:T(8,128)(2,1)S(1)} collective-permute-done((bf16[8,1152]{1,0:T(8,128)(2,1)S(1)}, bf16[8,1152]{1,0:T(8,128)(2,1)S(1)}, u32[]{:S(2)}, u32[]{:S(2)}) %collective-permute-start) | collective-permute-done | bytes 18464 | tf_op jit(solution)/shard_map/ppermute | solution.py:361
  9.4 2.9 %collective-permute-done.1.x1 = bf16[8,1152]{1,0:T(8,128)(2,1)S(1)} collective-permute-done((bf16[8,1152]{1,0:T(8,128)(2,1)S(1)}, bf16[8,1152]{1,0:T(8,128)(2,1)S(1)}, u32[]{:S(2)}, u32[]{:S(2)}) %collective-permute-start.1) | collective-permute-done | bytes 18464 | tf_op jit(solution)/shard_map/ppermute | solution.py:361
  12.3 0.4 %route.1 = (bf16[48,1152]{1,0:T(8,128)(2,1)S(1)}, bf16[32,128]{1,0:T(8,128)(2,1)S(1)}, bf16[16,1152]{1,0:T(8,128)(2,1)S(1)}, bf16[16,1152]{1,0:T(8,128)(2,1)S(1)}, bf16[16,1152]{1,0:T(8,128)(2,1)S(1)}) custom-call(bf16[8,1152]{1,0:T(8,128)(2,1)S(1)} %collective-permute-done.x0, bf16[8,1152]{1,0:T(8,128)(2,1)S(1)} %collective-permute-done.1.x1, ...), custom_call_target="tpu_custom_call" | custom-call | flops 1048576 | bytes 294912 | tf_op jit(solution)/shard_map/route/pallas_call | solution.py:198
  12.8 1.6 %collective-permute-start.7 = (bf16[16,1152]{1,0:T(8,128)(2,1)S(1)}, bf16[16,1152]{1,0:T(8,128)(2,1)S(1)}, u32[]{:S(2)}, u32[]{:S(2)}) collective-permute-start(bf16[16,1152]{1,0:T(8,128)(2,1)S(1)} %get-tuple-element.35), channel_id=1, source_target_pairs={{0,8},{4,12},{8,0},{12,4},{1,9},{5,13},{9,1},{13,5},{2,10},{6,14},... | collective-permute-start | bytes 110600 | tf_op jit(solution)/shard_map/ppermute | solution.py:361
  14.4 0.3 collective-permute-start.8
  14.7 1.2 %project.2 = (bf16[64,1024]{1,0:T(8,128)(2,1)S(1)}, bf16[64,1024]{1,0:T(8,128)(2,1)S(1)}, bf16[64,1024]{1,0:T(8,128)(2,1)S(1)}) custom-call(bf16[48,1152]{1,0:T(8,128)(2,1)S(1)} %get-tuple-element.30.mine_ref, bf16[48,1152]{1,0:T(8,128)(2,1)S(1)} %collective-permute-done.3.other_ref.c1, bf16[1024,8192]{1,0:T(8,128)(2,1)S(1)} %copy-done), custom_call_target="tpu_custom_call" | custom-call | flops 402653184 | bytes 6291456 | tf_op jit(solution)/shard_map/project/pallas_call | solution.py:231
  16.0 0.9 %collective-permute-done.7.c2 = bf16[16,1152]{1,0:T(8,128)(2,1)S(1)} collective-permute-done((bf16[16,1152]{1,0:T(8,128)(2,1)S(1)}, bf16[16,1152]{1,0:T(8,128)(2,1)S(1)}, u32[]{:S(2)}, u32[]{:S(2)}) %collective-permute-start.7) | collective-permute-done | bytes 36896 | tf_op jit(solution)/shard_map/ppermute | solution.py:361
  16.8 1.0 %collective-permute-done.8.c3 = bf16[16,1152]{1,0:T(8,128)(2,1)S(1)} collective-permute-done((bf16[16,1152]{1,0:T(8,128)(2,1)S(1)}, bf16[16,1152]{1,0:T(8,128)(2,1)S(1)}, u32[]{:S(2)}, u32[]{:S(2)}) %collective-permute-start.8) | collective-permute-done | bytes 36896 | tf_op jit(solution)/shard_map/ppermute | solution.py:361
  17.8 0.3 down.1
  18.1 0.2 collective-permute-start.9
  18.4 2.0 %collective-permute-start.10 = (bf16[64,128]{1,0:T(8,128)(2,1)S(1)}, bf16[64,128]{1,0:T(8,128)(2,1)S(1)}, u32[]{:S(2)}, u32[]{:S(2)}) collective-permute-start(bf16[64,128]{1,0:T(8,128)(2,1)S(1)} %get-tuple-element.37.l0), channel_id=1, source_target_pairs={{0,2},{1,3},{2,0},{3,1},{4,6},{5,7},{6,4},{7,5},{8,10},{9,11},{10,... | collective-permute-start | bytes 49160 | tf_op jit(solution)/shard_map/ppermute | solution.py:361
  20.4 2.2 %collective-permute-start.11 = (bf16[64,128]{1,0:T(8,128)(2,1)S(1)}, bf16[64,128]{1,0:T(8,128)(2,1)S(1)}, u32[]{:S(2)}, u32[]{:S(2)}) collective-permute-start(bf16[64,128]{1,0:T(8,128)(2,1)S(1)} %get-tuple-element.37.l0), channel_id=1, source_target_pairs={{0,3},{1,2},{2,1},{3,0},{4,7},{5,6},{6,5},{7,4},{8,11},{9,10},{10,... | collective-permute-start | bytes 49160 | tf_op jit(solution)/shard_map/ppermute | solution.py:361
  22.6 0.5 %project.3 = bf16[64,1024]{1,0:T(8,128)(2,1)S(1)} custom-call(bf16[48,1152]{1,0:T(8,128)(2,1)S(1)} %get-tuple-element.30.mine_ref, bf16[48,1152]{1,0:T(8,128)(2,1)S(1)} %collective-permute-done.3.other_ref.c1, bf16[1024,8192]{1,0:T(8,128)(2,1)S(1)} %copy-done, bf16[64,1024]{1,0:T(8,128)(2,1)S(1)} %collective-permute-done.5.refs_0_), custom_call_target="tpu_custom_call" | custom-call | flops 134217728 | bytes 2097152 | tf_op jit(solution)/shard_map/project/pallas_call | solution.py:231
  23.1 2.3 %collective-permute-start.6 = (bf16[64,1024]{1,0:T(8,128)(2,1)S(1)}, bf16[64,1024]{1,0:T(8,128)(2,1)S(1)}, u32[]{:S(2)}, u32[]{:S(2)}) collective-permute-start(bf16[64,1024]{1,0:T(8,128)(2,1)S(1)} %project.3), channel_id=1, source_target_pairs={{0,2},{1,3},{2,0},{3,1},{4,6},{5,7},{6,4},{7,5},{8,10},{9,11},{10,... | collective-permute-start | bytes 393224 | tf_op jit(solution)/shard_map/ppermute | solution.py:361
  25.4 0.8 %collective-permute-done.11.l3 = bf16[64,128]{1,0:T(8,128)(2,1)S(1)} collective-permute-done((bf16[64,128]{1,0:T(8,128)(2,1)S(1)}, bf16[64,128]{1,0:T(8,128)(2,1)S(1)}, u32[]{:S(2)}, u32[]{:S(2)}) %collective-permute-start.11) | collective-permute-done | bytes 16416 | tf_op jit(solution)/shard_map/ppermute | solution.py:361
  26.1 1.0 %up.1 = (bf16[16,2048]{1,0:T(8,128)(2,1)S(1)}, bf16[16,2048]{1,0:T(8,128)(2,1)S(1)}, bf16[16,2048]{1,0:T(8,128)(2,1)S(1)}, bf16[16,2048]{1,0:T(8,128)(2,1)S(1)}) custom-call(s32[16]{0:T(128)S(1)} %copy-done.3, bf16[64,128]{1,0:T(8,128)(2,1)S(1)} %get-tuple-element.37.l0, bf16[64,128]{1,0:T(8,128)(2,1)S(1)} %collective-permute-done.9.l1, ...), custom_call_target="tpu_custom_call" | custom-call | flops 17179869184 | bytes 2097152 | tf_op jit(solution)/shard_map/up/pallas_call | solution.py:301
  27.2 1.7 %collective-permute-start.14 = (bf16[16,2048]{1,0:T(8,128)(2,1)S(1)}, bf16[16,2048]{1,0:T(8,128)(2,1)S(1)}, u32[]{:S(2)}, u32[]{:S(2)}) collective-permute-start(bf16[16,2048]{1,0:T(8,128)(2,1)S(1)} %get-tuple-element.43), channel_id=1, source_target_pairs={{0,8},{4,12},{8,0},{12,4},{1,9},{5,13},{9,1},{13,5},{2,10},{6,14},... | collective-permute-start | bytes 196616 | tf_op jit(solution)/shard_map/ppermute | solution.py:361
  29.0 0.7 %collective-permute-done.4.y1 = bf16[64,1024]{1,0:T(8,128)(2,1)S(1)} collective-permute-done((bf16[64,1024]{1,0:T(8,128)(2,1)S(1)}, bf16[64,1024]{1,0:T(8,128)(2,1)S(1)}, u32[]{:S(2)}, u32[]{:S(2)}) %collective-permute-start.4) | collective-permute-done | bytes 131104 | tf_op jit(solution)/shard_map/ppermute | solution.py:361
  29.8 1.9 %collective-permute-done.6.y2 = bf16[64,1024]{1,0:T(8,128)(2,1)S(1)} collective-permute-done((bf16[64,1024]{1,0:T(8,128)(2,1)S(1)}, bf16[64,1024]{1,0:T(8,128)(2,1)S(1)}, u32[]{:S(2)}, u32[]{:S(2)}) %collective-permute-start.6) | collective-permute-done | bytes 131104 | tf_op jit(solution)/shard_map/ppermute | solution.py:361
  31.8 1.2 %collective-permute-done.15.a3 = bf16[16,2048]{1,0:T(8,128)(2,1)S(1)} collective-permute-done((bf16[16,2048]{1,0:T(8,128)(2,1)S(1)}, bf16[16,2048]{1,0:T(8,128)(2,1)S(1)}, u32[]{:S(2)}, u32[]{:S(2)}) %collective-permute-start.15) | collective-permute-done | bytes 65568 | tf_op jit(solution)/shard_map/ppermute | solution.py:361
  33.0 0.8 %finish.1 = bf16[32,2048]{1,0:T(8,128)(2,1)} custom-call(bf16[32,128]{1,0:T(8,128)(2,1)S(1)} %get-tuple-element.29.pick_ref, f32[32,1024]{1,0:T(8,128)S(1)} %get-tuple-element.40.m0, bf16[32,1024]{1,0:T(8,128)(2,1)S(1)} %collective-permute-done.12.m1, bf16[16,2048]{1,0:T(8,128)(2,1)S(1)} %get-tuple-element.39._.a0, ...), custom_call_target="tpu_custom_call" | custom-call | flops 16777216 | bytes 524288 | tf_op jit(solution)/shard_map/finish/pallas_call | solution.py:348
  (24 shorter events, 0.6 us)
Async XLA Ops:
  0.0 14.7 %copy-start = (bf16[1024,8192]{1,0:T(8,128)(2,1)S(1)}, bf16[1024,8192]{1,0:T(8,128)(2,1)}, u32[]{:S(2)}) copy-start(bf16[1024,8192]{1,0:T(8,128)(2,1)} %w_ref.3) | copy-start | bytes 50331652
  2.5 15.3 %copy-start.2 = (bf16[4,1024,128]{2,1,0:T(8,128)(2,1)S(1)}, bf16[4,1024,128]{2,1,0:T(8,128)(2,1)}, u32[]{:S(2)}) copy-start(bf16[4,1024,128]{2,1,0:T(8,128)(2,1)} %down_ref.1) | copy-start | bytes 3145732
  2.5 6.9 %collective-permute-start = (bf16[8,1152]{1,0:T(8,128)(2,1)S(1)}, bf16[8,1152]{1,0:T(8,128)(2,1)S(1)}, u32[]{:S(2)}, u32[]{:S(2)}) collective-permute-start(bf16[8,1152]{1,0:T(8,128)(2,1)S(1)} %get-tuple-element.25), channel_id=1, source_target_pairs={{0,3},{1,2},{2,1},{3,0},{4,7},{5,6},{6,5},{7,4},{8,11},{9,10},{10,... | collective-permute-start | bytes 55304 | tf_op jit(solution)/shard_map/ppermute | solution.py:361
  7.6 4.7 %collective-permute-start.1 = (bf16[8,1152]{1,0:T(8,128)(2,1)S(1)}, bf16[8,1152]{1,0:T(8,128)(2,1)S(1)}, u32[]{:S(2)}, u32[]{:S(2)}) collective-permute-start(bf16[8,1152]{1,0:T(8,128)(2,1)S(1)} %get-tuple-element.26), channel_id=1, source_target_pairs={{0,2},{1,3},{2,0},{3,1},{4,6},{5,7},{6,4},{7,5},{8,10},{9,11},{10,... | collective-permute-start | bytes 55304 | tf_op jit(solution)/shard_map/ppermute | solution.py:361
  7.6 4.7 %collective-permute-start.2 = (bf16[8,1152]{1,0:T(8,128)(2,1)S(1)}, bf16[8,1152]{1,0:T(8,128)(2,1)S(1)}, u32[]{:S(2)}, u32[]{:S(2)}) collective-permute-start(bf16[8,1152]{1,0:T(8,128)(2,1)S(1)} %get-tuple-element.27), channel_id=1, source_target_pairs={{0,1},{1,0},{2,3},{3,2},{4,5},{5,4},{6,7},{7,6},{8,9},{9,8},{10,11... | collective-permute-start | bytes 55304 | tf_op jit(solution)/shard_map/ppermute | solution.py:361
  12.7 1.9 %collective-permute-start.3 = (bf16[48,1152]{1,0:T(8,128)(2,1)S(1)}, bf16[48,1152]{1,0:T(8,128)(2,1)S(1)}, u32[]{:S(2)}, u32[]{:S(2)}) collective-permute-start(bf16[48,1152]{1,0:T(8,128)(2,1)S(1)} %get-tuple-element.30.mine_ref), channel_id=1, source_target_pairs={{0,4},{4,0},{8,12},{12,8},{1,5},{5,1},{9,13},{13,9},{2,6},{6,2},{1... | collective-permute-start | bytes 331784 | tf_op jit(solution)/shard_map/ppermute | solution.py:361
  12.8 4.0 %collective-permute-start.7 = (bf16[16,1152]{1,0:T(8,128)(2,1)S(1)}, bf16[16,1152]{1,0:T(8,128)(2,1)S(1)}, u32[]{:S(2)}, u32[]{:S(2)}) collective-permute-start(bf16[16,1152]{1,0:T(8,128)(2,1)S(1)} %get-tuple-element.35), channel_id=1, source_target_pairs={{0,8},{4,12},{8,0},{12,4},{1,9},{5,13},{9,1},{13,5},{2,10},{6,14},... | collective-permute-start | bytes 110600 | tf_op jit(solution)/shard_map/ppermute | solution.py:361
  14.4 3.4 %collective-permute-start.8 = (bf16[16,1152]{1,0:T(8,128)(2,1)S(1)}, bf16[16,1152]{1,0:T(8,128)(2,1)S(1)}, u32[]{:S(2)}, u32[]{:S(2)}) collective-permute-start(bf16[16,1152]{1,0:T(8,128)(2,1)S(1)} %get-tuple-element.36), channel_id=1, source_target_pairs={{0,12},{4,8},{8,4},{12,0},{1,13},{5,9},{9,5},{13,1},{2,14},{6,10},... | collective-permute-start | bytes 110600 | tf_op jit(solution)/shard_map/ppermute | solution.py:361
  15.9 6.7 %collective-permute-start.5 = (bf16[64,1024]{1,0:T(8,128)(2,1)S(1)}, bf16[64,1024]{1,0:T(8,128)(2,1)S(1)}, u32[]{:S(2)}, u32[]{:S(2)}) collective-permute-start(bf16[64,1024]{1,0:T(8,128)(2,1)S(1)} %get-tuple-element.33), channel_id=1, source_target_pairs={{0,1},{1,0},{2,3},{3,2},{4,5},{5,4},{6,7},{7,6},{8,9},{9,8},{10,11... | collective-permute-start | bytes 393224 | tf_op jit(solution)/shard_map/ppermute | solution.py:361
  18.1 8.0 %copy-start.1 = (bf16[4,128,2048]{2,1,0:T(8,128)(2,1)S(1)}, bf16[4,128,2048]{2,1,0:T(8,128)(2,1)}, u32[]{:S(2)}) copy-start(bf16[4,128,2048]{2,1,0:T(8,128)(2,1)} %up_ref.1) | copy-start | bytes 6291460
  18.1 8.0 %copy-start.3 = (s32[16]{0:T(128)S(1)}, s32[16]{0:T(128)}, u32[]{:S(2)}) copy-start(s32[16]{0:T(128)} %ranks.1) | copy-start | bytes 196
  18.1 7.2 %collective-permute-start.9 = (bf16[64,128]{1,0:T(8,128)(2,1)S(1)}, bf16[64,128]{1,0:T(8,128)(2,1)S(1)}, u32[]{:S(2)}, u32[]{:S(2)}) collective-permute-start(bf16[64,128]{1,0:T(8,128)(2,1)S(1)} %get-tuple-element.37.l0), channel_id=1, source_target_pairs={{0,1},{1,0},{2,3},{3,2},{4,5},{5,4},{6,7},{7,6},{8,9},{9,8},{10,11... | collective-permute-start | bytes 49160 | tf_op jit(solution)/shard_map/ppermute | solution.py:361
  18.4 7.0 %collective-permute-start.10 = (bf16[64,128]{1,0:T(8,128)(2,1)S(1)}, bf16[64,128]{1,0:T(8,128)(2,1)S(1)}, u32[]{:S(2)}, u32[]{:S(2)}) collective-permute-start(bf16[64,128]{1,0:T(8,128)(2,1)S(1)} %get-tuple-element.37.l0), channel_id=1, source_target_pairs={{0,2},{1,3},{2,0},{3,1},{4,6},{5,7},{6,4},{7,5},{8,10},{9,11},{10,... | collective-permute-start | bytes 49160 | tf_op jit(solution)/shard_map/ppermute | solution.py:361
  20.4 5.7 %collective-permute-start.11 = (bf16[64,128]{1,0:T(8,128)(2,1)S(1)}, bf16[64,128]{1,0:T(8,128)(2,1)S(1)}, u32[]{:S(2)}, u32[]{:S(2)}) collective-permute-start(bf16[64,128]{1,0:T(8,128)(2,1)S(1)} %get-tuple-element.37.l0), channel_id=1, source_target_pairs={{0,3},{1,2},{2,1},{3,0},{4,7},{5,6},{6,5},{7,4},{8,11},{9,10},{10,... | collective-permute-start | bytes 49160 | tf_op jit(solution)/shard_map/ppermute | solution.py:361
  22.6 7.2 %collective-permute-start.4 = (bf16[64,1024]{1,0:T(8,128)(2,1)S(1)}, bf16[64,1024]{1,0:T(8,128)(2,1)S(1)}, u32[]{:S(2)}, u32[]{:S(2)}) collective-permute-start(bf16[64,1024]{1,0:T(8,128)(2,1)S(1)} %get-tuple-element.32), channel_id=1, source_target_pairs={{0,1},{1,0},{2,3},{3,2},{4,5},{5,4},{6,7},{7,6},{8,9},{9,8},{10,11... | collective-permute-start | bytes 393224 | tf_op jit(solution)/shard_map/ppermute | solution.py:361
  23.1 8.6 %collective-permute-start.6 = (bf16[64,1024]{1,0:T(8,128)(2,1)S(1)}, bf16[64,1024]{1,0:T(8,128)(2,1)S(1)}, u32[]{:S(2)}, u32[]{:S(2)}) collective-permute-start(bf16[64,1024]{1,0:T(8,128)(2,1)S(1)} %project.3), channel_id=1, source_target_pairs={{0,2},{1,3},{2,0},{3,1},{4,6},{5,7},{6,4},{7,5},{8,10},{9,11},{10,... | collective-permute-start | bytes 393224 | tf_op jit(solution)/shard_map/ppermute | solution.py:361
  27.1 4.7 %collective-permute-start.13 = (bf16[16,2048]{1,0:T(8,128)(2,1)S(1)}, bf16[16,2048]{1,0:T(8,128)(2,1)S(1)}, u32[]{:S(2)}, u32[]{:S(2)}) collective-permute-start(bf16[16,2048]{1,0:T(8,128)(2,1)S(1)} %get-tuple-element.42), channel_id=1, source_target_pairs={{0,4},{4,0},{8,12},{12,8},{1,5},{5,1},{9,13},{13,9},{2,6},{6,2},{1... | collective-permute-start | bytes 196616 | tf_op jit(solution)/shard_map/ppermute | solution.py:361
  27.2 4.6 %collective-permute-start.14 = (bf16[16,2048]{1,0:T(8,128)(2,1)S(1)}, bf16[16,2048]{1,0:T(8,128)(2,1)S(1)}, u32[]{:S(2)}, u32[]{:S(2)}) collective-permute-start(bf16[16,2048]{1,0:T(8,128)(2,1)S(1)} %get-tuple-element.43), channel_id=1, source_target_pairs={{0,8},{4,12},{8,0},{12,4},{1,9},{5,13},{9,1},{13,5},{2,10},{6,14},... | collective-permute-start | bytes 196616 | tf_op jit(solution)/shard_map/ppermute | solution.py:361
  28.9 4.0 %collective-permute-start.15 = (bf16[16,2048]{1,0:T(8,128)(2,1)S(1)}, bf16[16,2048]{1,0:T(8,128)(2,1)S(1)}, u32[]{:S(2)}, u32[]{:S(2)}) collective-permute-start(bf16[16,2048]{1,0:T(8,128)(2,1)S(1)} %get-tuple-element.44), channel_id=1, source_target_pairs={{0,12},{4,8},{8,4},{12,0},{1,13},{5,9},{9,5},{13,1},{2,14},{6,10},... | collective-permute-start | bytes 196616 | tf_op jit(solution)/shard_map/ppermute | solution.py:361
  31.7 1.3 %collective-permute-start.12 = (bf16[32,1024]{1,0:T(8,128)(2,1)S(1)}, bf16[32,1024]{1,0:T(8,128)(2,1)S(1)}, u32[]{:S(2)}, u32[]{:S(2)}) collective-permute-start(bf16[32,1024]{1,0:T(8,128)(2,1)S(1)} %get-tuple-element.41), channel_id=1, source_target_pairs={{0,4},{4,0},{8,12},{12,8},{1,5},{5,1},{9,13},{13,9},{2,6},{6,2},{1... | collective-permute-start | bytes 196616 | tf_op jit(solution)/shard_map/ppermute | solution.py:361

commit v7 on v4

--- a/solution.py
+++ b/solution.py
@@ -73,6 +73,7 @@
         copy.start()
     for r in order:
         keys_in[r].start()
+    for r in order:
         values_in[r].start()
     for copy in ready:
         copy.wait()
@@ -151,7 +152,7 @@
             pltpu.SemaphoreType.DMA((2, kv)),
         ],
         compiler_params=params(),
-        cost_estimate=cost(2**31, 2 * keys.size * 2),
+        cost_estimate=cost(2**35, 2 * keys.size * 2),
         name="attend",
     )(*[pltpu.with_memory_space_constraint(x, pltpu.HBM) for x in (length, adapter, query, fresh_key, fresh_value, keys, values)])
 
@@ -205,64 +206,32 @@
     )(*blocks)
 
 
-def project_kernel(*refs, which, tile, add, after):
-    rows_ref, w_hbm = refs[:2]
-    addend = refs[2] if add else None
-    skip = 2 + add + after
-    outs = refs[skip : skip + len(which)]
-    buf, sems = refs[skip + len(which) :]
+def project_kernel(rows_ref, w_ref, *refs, which, tile, add):
+    addend, outs = (refs[0], refs[1:]) if add else (None, refs)
     width = outs[0].shape[1]
-    tiles = width // tile
     me = lax.axis_index("tensor")
-    copies = []
+    rows = rows_ref[...]
     for k, r in enumerate(which):
         start = jnp.bitwise_xor(me, r) * width
-        for j in range(tiles):
-            at = pl.ds(pl.multiple_of(start + j * tile, tile), tile)
-            n = k * tiles + j
-            copies.append(pltpu.make_async_copy(w_hbm.at[:, at], buf.at[n], sems.at[n]))
-    for copy in copies:
-        copy.start()
-    rows = rows_ref[...]
-    for k, out in enumerate(outs):
-        for j in range(tiles):
-            n = k * tiles + j
-            copies[n].wait()
-            product = jnp.dot(rows, buf[n], preferred_element_type=F32)
-            span = slice(j * tile, (j + 1) * tile)
-            if add:
+        for low in range(0, width, tile):
+            at = pl.ds(pl.multiple_of(start + low, tile), tile)
+            product = jnp.dot(rows, w_ref[:, at], preferred_element_type=F32)
+            span = slice(low, low + tile)
+            if add and k == 0:
                 product = product + addend[:, span].astype(F32)
-            out[:, span] = product.astype(BF16)
-
-
-def project(rows, weight, width, which, addend=None, after=None, tile=512):
+            outs[k][:, span] = product.astype(BF16)
+
+
+def project(rows, weight, width, which, addend=None, tile=512):
     count, depth = rows.shape
-    tiles = width // tile
     parts = len(which)
     vmem = pl.BlockSpec(memory_space=pltpu.VMEM)
-    in_specs = [vmem, pl.BlockSpec(memory_space=pltpu.HBM)]
-    operands = [rows, pltpu.with_memory_space_constraint(weight, pltpu.HBM)]
-    if addend is not None:
-        in_specs.append(vmem)
-        operands.append(addend)
-    if after is not None:
-        in_specs.append(pl.BlockSpec(memory_space=pl.ANY))
-        operands.append(after)
-    return pl.pallas_call(
-        functools.partial(
-            project_kernel,
-            which=which,
-            tile=tile,
-            add=addend is not None,
-            after=after is not None,
-        ),
-        in_specs=in_specs,
+    operands = [rows, weight] + ([] if addend is None else [addend])
+    return pl.pallas_call(
+        functools.partial(project_kernel, which=which, tile=tile, add=addend is not None),
+        in_specs=[vmem] * len(operands),
         out_specs=[vmem] * parts,
         out_shape=[sds((count, width))] * parts,
-        scratch_shapes=[
-            pltpu.VMEM((parts * tiles, depth, tile), BF16),
-            pltpu.SemaphoreType.DMA((parts * tiles,)),
-        ],
         compiler_params=params(),
         cost_estimate=cost(2 * count * depth * width * parts, depth * width * 2 * parts),
         name="project",
@@ -316,7 +285,7 @@
         for a in range(1, local):
             total = total + jnp.dot(kept[a], up_ref[a, :, span], preferred_element_type=F32)
         adapted = total.astype(BF16)
-        for r, out in enumerate(outs):
+        for r, out in zip((2, 3, 1, 0), outs):
             out[:, span] = adapted[r * cap : (r + 1) * cap]
 
 
@@ -336,7 +305,7 @@
     )(ranks, *shares, slot, weight)
 
 
-def finish_kernel(pick_ref, y0, y1, y2, a0, a1, a2, a3, out):
+def finish_kernel(pick_ref, y0, y1, y2, a2, a3, a1, a0, out):
     rows = jnp.concatenate([a[...] for a in (a0, a1, a2, a3)], axis=0)
     pick = pick_ref[...][:, : rows.shape[0]]
     adapted = jnp.dot(pick, rows, preferred_element_type=F32)
@@ -405,7 +374,7 @@
     cross_in = across(cross, "tensor", 2)
 
     lifted = up(rank_per_adapter, shares, slot, adapter_up_weight, batch_count)
-    lifted = [lifted[0]] + [across(lifted[r], "batch", r) for r in (1, 2, 3)]
+    lifted = [across(a, "batch", r) for a, r in zip(lifted, (2, 3, 1))] + [lifted[3]]
     return finish(pick, (mine, near_in, cross_in), lifted)
 
 

time: 37.1 us -> 33.2 us (0.89)
  Pallas kernels: 14 us -> 8.19 us
  waiting for transfers between devices: 5.24 us -> 8.3 us
  starting transfers between devices: 17.5 us -> 16.4 us
    pallas_call x3, Pallas kernels: 8.86 us -> 3.18 us  [project(): pl.pallas_call(functools.partial(project_kernel, which=which, tile=tile,...]
    ppermute x15, waiting for transfers between devices: 5.24 us -> 8.3 us  [across(): return lax.ppermute(value, axis, [(i, i ^ r) for i in range(n)])]
    ppermute x15, starting transfers between devices: 17.5 us -> 16.4 us  [across(): return lax.ppermute(value, axis, [(i, i ^ r) for i in range(n)])]
  transfers between devices with their start and end apart: 15 -> 15, of which waited for: 4 -> 7; matrix products, arithmetic and copies ran while one was open for 0% -> 0% of each run, Pallas kernels for 28% -> 13%
where the time goes in v7:
time: 33.2 us; the launch traced here: 33 us
  starting transfers between devices  16.4 us (49%)
  waiting for transfers between devices  8.3 us (25%)
  Pallas kernels  8.19 us (25%)
    ppermute x15, starting transfers between devices, across(): return lax.ppermute(value, axis, [(i, i ^ r) for i in range(n)])  16.4 us
    ppermute x15, waiting for transfers between devices, across(): return lax.ppermute(value, axis, [(i, i ^ r) for i in range(n)])  8.3 us
    pallas_call x3, Pallas kernels, project(): pl.pallas_call(functools.partial(project_kernel, which=which, tile=tile,...  3.18 us
    pallas_call x1, Pallas kernels, attend_blocks(): pl.pallas_call(functools.partial(attend_kernel, kv=kv), in_specs=[hbm] *...  2.49 us
    pallas_call x1, Pallas kernels, up(): pl.pallas_call(functools.partial(up_kernel, tile=tile), in_specs=[pl.Bloc...  0.98 us
    pallas_call x1, Pallas kernels, finish(): pl.pallas_call(finish_kernel, in_specs=[vmem] * 8, out_specs=vmem, out_sh...  0.83 us
  transfers between devices with their start and end apart: 15, of which 7 were waited for; matrix products, arithmetic and copies ran while one was open for 0% of the time, Pallas kernels for 13%

profile of v7, /device:TPU:0, one launch (start us, length us, event | category | flops | bytes accessed | tf_op | source)
XLA Modules:
  0.0 33.0 jit_solution(2242082445647187114)
XLA Ops:
  0.0 2.5 %attend.1 = (bf16[8,1152]{1,0:T(8,128)(2,1)S(1)}, bf16[8,1152]{1,0:T(8,128)(2,1)S(1)}, bf16[8,1152]{1,0:T(8,128)(2,1)S(1)}, bf16[8,1152]{1,0:T(8,128)(2,1)S(1)}) custom-call(s32[8]{0:T(128)} %refs_0_.1, s32[8]{0:T(128)} %refs_1_.1, bf16[8,4096]{1,0:T(8,128)(2,1)} %refs_2_.1, bf16[8,512]{1,0:T(8,128)(2,1)} %refs_3_.1, bf16[8,512]{1,0:T(8,128)(2,1)} %refs_4_.1, ...), custom_call_target="tpu_custom_call" | custom-call | flops 34359738368 | bytes 2097152 | tf_op jit(solution)/shard_map/attend/pallas_call | solution.py:138
  2.5 5.1 %collective-permute-start = (bf16[8,1152]{1,0:T(8,128)(2,1)S(1)}, bf16[8,1152]{1,0:T(8,128)(2,1)S(1)}, u32[]{:S(2)}, u32[]{:S(2)}) collective-permute-start(bf16[8,1152]{1,0:T(8,128)(2,1)S(1)} %get-tuple-element.23), channel_id=1, source_target_pairs={{0,3},{1,2},{2,1},{3,0},{4,7},{5,6},{6,5},{7,4},{8,11},{9,10},{10,... | collective-permute-start | bytes 55304 | tf_op jit(solution)/shard_map/ppermute | solution.py:331
  7.6 0.6 %collective-permute-start.2 = (bf16[8,1152]{1,0:T(8,128)(2,1)S(1)}, bf16[8,1152]{1,0:T(8,128)(2,1)S(1)}, u32[]{:S(2)}, u32[]{:S(2)}) collective-permute-start(bf16[8,1152]{1,0:T(8,128)(2,1)S(1)} %get-tuple-element.25), channel_id=1, source_target_pairs={{0,1},{1,0},{2,3},{3,2},{4,5},{5,4},{6,7},{7,6},{8,9},{9,8},{10,11... | collective-permute-start | bytes 55304 | tf_op jit(solution)/shard_map/ppermute | solution.py:331
  8.3 1.1 %collective-permute-done.x0 = bf16[8,1152]{1,0:T(8,128)(2,1)S(1)} collective-permute-done((bf16[8,1152]{1,0:T(8,128)(2,1)S(1)}, bf16[8,1152]{1,0:T(8,128)(2,1)S(1)}, u32[]{:S(2)}, u32[]{:S(2)}) %collective-permute-start) | collective-permute-done | bytes 18464 | tf_op jit(solution)/shard_map/ppermute | solution.py:331
  9.4 2.9 %collective-permute-done.1.x1 = bf16[8,1152]{1,0:T(8,128)(2,1)S(1)} collective-permute-done((bf16[8,1152]{1,0:T(8,128)(2,1)S(1)}, bf16[8,1152]{1,0:T(8,128)(2,1)S(1)}, u32[]{:S(2)}, u32[]{:S(2)}) %collective-permute-start.1) | collective-permute-done | bytes 18464 | tf_op jit(solution)/shard_map/ppermute | solution.py:331
  12.3 0.4 %route.1 = (bf16[32,1024]{1,0:T(8,128)(2,1)S(1)}, bf16[32,128]{1,0:T(8,128)(2,1)S(1)}, bf16[16,1152]{1,0:T(8,128)(2,1)S(1)}, bf16[16,1152]{1,0:T(8,128)(2,1)S(1)...) custom-call(bf16[8,1152]{1,0:T(8,128)(2,1)S(1)} %collective-permute-done.x0, ...), custom_call_target="tpu_custom_call" | custom-call | flops 1048576 | bytes 294912 | tf_op jit(solution)/shard_map/route/pallas_call | solution.py:197
  12.8 1.6 %collective-permute-start.7 = (bf16[16,1152]{1,0:T(8,128)(2,1)S(1)}, bf16[16,1152]{1,0:T(8,128)(2,1)S(1)}, u32[]{:S(2)}, u32[]{:S(2)}) collective-permute-start(bf16[16,1152]{1,0:T(8,128)(2,1)S(1)} %get-tuple-element.33), channel_id=1, source_target_pairs={{0,8},{4,12},{8,0},{12,4},{1,9},{5,13},{9,1},{13,5},{2,10},{6,14},... | collective-permute-start | bytes 110600 | tf_op jit(solution)/shard_map/ppermute | solution.py:331
  14.7 1.5 %project.4 = (bf16[32,2048]{1,0:T(8,128)(2,1)S(1)}, bf16[32,2048]{1,0:T(8,128)(2,1)S(1)}) custom-call(bf16[32,1024]{1,0:T(8,128)(2,1)S(1)} %get-tuple-element.28.rows_ref, bf16[1024,8192]{1,0:T(8,128)(2,1)S(1)} %copy-done), custom_call_target="tpu_custom_call" | custom-call | flops 268435456 | bytes 8388608 | tf_op jit(solution)/shard_map/project/pallas_call | solution.py:230
  16.2 0.6 %collective-permute-done.7.c2 = bf16[16,1152]{1,0:T(8,128)(2,1)S(1)} collective-permute-done((bf16[16,1152]{1,0:T(8,128)(2,1)S(1)}, bf16[16,1152]{1,0:T(8,128)(2,1)S(1)}, u32[]{:S(2)}, u32[]{:S(2)}) %collective-permute-start.7) | collective-permute-done | bytes 36896 | tf_op jit(solution)/shard_map/ppermute | solution.py:331
  16.8 1.0 %collective-permute-done.8.c3 = bf16[16,1152]{1,0:T(8,128)(2,1)S(1)} collective-permute-done((bf16[16,1152]{1,0:T(8,128)(2,1)S(1)}, bf16[16,1152]{1,0:T(8,128)(2,1)S(1)}, u32[]{:S(2)}, u32[]{:S(2)}) %collective-permute-start.8) | collective-permute-done | bytes 36896 | tf_op jit(solution)/shard_map/ppermute | solution.py:331
  18.1 2.1 %collective-permute-start.10 = (bf16[64,128]{1,0:T(8,128)(2,1)S(1)}, bf16[64,128]{1,0:T(8,128)(2,1)S(1)}, u32[]{:S(2)}, u32[]{:S(2)}) collective-permute-start(bf16[64,128]{1,0:T(8,128)(2,1)S(1)} %get-tuple-element.35.l0), channel_id=1, source_target_pairs={{0,2},{1,3},{2,0},{3,1},{4,6},{5,7},{6,4},{7,5},{8,10},{9,11},{10,... | collective-permute-start | bytes 49160 | tf_op jit(solution)/shard_map/ppermute | solution.py:331
  20.2 0.8 %collective-permute-start.11 = (bf16[64,128]{1,0:T(8,128)(2,1)S(1)}, bf16[64,128]{1,0:T(8,128)(2,1)S(1)}, u32[]{:S(2)}, u32[]{:S(2)}) collective-permute-start(bf16[64,128]{1,0:T(8,128)(2,1)S(1)} %get-tuple-element.35.l0), channel_id=1, source_target_pairs={{0,3},{1,2},{2,1},{3,0},{4,7},{5,6},{6,5},{7,4},{8,11},{9,10},{10,... | collective-permute-start | bytes 49160 | tf_op jit(solution)/shard_map/ppermute | solution.py:331
  21.0 0.7 %collective-permute-start.9 = (bf16[64,128]{1,0:T(8,128)(2,1)S(1)}, bf16[64,128]{1,0:T(8,128)(2,1)S(1)}, u32[]{:S(2)}, u32[]{:S(2)}) collective-permute-start(bf16[64,128]{1,0:T(8,128)(2,1)S(1)} %get-tuple-element.35.l0), channel_id=1, source_target_pairs={{0,1},{1,0},{2,3},{3,2},{4,5},{5,4},{6,7},{7,6},{8,9},{9,8},{10,11... | collective-permute-start | bytes 49160 | tf_op jit(solution)/shard_map/ppermute | solution.py:331
  21.7 1.4 %collective-permute-start.3 = (bf16[32,2048]{1,0:T(8,128)(2,1)S(1)}, bf16[32,2048]{1,0:T(8,128)(2,1)S(1)}, u32[]{:S(2)}, u32[]{:S(2)}) collective-permute-start(bf16[32,2048]{1,0:T(8,128)(2,1)S(1)} %get-tuple-element.29), channel_id=1, source_target_pairs={{0,1},{1,0},{2,3},{3,2},{4,5},{5,4},{6,7},{7,6},{8,9},{9,8},{10,11... | collective-permute-start | bytes 393224 | tf_op jit(solution)/shard_map/ppermute | solution.py:331
  23.0 0.8 %project.5 = bf16[32,2048]{1,0:T(8,128)(2,1)S(1)} custom-call(bf16[32,1024]{1,0:T(8,128)(2,1)S(1)} %get-tuple-element.28.rows_ref, bf16[1024,8192]{1,0:T(8,128)(2,1)S(1)} %copy-done, bf16[32,2048]{1,0:T(8,128)(2,1)S(1)} %collective-permute-done.4.refs_0_), custom_call_target="tpu_custom_call" | custom-call | flops 134217728 | bytes 4194304 | tf_op jit(solution)/shard_map/project/pallas_call | solution.py:230
  23.9 1.6 %collective-permute-start.5 = (bf16[32,2048]{1,0:T(8,128)(2,1)S(1)}, bf16[32,2048]{1,0:T(8,128)(2,1)S(1)}, u32[]{:S(2)}, u32[]{:S(2)}) collective-permute-start(bf16[32,2048]{1,0:T(8,128)(2,1)S(1)} %project.5), channel_id=1, source_target_pairs={{0,2},{1,3},{2,0},{3,1},{4,6},{5,7},{6,4},{7,5},{8,10},{9,11},{10,... | collective-permute-start | bytes 393224 | tf_op jit(solution)/shard_map/ppermute | solution.py:331
  25.5 0.4 %collective-permute-done.11.l3 = bf16[64,128]{1,0:T(8,128)(2,1)S(1)} collective-permute-done((bf16[64,128]{1,0:T(8,128)(2,1)S(1)}, bf16[64,128]{1,0:T(8,128)(2,1)S(1)}, u32[]{:S(2)}, u32[]{:S(2)}) %collective-permute-start.11) | collective-permute-done | bytes 16416 | tf_op jit(solution)/shard_map/ppermute | solution.py:331
  25.9 1.0 %up.1 = (bf16[16,2048]{1,0:T(8,128)(2,1)S(1)}, bf16[16,2048]{1,0:T(8,128)(2,1)S(1)}, bf16[16,2048]{1,0:T(8,128)(2,1)S(1)}, bf16[16,2048]{1,0:T(8,128)(2,1)S(1)}) custom-call(s32[16]{0:T(128)S(1)} %copy-done.3, bf16[64,128]{1,0:T(8,128)(2,1)S(1)} %get-tuple-element.35.l0, bf16[64,128]{1,0:T(8,128)(2,1)S(1)} %collective-permute-done.9.l1, ...), custom_call_target="tpu_custom_call" | custom-call | flops 17179869184 | bytes 2097152 | tf_op jit(solution)/shard_map/up/pallas_call | solution.py:297
  26.9 0.9 %collective-permute-start.12 = (bf16[16,2048]{1,0:T(8,128)(2,1)S(1)}, bf16[16,2048]{1,0:T(8,128)(2,1)S(1)}, u32[]{:S(2)}, u32[]{:S(2)}) collective-permute-start(bf16[16,2048]{1,0:T(8,128)(2,1)S(1)} %get-tuple-element.37), channel_id=1, source_target_pairs={{0,8},{4,12},{8,0},{12,4},{1,9},{5,13},{9,1},{13,5},{2,10},{6,14},... | collective-permute-start | bytes 196616 | tf_op jit(solution)/shard_map/ppermute | solution.py:331
  27.8 1.3 %collective-permute-start.14 = (bf16[16,2048]{1,0:T(8,128)(2,1)S(1)}, bf16[16,2048]{1,0:T(8,128)(2,1)S(1)}, u32[]{:S(2)}, u32[]{:S(2)}) collective-permute-start(bf16[16,2048]{1,0:T(8,128)(2,1)S(1)} %get-tuple-element.39), channel_id=1, source_target_pairs={{0,4},{4,0},{8,12},{12,8},{1,5},{5,1},{9,13},{13,9},{2,6},{6,2},{1... | collective-permute-start | bytes 196616 | tf_op jit(solution)/shard_map/ppermute | solution.py:331
  29.1 0.8 %project.3.y0 = bf16[32,2048]{1,0:T(8,128)(2,1)S(1)} custom-call(bf16[32,1024]{1,0:T(8,128)(2,1)S(1)} %get-tuple-element.28.rows_ref, bf16[1024,8192]{1,0:T(8,128)(2,1)S(1)} %copy-done), custom_call_target="tpu_custom_call" | custom-call | flops 134217728 | bytes 4194304 | tf_op jit(solution)/shard_map/project/pallas_call | solution.py:230
  29.9 1.7 %collective-permute-done.12.a2 = bf16[16,2048]{1,0:T(8,128)(2,1)S(1)} collective-permute-done((bf16[16,2048]{1,0:T(8,128)(2,1)S(1)}, bf16[16,2048]{1,0:T(8,128)(2,1)S(1)}, u32[]{:S(2)}, u32[]{:S(2)}) %collective-permute-start.12) | collective-permute-done | bytes 65568 | tf_op jit(solution)/shard_map/ppermute | solution.py:331
  31.6 0.6 %collective-permute-done.13.a3 = bf16[16,2048]{1,0:T(8,128)(2,1)S(1)} collective-permute-done((bf16[16,2048]{1,0:T(8,128)(2,1)S(1)}, bf16[16,2048]{1,0:T(8,128)(2,1)S(1)}, u32[]{:S(2)}, u32[]{:S(2)}) %collective-permute-start.13) | collective-permute-done | bytes 65568 | tf_op jit(solution)/shard_map/ppermute | solution.py:331
  32.2 0.8 %finish.1 = bf16[32,2048]{1,0:T(8,128)(2,1)} custom-call(bf16[32,128]{1,0:T(8,128)(2,1)S(1)} %get-tuple-element.27.pick_ref, bf16[32,2048]{1,0:T(8,128)(2,1)S(1)} %project.3.y0, bf16[32,2048]{1,0:T(8,128)(2,1)S(1)} %collective-permute-done.3.y1, bf16[32,2048]{1,0:T(8,128)(2,1)S(1)} %collective-permute-done.5.y2, ...), custom_call_target="tpu_custom_call" | custom-call | flops 16777216 | bytes 1048576 | tf_op jit(solution)/shard_map/finish/pallas_call | solution.py:318
  (22 shorter events, 0.7 us)
Async XLA Ops:
  0.0 14.7 %copy-start = (bf16[1024,8192]{1,0:T(8,128)(2,1)S(1)}, bf16[1024,8192]{1,0:T(8,128)(2,1)}, u32[]{:S(2)}) copy-start(bf16[1024,8192]{1,0:T(8,128)(2,1)} %w_ref.5) | copy-start | bytes 50331652
  2.5 15.3 %copy-start.2 = (bf16[4,1024,128]{2,1,0:T(8,128)(2,1)S(1)}, bf16[4,1024,128]{2,1,0:T(8,128)(2,1)}, u32[]{:S(2)}) copy-start(bf16[4,1024,128]{2,1,0:T(8,128)(2,1)} %down_ref.1) | copy-start | bytes 3145732
  2.5 6.9 %collective-permute-start = (bf16[8,1152]{1,0:T(8,128)(2,1)S(1)}, bf16[8,1152]{1,0:T(8,128)(2,1)S(1)}, u32[]{:S(2)}, u32[]{:S(2)}) collective-permute-start(bf16[8,1152]{1,0:T(8,128)(2,1)S(1)} %get-tuple-element.23), channel_id=1, source_target_pairs={{0,3},{1,2},{2,1},{3,0},{4,7},{5,6},{6,5},{7,4},{8,11},{9,10},{10,... | collective-permute-start | bytes 55304 | tf_op jit(solution)/shard_map/ppermute | solution.py:331
  7.6 4.7 %collective-permute-start.1 = (bf16[8,1152]{1,0:T(8,128)(2,1)S(1)}, bf16[8,1152]{1,0:T(8,128)(2,1)S(1)}, u32[]{:S(2)}, u32[]{:S(2)}) collective-permute-start(bf16[8,1152]{1,0:T(8,128)(2,1)S(1)} %get-tuple-element.24), channel_id=1, source_target_pairs={{0,2},{1,3},{2,0},{3,1},{4,6},{5,7},{6,4},{7,5},{8,10},{9,11},{10,... | collective-permute-start | bytes 55304 | tf_op jit(solution)/shard_map/ppermute | solution.py:331
  7.6 4.7 %collective-permute-start.2 = (bf16[8,1152]{1,0:T(8,128)(2,1)S(1)}, bf16[8,1152]{1,0:T(8,128)(2,1)S(1)}, u32[]{:S(2)}, u32[]{:S(2)}) collective-permute-start(bf16[8,1152]{1,0:T(8,128)(2,1)S(1)} %get-tuple-element.25), channel_id=1, source_target_pairs={{0,1},{1,0},{2,3},{3,2},{4,5},{5,4},{6,7},{7,6},{8,9},{9,8},{10,11... | collective-permute-start | bytes 55304 | tf_op jit(solution)/shard_map/ppermute | solution.py:331
  12.7 3.5 %collective-permute-start.6 = (bf16[16,1152]{1,0:T(8,128)(2,1)S(1)}, bf16[16,1152]{1,0:T(8,128)(2,1)S(1)}, u32[]{:S(2)}, u32[]{:S(2)}) collective-permute-start(bf16[16,1152]{1,0:T(8,128)(2,1)S(1)} %get-tuple-element.32), channel_id=1, source_target_pairs={{0,4},{4,0},{8,12},{12,8},{1,5},{5,1},{9,13},{13,9},{2,6},{6,2},{1... | collective-permute-start | bytes 110600 | tf_op jit(solution)/shard_map/ppermute | solution.py:331
  12.8 4.0 %collective-permute-start.7 = (bf16[16,1152]{1,0:T(8,128)(2,1)S(1)}, bf16[16,1152]{1,0:T(8,128)(2,1)S(1)}, u32[]{:S(2)}, u32[]{:S(2)}) collective-permute-start(bf16[16,1152]{1,0:T(8,128)(2,1)S(1)} %get-tuple-element.33), channel_id=1, source_target_pairs={{0,8},{4,12},{8,0},{12,4},{1,9},{5,13},{9,1},{13,5},{2,10},{6,14},... | collective-permute-start | bytes 110600 | tf_op jit(solution)/shard_map/ppermute | solution.py:331
  14.4 3.4 %collective-permute-start.8 = (bf16[16,1152]{1,0:T(8,128)(2,1)S(1)}, bf16[16,1152]{1,0:T(8,128)(2,1)S(1)}, u32[]{:S(2)}, u32[]{:S(2)}) collective-permute-start(bf16[16,1152]{1,0:T(8,128)(2,1)S(1)} %get-tuple-element.34), channel_id=1, source_target_pairs={{0,12},{4,8},{8,4},{12,0},{1,13},{5,9},{9,5},{13,1},{2,14},{6,10},... | collective-permute-start | bytes 110600 | tf_op jit(solution)/shard_map/ppermute | solution.py:331
  16.2 6.9 %collective-permute-start.4 = (bf16[32,2048]{1,0:T(8,128)(2,1)S(1)}, bf16[32,2048]{1,0:T(8,128)(2,1)S(1)}, u32[]{:S(2)}, u32[]{:S(2)}) collective-permute-start(bf16[32,2048]{1,0:T(8,128)(2,1)S(1)} %get-tuple-element.30), channel_id=1, source_target_pairs={{0,1},{1,0},{2,3},{3,2},{4,5},{5,4},{6,7},{7,6},{8,9},{9,8},{10,11... | collective-permute-start | bytes 393224 | tf_op jit(solution)/shard_map/ppermute | solution.py:331
  18.1 7.8 %copy-start.1 = (bf16[4,128,2048]{2,1,0:T(8,128)(2,1)S(1)}, bf16[4,128,2048]{2,1,0:T(8,128)(2,1)}, u32[]{:S(2)}) copy-start(bf16[4,128,2048]{2,1,0:T(8,128)(2,1)} %up_ref.1) | copy-start | bytes 6291460
  18.1 7.8 %copy-start.3 = (s32[16]{0:T(128)S(1)}, s32[16]{0:T(128)}, u32[]{:S(2)}) copy-start(s32[16]{0:T(128)} %ranks.1) | copy-start | bytes 196
  18.1 7.4 %collective-permute-start.10 = (bf16[64,128]{1,0:T(8,128)(2,1)S(1)}, bf16[64,128]{1,0:T(8,128)(2,1)S(1)}, u32[]{:S(2)}, u32[]{:S(2)}) collective-permute-start(bf16[64,128]{1,0:T(8,128)(2,1)S(1)} %get-tuple-element.35.l0), channel_id=1, source_target_pairs={{0,2},{1,3},{2,0},{3,1},{4,6},{5,7},{6,4},{7,5},{8,10},{9,11},{10,... | collective-permute-start | bytes 49160 | tf_op jit(solution)/shard_map/ppermute | solution.py:331
  20.2 5.6 %collective-permute-start.11 = (bf16[64,128]{1,0:T(8,128)(2,1)S(1)}, bf16[64,128]{1,0:T(8,128)(2,1)S(1)}, u32[]{:S(2)}, u32[]{:S(2)}) collective-permute-start(bf16[64,128]{1,0:T(8,128)(2,1)S(1)} %get-tuple-element.35.l0), channel_id=1, source_target_pairs={{0,3},{1,2},{2,1},{3,0},{4,7},{5,6},{6,5},{7,4},{8,11},{9,10},{10,... | collective-permute-start | bytes 49160 | tf_op jit(solution)/shard_map/ppermute | solution.py:331
  21.0 4.8 %collective-permute-start.9 = (bf16[64,128]{1,0:T(8,128)(2,1)S(1)}, bf16[64,128]{1,0:T(8,128)(2,1)S(1)}, u32[]{:S(2)}, u32[]{:S(2)}) collective-permute-start(bf16[64,128]{1,0:T(8,128)(2,1)S(1)} %get-tuple-element.35.l0), channel_id=1, source_target_pairs={{0,1},{1,0},{2,3},{3,2},{4,5},{5,4},{6,7},{7,6},{8,9},{9,8},{10,11... | collective-permute-start | bytes 49160 | tf_op jit(solution)/shard_map/ppermute | solution.py:331
  21.7 10.5 %collective-permute-start.3 = (bf16[32,2048]{1,0:T(8,128)(2,1)S(1)}, bf16[32,2048]{1,0:T(8,128)(2,1)S(1)}, u32[]{:S(2)}, u32[]{:S(2)}) collective-permute-start(bf16[32,2048]{1,0:T(8,128)(2,1)S(1)} %get-tuple-element.29), channel_id=1, source_target_pairs={{0,1},{1,0},{2,3},{3,2},{4,5},{5,4},{6,7},{7,6},{8,9},{9,8},{10,11... | collective-permute-start | bytes 393224 | tf_op jit(solution)/shard_map/ppermute | solution.py:331
  23.9 8.3 %collective-permute-start.5 = (bf16[32,2048]{1,0:T(8,128)(2,1)S(1)}, bf16[32,2048]{1,0:T(8,128)(2,1)S(1)}, u32[]{:S(2)}, u32[]{:S(2)}) collective-permute-start(bf16[32,2048]{1,0:T(8,128)(2,1)S(1)} %project.5), channel_id=1, source_target_pairs={{0,2},{1,3},{2,0},{3,1},{4,6},{5,7},{6,4},{7,5},{8,10},{9,11},{10,... | collective-permute-start | bytes 393224 | tf_op jit(solution)/shard_map/ppermute | solution.py:331
  26.9 4.7 %collective-permute-start.12 = (bf16[16,2048]{1,0:T(8,128)(2,1)S(1)}, bf16[16,2048]{1,0:T(8,128)(2,1)S(1)}, u32[]{:S(2)}, u32[]{:S(2)}) collective-permute-start(bf16[16,2048]{1,0:T(8,128)(2,1)S(1)} %get-tuple-element.37), channel_id=1, source_target_pairs={{0,8},{4,12},{8,0},{12,4},{1,9},{5,13},{9,1},{13,5},{2,10},{6,14},... | collective-permute-start | bytes 196616 | tf_op jit(solution)/shard_map/ppermute | solution.py:331
  27.8 4.4 %collective-permute-start.13 = (bf16[16,2048]{1,0:T(8,128)(2,1)S(1)}, bf16[16,2048]{1,0:T(8,128)(2,1)S(1)}, u32[]{:S(2)}, u32[]{:S(2)}) collective-permute-start(bf16[16,2048]{1,0:T(8,128)(2,1)S(1)} %get-tuple-element.38), channel_id=1, source_target_pairs={{0,12},{4,8},{8,4},{12,0},{1,13},{5,9},{9,5},{13,1},{2,14},{6,10},... | collective-permute-start | bytes 196616 | tf_op jit(solution)/shard_map/ppermute | solution.py:331
  27.8 4.4 %collective-permute-start.14 = (bf16[16,2048]{1,0:T(8,128)(2,1)S(1)}, bf16[16,2048]{1,0:T(8,128)(2,1)S(1)}, u32[]{:S(2)}, u32[]{:S(2)}) collective-permute-start(bf16[16,2048]{1,0:T(8,128)(2,1)S(1)} %get-tuple-element.39), channel_id=1, source_target_pairs={{0,4},{4,0},{8,12},{12,8},{1,5},{5,1},{9,13},{13,9},{2,6},{6,2},{1... | collective-permute-start | bytes 196616 | tf_op jit(solution)/shard_map/ppermute | solution.py:331

commit v8 on v7

--- a/solution.py
+++ b/solution.py
@@ -31,18 +31,19 @@
     return jax.ShapeDtypeStruct(shape, dtype)
 
 
-def column_of(ref, count):
+def column_of(values):
+    count = len(values)
     rows = lax.broadcasted_iota(jnp.int32, (count, LANES), 0)
-    out = jnp.full((count, LANES), ref[0], jnp.int32)
+    out = jnp.full((count, LANES), values[0], jnp.int32)
     for i in range(1, count):
-        out = jnp.where(rows == i, ref[i], out)
+        out = jnp.where(rows == i, values[i], out)
     return out
 
 
 def attend_kernel(*refs, kv):
-    length_hbm, adapter_hbm, q_hbm, fk_hbm, fv_hbm, k_hbm, v_hbm = refs[:7]
-    outs = refs[7 : 7 + kv]
-    length, adapter, q_buf, fk_buf, fv_buf, k_buf, v_buf, small, big = refs[7 + kv :]
+    length_hbm, adapter_hbm, ranks_hbm, q_hbm, fk_hbm, fv_hbm, k_hbm, v_hbm = refs[:8]
+    outs = refs[8 : 8 + kv]
+    length, adapter, ranks, q_buf, fk_buf, fv_buf, k_buf, v_buf, small, big = refs[8 + kv :]
     requests, _, longest, dim = k_hbm.shape
     width = q_hbm.shape[1] // kv
     group = width // dim
@@ -60,28 +61,29 @@
                 (fv_hbm, fv_buf),
                 (length_hbm, length),
                 (adapter_hbm, adapter),
+                (ranks_hbm, ranks),
             )
         )
     ]
-    keys_in = {}
-    values_in = {}
-    for r in order:
-        head = jnp.bitwise_xor(me, r)
-        keys_in[r] = pltpu.make_async_copy(k_hbm.at[:, head], k_buf.at[r], big.at[0, r])
-        values_in[r] = pltpu.make_async_copy(v_hbm.at[:, head], v_buf.at[r], big.at[1, r])
+    keys_in = pltpu.make_async_copy(k_hbm, k_buf, big.at[0])
+    values_in = pltpu.make_async_copy(v_hbm, v_buf, big.at[1])
     for copy in ready:
         copy.start()
-    for r in order:
-        keys_in[r].start()
-    for r in order:
-        values_in[r].start()
+    keys_in.start()
+    values_in.start()
     for copy in ready:
         copy.wait()
 
     request = lax.rem(lax.broadcasted_iota(jnp.int32, (rows, longest), 0), requests)
-    lengths = jnp.concatenate([column_of(length, requests)] * group, axis=0)
+    lengths = jnp.concatenate(
+        [column_of([length[i] for i in range(requests)])] * group, axis=0
+    )
     valid = lax.broadcasted_iota(jnp.int32, (rows, longest), 1) < lengths
-    ids = column_of(adapter, requests).astype(F32)
+    named = [adapter[i] for i in range(requests)]
+    lane = lax.broadcasted_iota(jnp.int32, (requests, LANES), 1)
+    ids = jnp.where(
+        lane < LANES // 2, column_of(named), column_of([ranks[a] for a in named])
+    ).astype(F32)
     scores, own, fresh_value = {}, {}, {}
     for r in order:
         head = jnp.bitwise_xor(me, r)
@@ -92,12 +94,11 @@
         fresh_value[r] = jnp.concatenate([fv_buf[:, mine].astype(F32)] * group, axis=0)
         own[r] = jnp.sum(queries * fresh_key, axis=1, keepdims=True) * scaling
         scores[r] = queries.astype(BF16)
-    for r in order:
-        keys_in[r].wait()
+    keys_in.wait()
     for r in order:
         every = lax.dot_general(
             scores[r],
-            k_buf[r].reshape(requests * longest, dim),
+            k_buf[:, jnp.bitwise_xor(me, r)].reshape(requests * longest, dim),
             (((1,), (1,)), ((), ())),
             preferred_element_type=F32,
         )
@@ -117,13 +118,12 @@
         spread[r] = jnp.concatenate(
             [jnp.where(request == i, weights, 0.0) for i in range(requests)], axis=1
         ).astype(BF16)
-    for r in order:
-        values_in[r].wait()
+    values_in.wait()
     for r in order:
         own_weight = (own_exp[r] * inverse[r]).astype(BF16).astype(F32)
         result = (
             jnp.dot(
-                spread[r], v_buf[r].reshape(requests * longest, dim), preferred_element_type=F32
+                spread[r], v_buf[:, jnp.bitwise_xor(me, r)].reshape(requests * longest, dim), preferred_element_type=F32
             )
             + own_weight * fresh_value[r]
         )
@@ -131,30 +131,31 @@
         outs[kv - 1 - r][...] = jnp.concatenate(pieces + [ids], axis=1).astype(BF16)
 
 
-def attend_blocks(length, adapter, query, fresh_key, fresh_value, keys, values):
+def attend_blocks(length, adapter, ranks, query, fresh_key, fresh_value, keys, values):
     requests, kv, longest, dim = keys.shape
     width = query.shape[1] // kv
     hbm = pl.BlockSpec(memory_space=pltpu.HBM)
     return pl.pallas_call(
         functools.partial(attend_kernel, kv=kv),
-        in_specs=[hbm] * 7,
+        in_specs=[hbm] * 8,
         out_specs=[pl.BlockSpec(memory_space=pltpu.VMEM)] * kv,
         out_shape=[sds((requests, width + LANES))] * kv,
         scratch_shapes=[
             pltpu.SMEM(length.shape, jnp.int32),
             pltpu.SMEM(adapter.shape, jnp.int32),
+            pltpu.SMEM(ranks.shape, jnp.int32),
             pltpu.VMEM(query.shape, BF16),
             pltpu.VMEM(fresh_key.shape, BF16),
             pltpu.VMEM(fresh_value.shape, BF16),
-            pltpu.VMEM((kv, requests, longest, dim), BF16),
-            pltpu.VMEM((kv, requests, longest, dim), BF16),
-            pltpu.SemaphoreType.DMA((5,)),
-            pltpu.SemaphoreType.DMA((2, kv)),
+            pltpu.VMEM(keys.shape, BF16),
+            pltpu.VMEM(values.shape, BF16),
+            pltpu.SemaphoreType.DMA((6,)),
+            pltpu.SemaphoreType.DMA((2,)),
         ],
         compiler_params=params(),
         cost_estimate=cost(2**35, 2 * keys.size * 2),
         name="attend",
-    )(*[pltpu.with_memory_space_constraint(x, pltpu.HBM) for x in (length, adapter, query, fresh_key, fresh_value, keys, values)])
+    )(*[pltpu.with_memory_space_constraint(x, pltpu.HBM) for x in (length, adapter, ranks, query, fresh_key, fresh_value, keys, values)])
 
 
 def route_kernel(x0, x1, x2, x3, rows_ref, pick_ref, c0, c1, c2, c3, held, *, local, cap):
@@ -238,11 +239,17 @@
     )(*operands)
 
 
-def down_kernel(c0, c1, c2, c3, down_ref, low_ref, slot_ref):
+def down_kernel(c0, c1, c2, c3, down_ref, low_ref, slot_ref, factor_ref):
     local, width, rank = down_ref.shape
     chosen = jnp.concatenate([c[...] for c in (c0, c1, c2, c3)], axis=0)
     values = chosen[:, :width]
-    slot = chosen[:, width:].astype(F32).astype(jnp.int32) - lax.axis_index("batch") * local
+    tail = chosen[:, width:].astype(F32)
+    half = tail.shape[1] // 2
+    slot = jnp.concatenate([tail[:, :half]] * 2, axis=1).astype(jnp.int32)
+    slot = slot - lax.axis_index("batch") * local
+    ranks = jnp.concatenate([tail[:, half:]] * 2, axis=1)
+    lane = lax.broadcasted_iota(jnp.int32, slot.shape, 1).astype(F32)
+    factor_ref[...] = jnp.where(lane < ranks, ADAPTER_SCALE / jnp.maximum(ranks, 1.0), 0.0)
     low = jnp.zeros((chosen.shape[0], rank), F32)
     for a in range(local):
         product = jnp.dot(values, down_ref[a], preferred_element_type=F32)
@@ -258,51 +265,47 @@
     return pl.pallas_call(
         down_kernel,
         in_specs=[vmem] * 5,
-        out_specs=[vmem] * 2,
-        out_shape=[sds((rows, rank)), sds((rows, rank), jnp.int32)],
+        out_specs=[vmem] * 3,
+        out_shape=[sds((rows, rank)), sds((rows, rank), jnp.int32), sds((rows, rank), F32)],
         compiler_params=params(),
         cost_estimate=cost(2**34, weight.size * 2),
         name="down",
     )(*chosen, weight)
 
 
-def up_kernel(ranks, l0, l1, l2, l3, slot_ref, up_ref, *outs, tile):
-    local, _, width = up_ref.shape
+def up_kernel(l0, l1, l2, l3, slot_ref, factor_ref, up_ref, *outs, tile):
+    local, depth, width = up_ref.shape
     low = l0[...].astype(F32)
     for share in (l1, l2, l3):
         low = low + share[...].astype(F32)
+    low = low * factor_ref[...]
     slot = slot_ref[...]
-    lane = lax.broadcasted_iota(jnp.int32, low.shape, 1)
-    kept = []
-    for a in range(local):
-        rank = ranks[lax.axis_index("batch") * local + a]
-        factor = ADAPTER_SCALE / jnp.full(low.shape, rank, jnp.int32).astype(F32)
-        kept.append(jnp.where((slot == a) & (lane < rank), low * factor, 0.0).astype(BF16))
+    kept = jnp.concatenate(
+        [jnp.where(slot == a, low, 0.0).astype(BF16) for a in range(local)], axis=1
+    )
     cap = outs[0].shape[0]
     for start in range(0, width, tile):
         span = slice(start, start + tile)
-        total = jnp.dot(kept[0], up_ref[0, :, span], preferred_element_type=F32)
-        for a in range(1, local):
-            total = total + jnp.dot(kept[a], up_ref[a, :, span], preferred_element_type=F32)
-        adapted = total.astype(BF16)
+        block = up_ref[:, :, span].reshape(local * depth, tile)
+        adapted = jnp.dot(kept, block, preferred_element_type=F32).astype(BF16)
         for r, out in zip((2, 3, 1, 0), outs):
             out[:, span] = adapted[r * cap : (r + 1) * cap]
 
 
-def up(ranks, shares, slot, weight, parts, tile=512):
+def up(shares, slot, factor, weight, parts, tile=512):
     local, rank, width = weight.shape
     rows = slot.shape[0]
     cap = rows // parts
     vmem = pl.BlockSpec(memory_space=pltpu.VMEM)
     return pl.pallas_call(
         functools.partial(up_kernel, tile=tile),
-        in_specs=[pl.BlockSpec(memory_space=pltpu.SMEM)] + [vmem] * 6,
+        in_specs=[vmem] * 7,
         out_specs=[vmem] * parts,
         out_shape=[sds((cap, width))] * parts,
         compiler_params=params(),
         cost_estimate=cost(2**34, weight.size * 2),
         name="up",
-    )(ranks, *shares, slot, weight)
+    )(*shares, slot, factor, weight)
 
 
 def finish_kernel(pick_ref, y0, y1, y2, a2, a3, a1, a0, out):
@@ -353,6 +356,7 @@
     blocks = attend_blocks(
         cached_length,
         request_adapter,
+        rank_per_adapter,
         query,
         fresh_key,
         fresh_value,
@@ -367,13 +371,13 @@
     far_in = across(far, "tensor", 1)
     near_in = across(near, "tensor", 1)
 
-    low, slot = down(gathered, adapter_down_weight)
+    low, slot, factor = down(gathered, adapter_down_weight)
     shares = [low] + [across(low, "tensor", r) for r in (1, 2, 3)]
     (cross,) = project(rows, output_weight, width, (2,), addend=far_in)
     (mine,) = project(rows, output_weight, width, (0,))
     cross_in = across(cross, "tensor", 2)
 
-    lifted = up(rank_per_adapter, shares, slot, adapter_up_weight, batch_count)
+    lifted = up(shares, slot, factor, adapter_up_weight, batch_count)
     lifted = [across(a, "batch", r) for a, r in zip(lifted, (2, 3, 1))] + [lifted[3]]
     return finish(pick, (mine, near_in, cross_in), lifted)
 

time: 33.2 us -> 32.9 us (level)
  Pallas kernels: 8.19 us -> 7.67 us
    pallas_call x2, Pallas kernels: 1.28 us -> 0.79 us  [the longest x1 0.48 us: up(): pl.pallas_call(functools.partial(up_kernel, tile=tile), in_specs=[vmem] *...]
  transfers between devices with their start and end apart: 15 -> 15, of which waited for: 7 -> 8; matrix products, arithmetic and copies ran while one was open for 0% -> 0% of each run, Pallas kernels for 13% -> 12%
where the time goes in v8:
time: 32.9 us; the launch traced here: 32.8 us
  starting transfers between devices  16.4 us (50%)
  waiting for transfers between devices  8.59 us (26%)
  Pallas kernels  7.67 us (23%)
    ppermute x15, starting transfers between devices, across(): return lax.ppermute(value, axis, [(i, i ^ r) for i in range(n)])  16.4 us
    ppermute x15, waiting for transfers between devices, across(): return lax.ppermute(value, axis, [(i, i ^ r) for i in range(n)])  8.59 us
    pallas_call x3, Pallas kernels, project(): pl.pallas_call(functools.partial(project_kernel, which=which, tile=tile,...  3.17 us
    pallas_call x1, Pallas kernels, attend_blocks(): pl.pallas_call(functools.partial(attend_kernel, kv=kv), in_specs=[hbm] *...  2.47 us
    pallas_call x1, Pallas kernels, finish(): pl.pallas_call(finish_kernel, in_specs=[vmem] * 8, out_specs=vmem, out_sh...  0.83 us
  transfers between devices with their start and end apart: 15, of which 8 were waited for; matrix products, arithmetic and copies ran while one was open for 0% of the time, Pallas kernels for 12%

profile of v8, /device:TPU:0, one launch (start us, length us, event | category | flops | bytes accessed | tf_op | source)
XLA Modules:
  0.0 32.8 jit_solution(12394805850270230992)
XLA Ops:
  0.0 2.5 %attend.1 = (bf16[8,1152]{1,0:T(8,128)(2,1)S(1)}, bf16[8,1152]{1,0:T(8,128)(2,1)S(1)}, bf16[8,1152]{1,0:T(8,128)(2,1)S(1)}, bf16[8,1152]{1,0:T(8,128)(2,1)S(1)}) custom-call(s32[8]{0:T(128)} %refs_0_.1, s32[8]{0:T(128)} %refs_1_.1, s32[16]{0:T(128)} %refs_2_.1, bf16[8,4096]{1,0:T(8,128)(2,1)} %refs_3_.1, bf16[8,512]{1,0:T(8,128)(2,1)} %refs_4_.1, ...), custom_call_target="tpu_custom_call" | custom-call | flops 34359738368 | bytes 2097152 | tf_op jit(solution)/shard_map/attend/pallas_call | solution.py:138
  2.5 5.1 %collective-permute-start = (bf16[8,1152]{1,0:T(8,128)(2,1)S(1)}, bf16[8,1152]{1,0:T(8,128)(2,1)S(1)}, u32[]{:S(2)}, u32[]{:S(2)}) collective-permute-start(bf16[8,1152]{1,0:T(8,128)(2,1)S(1)} %get-tuple-element.24), channel_id=1, source_target_pairs={{0,3},{1,2},{2,1},{3,0},{4,7},{5,6},{6,5},{7,4},{8,11},{9,10},{10,... | collective-permute-start | bytes 55304 | tf_op jit(solution)/shard_map/ppermute | solution.py:334
  7.6 0.6 %collective-permute-start.2 = (bf16[8,1152]{1,0:T(8,128)(2,1)S(1)}, bf16[8,1152]{1,0:T(8,128)(2,1)S(1)}, u32[]{:S(2)}, u32[]{:S(2)}) collective-permute-start(bf16[8,1152]{1,0:T(8,128)(2,1)S(1)} %get-tuple-element.26), channel_id=1, source_target_pairs={{0,1},{1,0},{2,3},{3,2},{4,5},{5,4},{6,7},{7,6},{8,9},{9,8},{10,11... | collective-permute-start | bytes 55304 | tf_op jit(solution)/shard_map/ppermute | solution.py:334
  8.2 1.1 %collective-permute-done.x0 = bf16[8,1152]{1,0:T(8,128)(2,1)S(1)} collective-permute-done((bf16[8,1152]{1,0:T(8,128)(2,1)S(1)}, bf16[8,1152]{1,0:T(8,128)(2,1)S(1)}, u32[]{:S(2)}, u32[]{:S(2)}) %collective-permute-start) | collective-permute-done | bytes 18464 | tf_op jit(solution)/shard_map/ppermute | solution.py:334
  9.3 2.9 %collective-permute-done.1.x1 = bf16[8,1152]{1,0:T(8,128)(2,1)S(1)} collective-permute-done((bf16[8,1152]{1,0:T(8,128)(2,1)S(1)}, bf16[8,1152]{1,0:T(8,128)(2,1)S(1)}, u32[]{:S(2)}, u32[]{:S(2)}) %collective-permute-start.1) | collective-permute-done | bytes 18464 | tf_op jit(solution)/shard_map/ppermute | solution.py:334
  12.3 0.4 %route.1 = (bf16[32,1024]{1,0:T(8,128)(2,1)S(1)}, bf16[32,128]{1,0:T(8,128)(2,1)S(1)}, bf16[16,1152]{1,0:T(8,128)(2,1)S(1)}, bf16[16,1152]{1,0:T(8,128)(2,1)S(1)...) custom-call(bf16[8,1152]{1,0:T(8,128)(2,1)S(1)} %collective-permute-done.x0, ...), custom_call_target="tpu_custom_call" | custom-call | flops 1048576 | bytes 294912 | tf_op jit(solution)/shard_map/route/pallas_call | solution.py:198
  12.8 1.6 %collective-permute-start.7 = (bf16[16,1152]{1,0:T(8,128)(2,1)S(1)}, bf16[16,1152]{1,0:T(8,128)(2,1)S(1)}, u32[]{:S(2)}, u32[]{:S(2)}) collective-permute-start(bf16[16,1152]{1,0:T(8,128)(2,1)S(1)} %get-tuple-element.34), channel_id=1, source_target_pairs={{0,8},{4,12},{8,0},{12,4},{1,9},{5,13},{9,1},{13,5},{2,10},{6,14},... | collective-permute-start | bytes 110600 | tf_op jit(solution)/shard_map/ppermute | solution.py:334
  14.6 1.5 %project.4 = (bf16[32,2048]{1,0:T(8,128)(2,1)S(1)}, bf16[32,2048]{1,0:T(8,128)(2,1)S(1)}) custom-call(bf16[32,1024]{1,0:T(8,128)(2,1)S(1)} %get-tuple-element.29.rows_ref, bf16[1024,8192]{1,0:T(8,128)(2,1)S(1)} %copy-done), custom_call_target="tpu_custom_call" | custom-call | flops 268435456 | bytes 8388608 | tf_op jit(solution)/shard_map/project/pallas_call | solution.py:231
  16.2 0.6 %collective-permute-done.7.c2 = bf16[16,1152]{1,0:T(8,128)(2,1)S(1)} collective-permute-done((bf16[16,1152]{1,0:T(8,128)(2,1)S(1)}, bf16[16,1152]{1,0:T(8,128)(2,1)S(1)}, u32[]{:S(2)}, u32[]{:S(2)}) %collective-permute-start.7) | collective-permute-done | bytes 36896 | tf_op jit(solution)/shard_map/ppermute | solution.py:334
  16.8 1.0 %collective-permute-done.8.c3 = bf16[16,1152]{1,0:T(8,128)(2,1)S(1)} collective-permute-done((bf16[16,1152]{1,0:T(8,128)(2,1)S(1)}, bf16[16,1152]{1,0:T(8,128)(2,1)S(1)}, u32[]{:S(2)}, u32[]{:S(2)}) %collective-permute-start.8) | collective-permute-done | bytes 36896 | tf_op jit(solution)/shard_map/ppermute | solution.py:334
  18.1 2.1 %collective-permute-start.10 = (bf16[64,128]{1,0:T(8,128)(2,1)S(1)}, bf16[64,128]{1,0:T(8,128)(2,1)S(1)}, u32[]{:S(2)}, u32[]{:S(2)}) collective-permute-start(bf16[64,128]{1,0:T(8,128)(2,1)S(1)} %get-tuple-element.36.l0), channel_id=1, source_target_pairs={{0,2},{1,3},{2,0},{3,1},{4,6},{5,7},{6,4},{7,5},{8,10},{9,11},{10,... | collective-permute-start | bytes 49160 | tf_op jit(solution)/shard_map/ppermute | solution.py:334
  20.2 0.8 %collective-permute-start.11 = (bf16[64,128]{1,0:T(8,128)(2,1)S(1)}, bf16[64,128]{1,0:T(8,128)(2,1)S(1)}, u32[]{:S(2)}, u32[]{:S(2)}) collective-permute-start(bf16[64,128]{1,0:T(8,128)(2,1)S(1)} %get-tuple-element.36.l0), channel_id=1, source_target_pairs={{0,3},{1,2},{2,1},{3,0},{4,7},{5,6},{6,5},{7,4},{8,11},{9,10},{10,... | collective-permute-start | bytes 49160 | tf_op jit(solution)/shard_map/ppermute | solution.py:334
  21.0 0.7 %collective-permute-start.9 = (bf16[64,128]{1,0:T(8,128)(2,1)S(1)}, bf16[64,128]{1,0:T(8,128)(2,1)S(1)}, u32[]{:S(2)}, u32[]{:S(2)}) collective-permute-start(bf16[64,128]{1,0:T(8,128)(2,1)S(1)} %get-tuple-element.36.l0), channel_id=1, source_target_pairs={{0,1},{1,0},{2,3},{3,2},{4,5},{5,4},{6,7},{7,6},{8,9},{9,8},{10,11... | collective-permute-start | bytes 49160 | tf_op jit(solution)/shard_map/ppermute | solution.py:334
  21.6 1.4 %collective-permute-start.3 = (bf16[32,2048]{1,0:T(8,128)(2,1)S(1)}, bf16[32,2048]{1,0:T(8,128)(2,1)S(1)}, u32[]{:S(2)}, u32[]{:S(2)}) collective-permute-start(bf16[32,2048]{1,0:T(8,128)(2,1)S(1)} %get-tuple-element.30), channel_id=1, source_target_pairs={{0,1},{1,0},{2,3},{3,2},{4,5},{5,4},{6,7},{7,6},{8,9},{9,8},{10,11... | collective-permute-start | bytes 393224 | tf_op jit(solution)/shard_map/ppermute | solution.py:334
  23.0 0.8 %project.5 = bf16[32,2048]{1,0:T(8,128)(2,1)S(1)} custom-call(bf16[32,1024]{1,0:T(8,128)(2,1)S(1)} %get-tuple-element.29.rows_ref, bf16[1024,8192]{1,0:T(8,128)(2,1)S(1)} %copy-done, bf16[32,2048]{1,0:T(8,128)(2,1)S(1)} %collective-permute-done.4.refs_0_), custom_call_target="tpu_custom_call" | custom-call | flops 134217728 | bytes 4194304 | tf_op jit(solution)/shard_map/project/pallas_call | solution.py:231
  23.8 1.6 %collective-permute-start.5 = (bf16[32,2048]{1,0:T(8,128)(2,1)S(1)}, bf16[32,2048]{1,0:T(8,128)(2,1)S(1)}, u32[]{:S(2)}, u32[]{:S(2)}) collective-permute-start(bf16[32,2048]{1,0:T(8,128)(2,1)S(1)} %project.5), channel_id=1, source_target_pairs={{0,2},{1,3},{2,0},{3,1},{4,6},{5,7},{6,4},{7,5},{8,10},{9,11},{10,... | collective-permute-start | bytes 393224 | tf_op jit(solution)/shard_map/ppermute | solution.py:334
  25.4 0.4 %collective-permute-done.11.l3 = bf16[64,128]{1,0:T(8,128)(2,1)S(1)} collective-permute-done((bf16[64,128]{1,0:T(8,128)(2,1)S(1)}, bf16[64,128]{1,0:T(8,128)(2,1)S(1)}, u32[]{:S(2)}, u32[]{:S(2)}) %collective-permute-start.11) | collective-permute-done | bytes 16416 | tf_op jit(solution)/shard_map/ppermute | solution.py:334
  25.8 0.5 %up.1 = (bf16[16,2048]{1,0:T(8,128)(2,1)S(1)}, bf16[16,2048]{1,0:T(8,128)(2,1)S(1)}, bf16[16,2048]{1,0:T(8,128)(2,1)S(1)}, bf16[16,2048]{1,0:T(8,128)(2,1)S(1)}) custom-call(bf16[64,128]{1,0:T(8,128)(2,1)S(1)} %get-tuple-element.36.l0, bf16[64,128]{1,0:T(8,128)(2,1)S(1)} %collective-permute-done.9.l1, bf16[64,128]{1,0:T(8,128)(2,1)S(1)} %collective-permute-done.10.l2, ...), custom_call_target="tpu_custom_call" | custom-call | flops 17179869184 | bytes 2097152 | tf_op jit(solution)/shard_map/up/pallas_call | solution.py:300
  26.3 1.0 %collective-permute-start.12 = (bf16[16,2048]{1,0:T(8,128)(2,1)S(1)}, bf16[16,2048]{1,0:T(8,128)(2,1)S(1)}, u32[]{:S(2)}, u32[]{:S(2)}) collective-permute-start(bf16[16,2048]{1,0:T(8,128)(2,1)S(1)} %get-tuple-element.39), channel_id=1, source_target_pairs={{0,8},{4,12},{8,0},{12,4},{1,9},{5,13},{9,1},{13,5},{2,10},{6,14},... | collective-permute-start | bytes 196616 | tf_op jit(solution)/shard_map/ppermute | solution.py:334
  27.3 1.2 %collective-permute-start.14 = (bf16[16,2048]{1,0:T(8,128)(2,1)S(1)}, bf16[16,2048]{1,0:T(8,128)(2,1)S(1)}, u32[]{:S(2)}, u32[]{:S(2)}) collective-permute-start(bf16[16,2048]{1,0:T(8,128)(2,1)S(1)} %get-tuple-element.41), channel_id=1, source_target_pairs={{0,4},{4,0},{8,12},{12,8},{1,5},{5,1},{9,13},{13,9},{2,6},{6,2},{1... | collective-permute-start | bytes 196616 | tf_op jit(solution)/shard_map/ppermute | solution.py:334
  28.5 0.8 %project.3.y0 = bf16[32,2048]{1,0:T(8,128)(2,1)S(1)} custom-call(bf16[32,1024]{1,0:T(8,128)(2,1)S(1)} %get-tuple-element.29.rows_ref, bf16[1024,8192]{1,0:T(8,128)(2,1)S(1)} %copy-done), custom_call_target="tpu_custom_call" | custom-call | flops 134217728 | bytes 4194304 | tf_op jit(solution)/shard_map/project/pallas_call | solution.py:231
  29.3 1.7 %collective-permute-done.12.a2 = bf16[16,2048]{1,0:T(8,128)(2,1)S(1)} collective-permute-done((bf16[16,2048]{1,0:T(8,128)(2,1)S(1)}, bf16[16,2048]{1,0:T(8,128)(2,1)S(1)}, u32[]{:S(2)}, u32[]{:S(2)}) %collective-permute-start.12) | collective-permute-done | bytes 65568 | tf_op jit(solution)/shard_map/ppermute | solution.py:334
  31.0 0.6 %collective-permute-done.13.a3 = bf16[16,2048]{1,0:T(8,128)(2,1)S(1)} collective-permute-done((bf16[16,2048]{1,0:T(8,128)(2,1)S(1)}, bf16[16,2048]{1,0:T(8,128)(2,1)S(1)}, u32[]{:S(2)}, u32[]{:S(2)}) %collective-permute-start.13) | collective-permute-done | bytes 65568 | tf_op jit(solution)/shard_map/ppermute | solution.py:334
  31.9 0.8 %finish.1 = bf16[32,2048]{1,0:T(8,128)(2,1)} custom-call(bf16[32,128]{1,0:T(8,128)(2,1)S(1)} %get-tuple-element.28.pick_ref, bf16[32,2048]{1,0:T(8,128)(2,1)S(1)} %project.3.y0, bf16[32,2048]{1,0:T(8,128)(2,1)S(1)} %collective-permute-done.3.y1, bf16[32,2048]{1,0:T(8,128)(2,1)S(1)} %collective-permute-done.5.y2, ...), custom_call_target="tpu_custom_call" | custom-call | flops 16777216 | bytes 1048576 | tf_op jit(solution)/shard_map/finish/pallas_call | solution.py:321
  (20 shorter events, 1.0 us)
Async XLA Ops:
  0.0 14.6 %copy-start = (bf16[1024,8192]{1,0:T(8,128)(2,1)S(1)}, bf16[1024,8192]{1,0:T(8,128)(2,1)}, u32[]{:S(2)}) copy-start(bf16[1024,8192]{1,0:T(8,128)(2,1)} %w_ref.5) | copy-start | bytes 50331652
  2.5 15.3 %copy-start.2 = (bf16[4,1024,128]{2,1,0:T(8,128)(2,1)S(1)}, bf16[4,1024,128]{2,1,0:T(8,128)(2,1)}, u32[]{:S(2)}) copy-start(bf16[4,1024,128]{2,1,0:T(8,128)(2,1)} %down_ref.1) | copy-start | bytes 3145732
  2.5 6.8 %collective-permute-start = (bf16[8,1152]{1,0:T(8,128)(2,1)S(1)}, bf16[8,1152]{1,0:T(8,128)(2,1)S(1)}, u32[]{:S(2)}, u32[]{:S(2)}) collective-permute-start(bf16[8,1152]{1,0:T(8,128)(2,1)S(1)} %get-tuple-element.24), channel_id=1, source_target_pairs={{0,3},{1,2},{2,1},{3,0},{4,7},{5,6},{6,5},{7,4},{8,11},{9,10},{10,... | collective-permute-start | bytes 55304 | tf_op jit(solution)/shard_map/ppermute | solution.py:334
  7.6 4.7 %collective-permute-start.1 = (bf16[8,1152]{1,0:T(8,128)(2,1)S(1)}, bf16[8,1152]{1,0:T(8,128)(2,1)S(1)}, u32[]{:S(2)}, u32[]{:S(2)}) collective-permute-start(bf16[8,1152]{1,0:T(8,128)(2,1)S(1)} %get-tuple-element.25), channel_id=1, source_target_pairs={{0,2},{1,3},{2,0},{3,1},{4,6},{5,7},{6,4},{7,5},{8,10},{9,11},{10,... | collective-permute-start | bytes 55304 | tf_op jit(solution)/shard_map/ppermute | solution.py:334
  7.6 4.7 %collective-permute-start.2 = (bf16[8,1152]{1,0:T(8,128)(2,1)S(1)}, bf16[8,1152]{1,0:T(8,128)(2,1)S(1)}, u32[]{:S(2)}, u32[]{:S(2)}) collective-permute-start(bf16[8,1152]{1,0:T(8,128)(2,1)S(1)} %get-tuple-element.26), channel_id=1, source_target_pairs={{0,1},{1,0},{2,3},{3,2},{4,5},{5,4},{6,7},{7,6},{8,9},{9,8},{10,11... | collective-permute-start | bytes 55304 | tf_op jit(solution)/shard_map/ppermute | solution.py:334
  12.7 3.5 %collective-permute-start.6 = (bf16[16,1152]{1,0:T(8,128)(2,1)S(1)}, bf16[16,1152]{1,0:T(8,128)(2,1)S(1)}, u32[]{:S(2)}, u32[]{:S(2)}) collective-permute-start(bf16[16,1152]{1,0:T(8,128)(2,1)S(1)} %get-tuple-element.33), channel_id=1, source_target_pairs={{0,4},{4,0},{8,12},{12,8},{1,5},{5,1},{9,13},{13,9},{2,6},{6,2},{1... | collective-permute-start | bytes 110600 | tf_op jit(solution)/shard_map/ppermute | solution.py:334
  12.8 4.0 %collective-permute-start.7 = (bf16[16,1152]{1,0:T(8,128)(2,1)S(1)}, bf16[16,1152]{1,0:T(8,128)(2,1)S(1)}, u32[]{:S(2)}, u32[]{:S(2)}) collective-permute-start(bf16[16,1152]{1,0:T(8,128)(2,1)S(1)} %get-tuple-element.34), channel_id=1, source_target_pairs={{0,8},{4,12},{8,0},{12,4},{1,9},{5,13},{9,1},{13,5},{2,10},{6,14},... | collective-permute-start | bytes 110600 | tf_op jit(solution)/shard_map/ppermute | solution.py:334
  14.3 3.4 %collective-permute-start.8 = (bf16[16,1152]{1,0:T(8,128)(2,1)S(1)}, bf16[16,1152]{1,0:T(8,128)(2,1)S(1)}, u32[]{:S(2)}, u32[]{:S(2)}) collective-permute-start(bf16[16,1152]{1,0:T(8,128)(2,1)S(1)} %get-tuple-element.35), channel_id=1, source_target_pairs={{0,12},{4,8},{8,4},{12,0},{1,13},{5,9},{9,5},{13,1},{2,14},{6,10},... | collective-permute-start | bytes 110600 | tf_op jit(solution)/shard_map/ppermute | solution.py:334
  16.2 6.9 %collective-permute-start.4 = (bf16[32,2048]{1,0:T(8,128)(2,1)S(1)}, bf16[32,2048]{1,0:T(8,128)(2,1)S(1)}, u32[]{:S(2)}, u32[]{:S(2)}) collective-permute-start(bf16[32,2048]{1,0:T(8,128)(2,1)S(1)} %get-tuple-element.31), channel_id=1, source_target_pairs={{0,1},{1,0},{2,3},{3,2},{4,5},{5,4},{6,7},{7,6},{8,9},{9,8},{10,11... | collective-permute-start | bytes 393224 | tf_op jit(solution)/shard_map/ppermute | solution.py:334
  18.1 7.7 %copy-start.1 = (bf16[4,128,2048]{2,1,0:T(8,128)(2,1)S(1)}, bf16[4,128,2048]{2,1,0:T(8,128)(2,1)}, u32[]{:S(2)}) copy-start(bf16[4,128,2048]{2,1,0:T(8,128)(2,1)} %up_ref.1) | copy-start | bytes 6291460
  18.1 7.4 %collective-permute-start.10 = (bf16[64,128]{1,0:T(8,128)(2,1)S(1)}, bf16[64,128]{1,0:T(8,128)(2,1)S(1)}, u32[]{:S(2)}, u32[]{:S(2)}) collective-permute-start(bf16[64,128]{1,0:T(8,128)(2,1)S(1)} %get-tuple-element.36.l0), channel_id=1, source_target_pairs={{0,2},{1,3},{2,0},{3,1},{4,6},{5,7},{6,4},{7,5},{8,10},{9,11},{10,... | collective-permute-start | bytes 49160 | tf_op jit(solution)/shard_map/ppermute | solution.py:334
  20.2 5.6 %collective-permute-start.11 = (bf16[64,128]{1,0:T(8,128)(2,1)S(1)}, bf16[64,128]{1,0:T(8,128)(2,1)S(1)}, u32[]{:S(2)}, u32[]{:S(2)}) collective-permute-start(bf16[64,128]{1,0:T(8,128)(2,1)S(1)} %get-tuple-element.36.l0), channel_id=1, source_target_pairs={{0,3},{1,2},{2,1},{3,0},{4,7},{5,6},{6,5},{7,4},{8,11},{9,10},{10,... | collective-permute-start | bytes 49160 | tf_op jit(solution)/shard_map/ppermute | solution.py:334
  21.0 4.8 %collective-permute-start.9 = (bf16[64,128]{1,0:T(8,128)(2,1)S(1)}, bf16[64,128]{1,0:T(8,128)(2,1)S(1)}, u32[]{:S(2)}, u32[]{:S(2)}) collective-permute-start(bf16[64,128]{1,0:T(8,128)(2,1)S(1)} %get-tuple-element.36.l0), channel_id=1, source_target_pairs={{0,1},{1,0},{2,3},{3,2},{4,5},{5,4},{6,7},{7,6},{8,9},{9,8},{10,11... | collective-permute-start | bytes 49160 | tf_op jit(solution)/shard_map/ppermute | solution.py:334
  21.6 10.0 %collective-permute-start.3 = (bf16[32,2048]{1,0:T(8,128)(2,1)S(1)}, bf16[32,2048]{1,0:T(8,128)(2,1)S(1)}, u32[]{:S(2)}, u32[]{:S(2)}) collective-permute-start(bf16[32,2048]{1,0:T(8,128)(2,1)S(1)} %get-tuple-element.30), channel_id=1, source_target_pairs={{0,1},{1,0},{2,3},{3,2},{4,5},{5,4},{6,7},{7,6},{8,9},{9,8},{10,11... | collective-permute-start | bytes 393224 | tf_op jit(solution)/shard_map/ppermute | solution.py:334
  23.8 8.1 %collective-permute-start.5 = (bf16[32,2048]{1,0:T(8,128)(2,1)S(1)}, bf16[32,2048]{1,0:T(8,128)(2,1)S(1)}, u32[]{:S(2)}, u32[]{:S(2)}) collective-permute-start(bf16[32,2048]{1,0:T(8,128)(2,1)S(1)} %project.5), channel_id=1, source_target_pairs={{0,2},{1,3},{2,0},{3,1},{4,6},{5,7},{6,4},{7,5},{8,10},{9,11},{10,... | collective-permute-start | bytes 393224 | tf_op jit(solution)/shard_map/ppermute | solution.py:334
  26.3 4.7 %collective-permute-start.12 = (bf16[16,2048]{1,0:T(8,128)(2,1)S(1)}, bf16[16,2048]{1,0:T(8,128)(2,1)S(1)}, u32[]{:S(2)}, u32[]{:S(2)}) collective-permute-start(bf16[16,2048]{1,0:T(8,128)(2,1)S(1)} %get-tuple-element.39), channel_id=1, source_target_pairs={{0,8},{4,12},{8,0},{12,4},{1,9},{5,13},{9,1},{13,5},{2,10},{6,14},... | collective-permute-start | bytes 196616 | tf_op jit(solution)/shard_map/ppermute | solution.py:334
  27.3 4.4 %collective-permute-start.13 = (bf16[16,2048]{1,0:T(8,128)(2,1)S(1)}, bf16[16,2048]{1,0:T(8,128)(2,1)S(1)}, u32[]{:S(2)}, u32[]{:S(2)}) collective-permute-start(bf16[16,2048]{1,0:T(8,128)(2,1)S(1)} %get-tuple-element.40), channel_id=1, source_target_pairs={{0,12},{4,8},{8,4},{12,0},{1,13},{5,9},{9,5},{13,1},{2,14},{6,10},... | collective-permute-start | bytes 196616 | tf_op jit(solution)/shard_map/ppermute | solution.py:334
  27.3 4.4 %collective-permute-start.14 = (bf16[16,2048]{1,0:T(8,128)(2,1)S(1)}, bf16[16,2048]{1,0:T(8,128)(2,1)S(1)}, u32[]{:S(2)}, u32[]{:S(2)}) collective-permute-start(bf16[16,2048]{1,0:T(8,128)(2,1)S(1)} %get-tuple-element.41), channel_id=1, source_target_pairs={{0,4},{4,0},{8,12},{12,8},{1,5},{5,1},{9,13},{13,9},{2,6},{6,2},{1... | collective-permute-start | bytes 196616 | tf_op jit(solution)/shard_map/ppermute | solution.py:334

commit v9 on v8

--- a/solution.py
+++ b/solution.py
@@ -369,13 +369,14 @@
     gathered = [chosen[0]] + [across(chosen[r], "batch", r) for r in (1, 2, 3)]
     far, near = project(rows, output_weight, width, (3, 1))
     far_in = across(far, "tensor", 1)
-    near_in = across(near, "tensor", 1)
 
     low, slot, factor = down(gathered, adapter_down_weight)
     shares = [low] + [across(low, "tensor", r) for r in (1, 2, 3)]
     (cross,) = project(rows, output_weight, width, (2,), addend=far_in)
     (mine,) = project(rows, output_weight, width, (0,))
+    near, cross = lax.optimization_barrier((near, cross))
     cross_in = across(cross, "tensor", 2)
+    near_in = across(near, "tensor", 1)
 
     lifted = up(shares, slot, factor, adapter_up_weight, batch_count)
     lifted = [across(a, "batch", r) for a, r in zip(lifted, (2, 3, 1))] + [lifted[3]]

time: 32.9 us -> 32.5 us (0.988)
  starting transfers between devices: 16.4 us -> 16 us
    ppermute x15, starting transfers between devices: 16.4 us -> 16 us  [across(): return lax.ppermute(value, axis, [(i, i ^ r) for i in range(n)])]
where the time goes in v9:
time: 32.5 us; the launch traced here: 32.4 us
  starting transfers between devices  16 us (49%)
  waiting for transfers between devices  8.61 us (26%)
  Pallas kernels  7.68 us (24%)
    ppermute x15, starting transfers between devices, across(): return lax.ppermute(value, axis, [(i, i ^ r) for i in range(n)])  16 us
    ppermute x15, waiting for transfers between devices, across(): return lax.ppermute(value, axis, [(i, i ^ r) for i in range(n)])  8.61 us
    pallas_call x3, Pallas kernels, project(): pl.pallas_call(functools.partial(project_kernel, which=which, tile=tile,...  3.17 us
    pallas_call x1, Pallas kernels, attend_blocks(): pl.pallas_call(functools.partial(attend_kernel, kv=kv), in_specs=[hbm] *...  2.47 us
    pallas_call x1, Pallas kernels, finish(): pl.pallas_call(finish_kernel, in_specs=[vmem] * 8, out_specs=vmem, out_sh...  0.83 us
  transfers between devices with their start and end apart: 15, of which 8 were waited for; matrix products, arithmetic and copies ran while one was open for 0% of the time, Pallas kernels for 12%

profile of v9, /device:TPU:0, one launch (start us, length us, event | category | flops | bytes accessed | tf_op | source)
XLA Modules:
  0.0 32.4 jit_solution(2990591322393509238)
XLA Ops:
  0.0 2.5 %attend.1 = (bf16[8,1152]{1,0:T(8,128)(2,1)S(1)}, bf16[8,1152]{1,0:T(8,128)(2,1)S(1)}, bf16[8,1152]{1,0:T(8,128)(2,1)S(1)}, bf16[8,1152]{1,0:T(8,128)(2,1)S(1)}) custom-call(s32[8]{0:T(128)} %refs_0_.1, s32[8]{0:T(128)} %refs_1_.1, s32[16]{0:T(128)} %refs_2_.1, bf16[8,4096]{1,0:T(8,128)(2,1)} %refs_3_.1, bf16[8,512]{1,0:T(8,128)(2,1)} %refs_4_.1, ...), custom_call_target="tpu_custom_call" | custom-call | flops 34359738368 | bytes 2097152 | tf_op jit(solution)/shard_map/attend/pallas_call | solution.py:138
  2.5 5.1 %collective-permute-start = (bf16[8,1152]{1,0:T(8,128)(2,1)S(1)}, bf16[8,1152]{1,0:T(8,128)(2,1)S(1)}, u32[]{:S(2)}, u32[]{:S(2)}) collective-permute-start(bf16[8,1152]{1,0:T(8,128)(2,1)S(1)} %get-tuple-element.26), channel_id=1, source_target_pairs={{0,3},{1,2},{2,1},{3,0},{4,7},{5,6},{6,5},{7,4},{8,11},{9,10},{10,... | collective-permute-start | bytes 55304 | tf_op jit(solution)/shard_map/ppermute | solution.py:334
  7.6 0.6 %collective-permute-start.2 = (bf16[8,1152]{1,0:T(8,128)(2,1)S(1)}, bf16[8,1152]{1,0:T(8,128)(2,1)S(1)}, u32[]{:S(2)}, u32[]{:S(2)}) collective-permute-start(bf16[8,1152]{1,0:T(8,128)(2,1)S(1)} %get-tuple-element.28), channel_id=1, source_target_pairs={{0,1},{1,0},{2,3},{3,2},{4,5},{5,4},{6,7},{7,6},{8,9},{9,8},{10,11... | collective-permute-start | bytes 55304 | tf_op jit(solution)/shard_map/ppermute | solution.py:334
  8.2 1.1 %collective-permute-done.x0 = bf16[8,1152]{1,0:T(8,128)(2,1)S(1)} collective-permute-done((bf16[8,1152]{1,0:T(8,128)(2,1)S(1)}, bf16[8,1152]{1,0:T(8,128)(2,1)S(1)}, u32[]{:S(2)}, u32[]{:S(2)}) %collective-permute-start) | collective-permute-done | bytes 18464 | tf_op jit(solution)/shard_map/ppermute | solution.py:334
  9.3 2.9 %collective-permute-done.1.x1 = bf16[8,1152]{1,0:T(8,128)(2,1)S(1)} collective-permute-done((bf16[8,1152]{1,0:T(8,128)(2,1)S(1)}, bf16[8,1152]{1,0:T(8,128)(2,1)S(1)}, u32[]{:S(2)}, u32[]{:S(2)}) %collective-permute-start.1) | collective-permute-done | bytes 18464 | tf_op jit(solution)/shard_map/ppermute | solution.py:334
  12.3 0.4 %route.1 = (bf16[32,1024]{1,0:T(8,128)(2,1)S(1)}, bf16[32,128]{1,0:T(8,128)(2,1)S(1)}, bf16[16,1152]{1,0:T(8,128)(2,1)S(1)}, bf16[16,1152]{1,0:T(8,128)(2,1)S(1)...) custom-call(bf16[8,1152]{1,0:T(8,128)(2,1)S(1)} %collective-permute-done.x0, ...), custom_call_target="tpu_custom_call" | custom-call | flops 1048576 | bytes 294912 | tf_op jit(solution)/shard_map/route/pallas_call | solution.py:198
  12.8 1.6 %collective-permute-start.7 = (bf16[16,1152]{1,0:T(8,128)(2,1)S(1)}, bf16[16,1152]{1,0:T(8,128)(2,1)S(1)}, u32[]{:S(2)}, u32[]{:S(2)}) collective-permute-start(bf16[16,1152]{1,0:T(8,128)(2,1)S(1)} %get-tuple-element.38), channel_id=1, source_target_pairs={{0,8},{4,12},{8,0},{12,4},{1,9},{5,13},{9,1},{13,5},{2,10},{6,14},... | collective-permute-start | bytes 110600 | tf_op jit(solution)/shard_map/ppermute | solution.py:334
  14.6 1.5 %project.4 = (bf16[32,2048]{1,0:T(8,128)(2,1)S(1)}, bf16[32,2048]{1,0:T(8,128)(2,1)S(1)}) custom-call(bf16[32,1024]{1,0:T(8,128)(2,1)S(1)} %get-tuple-element.31.rows_ref, bf16[1024,8192]{1,0:T(8,128)(2,1)S(1)} %copy-done), custom_call_target="tpu_custom_call" | custom-call | flops 268435456 | bytes 8388608 | tf_op jit(solution)/shard_map/project/pallas_call | solution.py:231
  16.2 0.6 %collective-permute-done.7.c2 = bf16[16,1152]{1,0:T(8,128)(2,1)S(1)} collective-permute-done((bf16[16,1152]{1,0:T(8,128)(2,1)S(1)}, bf16[16,1152]{1,0:T(8,128)(2,1)S(1)}, u32[]{:S(2)}, u32[]{:S(2)}) %collective-permute-start.7) | collective-permute-done | bytes 36896 | tf_op jit(solution)/shard_map/ppermute | solution.py:334
  16.8 1.0 %collective-permute-done.8.c3 = bf16[16,1152]{1,0:T(8,128)(2,1)S(1)} collective-permute-done((bf16[16,1152]{1,0:T(8,128)(2,1)S(1)}, bf16[16,1152]{1,0:T(8,128)(2,1)S(1)}, u32[]{:S(2)}, u32[]{:S(2)}) %collective-permute-start.8) | collective-permute-done | bytes 36896 | tf_op jit(solution)/shard_map/ppermute | solution.py:334
  18.1 2.1 %collective-permute-start.10 = (bf16[64,128]{1,0:T(8,128)(2,1)S(1)}, bf16[64,128]{1,0:T(8,128)(2,1)S(1)}, u32[]{:S(2)}, u32[]{:S(2)}) collective-permute-start(bf16[64,128]{1,0:T(8,128)(2,1)S(1)} %get-tuple-element.40.l0), channel_id=1, source_target_pairs={{0,2},{1,3},{2,0},{3,1},{4,6},{5,7},{6,4},{7,5},{8,10},{9,11},{10,... | collective-permute-start | bytes 49160 | tf_op jit(solution)/shard_map/ppermute | solution.py:334
  20.2 0.8 %collective-permute-start.11 = (bf16[64,128]{1,0:T(8,128)(2,1)S(1)}, bf16[64,128]{1,0:T(8,128)(2,1)S(1)}, u32[]{:S(2)}, u32[]{:S(2)}) collective-permute-start(bf16[64,128]{1,0:T(8,128)(2,1)S(1)} %get-tuple-element.40.l0), channel_id=1, source_target_pairs={{0,3},{1,2},{2,1},{3,0},{4,7},{5,6},{6,5},{7,4},{8,11},{9,10},{10,... | collective-permute-start | bytes 49160 | tf_op jit(solution)/shard_map/ppermute | solution.py:334
  21.0 0.6 %collective-permute-start.9 = (bf16[64,128]{1,0:T(8,128)(2,1)S(1)}, bf16[64,128]{1,0:T(8,128)(2,1)S(1)}, u32[]{:S(2)}, u32[]{:S(2)}) collective-permute-start(bf16[64,128]{1,0:T(8,128)(2,1)S(1)} %get-tuple-element.40.l0), channel_id=1, source_target_pairs={{0,1},{1,0},{2,3},{3,2},{4,5},{5,4},{6,7},{7,6},{8,9},{9,8},{10,11... | collective-permute-start | bytes 49160 | tf_op jit(solution)/shard_map/ppermute | solution.py:334
  21.6 0.5 %collective-permute-done.3.refs_0_ = bf16[32,2048]{1,0:T(8,128)(2,1)S(1)} collective-permute-done((bf16[32,2048]{1,0:T(8,128)(2,1)S(1)}, bf16[32,2048]{1,0:T(8,128)(2,1)S(1)}, u32[]{:S(2)}, u32[]{:S(2)}) %collective-permute-start.3) | collective-permute-done | bytes 131104 | tf_op jit(solution)/shard_map/ppermute | solution.py:334
  22.1 0.8 %project.5 = bf16[32,2048]{1,0:T(8,128)(2,1)S(1)} custom-call(bf16[32,1024]{1,0:T(8,128)(2,1)S(1)} %get-tuple-element.31.rows_ref, bf16[1024,8192]{1,0:T(8,128)(2,1)S(1)} %copy-done, bf16[32,2048]{1,0:T(8,128)(2,1)S(1)} %collective-permute-done.3.refs_0_), custom_call_target="tpu_custom_call" | custom-call | flops 134217728 | bytes 4194304 | tf_op jit(solution)/shard_map/project/pallas_call | solution.py:231
  22.9 0.9 %collective-permute-start.4 = (bf16[32,2048]{1,0:T(8,128)(2,1)S(1)}, bf16[32,2048]{1,0:T(8,128)(2,1)S(1)}, u32[]{:S(2)}, u32[]{:S(2)}) collective-permute-start(bf16[32,2048]{1,0:T(8,128)(2,1)S(1)} %get-tuple-element.34), channel_id=1, source_target_pairs={{0,1},{1,0},{2,3},{3,2},{4,5},{5,4},{6,7},{7,6},{8,9},{9,8},{10,11... | collective-permute-start | bytes 393224 | tf_op jit(solution)/shard_map/ppermute | solution.py:334
  23.9 1.6 %collective-permute-start.5 = (bf16[32,2048]{1,0:T(8,128)(2,1)S(1)}, bf16[32,2048]{1,0:T(8,128)(2,1)S(1)}, u32[]{:S(2)}, u32[]{:S(2)}) collective-permute-start(bf16[32,2048]{1,0:T(8,128)(2,1)S(1)} %project.5), channel_id=1, source_target_pairs={{0,2},{1,3},{2,0},{3,1},{4,6},{5,7},{6,4},{7,5},{8,10},{9,11},{10,... | collective-permute-start | bytes 393224 | tf_op jit(solution)/shard_map/ppermute | solution.py:334
  25.8 0.5 %up.1 = (bf16[16,2048]{1,0:T(8,128)(2,1)S(1)}, bf16[16,2048]{1,0:T(8,128)(2,1)S(1)}, bf16[16,2048]{1,0:T(8,128)(2,1)S(1)}, bf16[16,2048]{1,0:T(8,128)(2,1)S(1)}) custom-call(bf16[64,128]{1,0:T(8,128)(2,1)S(1)} %get-tuple-element.40.l0, bf16[64,128]{1,0:T(8,128)(2,1)S(1)} %collective-permute-done.9.l1, bf16[64,128]{1,0:T(8,128)(2,1)S(1)} %collective-permute-done.10.l2, ...), custom_call_target="tpu_custom_call" | custom-call | flops 17179869184 | bytes 2097152 | tf_op jit(solution)/shard_map/up/pallas_call | solution.py:300
  26.3 0.8 %collective-permute-start.12 = (bf16[16,2048]{1,0:T(8,128)(2,1)S(1)}, bf16[16,2048]{1,0:T(8,128)(2,1)S(1)}, u32[]{:S(2)}, u32[]{:S(2)}) collective-permute-start(bf16[16,2048]{1,0:T(8,128)(2,1)S(1)} %get-tuple-element.43), channel_id=1, source_target_pairs={{0,8},{4,12},{8,0},{12,4},{1,9},{5,13},{9,1},{13,5},{2,10},{6,14},... | collective-permute-start | bytes 196616 | tf_op jit(solution)/shard_map/ppermute | solution.py:334
  27.2 1.4 %collective-permute-start.14 = (bf16[16,2048]{1,0:T(8,128)(2,1)S(1)}, bf16[16,2048]{1,0:T(8,128)(2,1)S(1)}, u32[]{:S(2)}, u32[]{:S(2)}) collective-permute-start(bf16[16,2048]{1,0:T(8,128)(2,1)S(1)} %get-tuple-element.45), channel_id=1, source_target_pairs={{0,4},{4,0},{8,12},{12,8},{1,5},{5,1},{9,13},{13,9},{2,6},{6,2},{1... | collective-permute-start | bytes 196616 | tf_op jit(solution)/shard_map/ppermute | solution.py:334
  28.5 0.8 %project.3.y0 = bf16[32,2048]{1,0:T(8,128)(2,1)S(1)} custom-call(bf16[32,1024]{1,0:T(8,128)(2,1)S(1)} %get-tuple-element.31.rows_ref, bf16[1024,8192]{1,0:T(8,128)(2,1)S(1)} %copy-done), custom_call_target="tpu_custom_call" | custom-call | flops 134217728 | bytes 4194304 | tf_op jit(solution)/shard_map/project/pallas_call | solution.py:231
  29.3 1.8 %collective-permute-done.12.a2 = bf16[16,2048]{1,0:T(8,128)(2,1)S(1)} collective-permute-done((bf16[16,2048]{1,0:T(8,128)(2,1)S(1)}, bf16[16,2048]{1,0:T(8,128)(2,1)S(1)}, u32[]{:S(2)}, u32[]{:S(2)}) %collective-permute-start.12) | collective-permute-done | bytes 65568 | tf_op jit(solution)/shard_map/ppermute | solution.py:334
  31.1 0.4 %collective-permute-done.13.a3 = bf16[16,2048]{1,0:T(8,128)(2,1)S(1)} collective-permute-done((bf16[16,2048]{1,0:T(8,128)(2,1)S(1)}, bf16[16,2048]{1,0:T(8,128)(2,1)S(1)}, u32[]{:S(2)}, u32[]{:S(2)}) %collective-permute-start.13) | collective-permute-done | bytes 65568 | tf_op jit(solution)/shard_map/ppermute | solution.py:334
  31.6 0.8 %finish.1 = bf16[32,2048]{1,0:T(8,128)(2,1)} custom-call(bf16[32,128]{1,0:T(8,128)(2,1)S(1)} %get-tuple-element.30.pick_ref, bf16[32,2048]{1,0:T(8,128)(2,1)S(1)} %project.3.y0, bf16[32,2048]{1,0:T(8,128)(2,1)S(1)} %collective-permute-done.4.y1, bf16[32,2048]{1,0:T(8,128)(2,1)S(1)} %collective-permute-done.5.y2, ...), custom_call_target="tpu_custom_call" | custom-call | flops 16777216 | bytes 1048576 | tf_op jit(solution)/shard_map/finish/pallas_call | solution.py:321
  (20 shorter events, 1.1 us)
Async XLA Ops:
  0.0 14.6 %copy-start = (bf16[1024,8192]{1,0:T(8,128)(2,1)S(1)}, bf16[1024,8192]{1,0:T(8,128)(2,1)}, u32[]{:S(2)}) copy-start(bf16[1024,8192]{1,0:T(8,128)(2,1)} %w_ref.5) | copy-start | bytes 50331652
  2.5 15.3 %copy-start.2 = (bf16[4,1024,128]{2,1,0:T(8,128)(2,1)S(1)}, bf16[4,1024,128]{2,1,0:T(8,128)(2,1)}, u32[]{:S(2)}) copy-start(bf16[4,1024,128]{2,1,0:T(8,128)(2,1)} %down_ref.1) | copy-start | bytes 3145732
  2.5 6.8 %collective-permute-start = (bf16[8,1152]{1,0:T(8,128)(2,1)S(1)}, bf16[8,1152]{1,0:T(8,128)(2,1)S(1)}, u32[]{:S(2)}, u32[]{:S(2)}) collective-permute-start(bf16[8,1152]{1,0:T(8,128)(2,1)S(1)} %get-tuple-element.26), channel_id=1, source_target_pairs={{0,3},{1,2},{2,1},{3,0},{4,7},{5,6},{6,5},{7,4},{8,11},{9,10},{10,... | collective-permute-start | bytes 55304 | tf_op jit(solution)/shard_map/ppermute | solution.py:334
  7.6 4.7 %collective-permute-start.1 = (bf16[8,1152]{1,0:T(8,128)(2,1)S(1)}, bf16[8,1152]{1,0:T(8,128)(2,1)S(1)}, u32[]{:S(2)}, u32[]{:S(2)}) collective-permute-start(bf16[8,1152]{1,0:T(8,128)(2,1)S(1)} %get-tuple-element.27), channel_id=1, source_target_pairs={{0,2},{1,3},{2,0},{3,1},{4,6},{5,7},{6,4},{7,5},{8,10},{9,11},{10,... | collective-permute-start | bytes 55304 | tf_op jit(solution)/shard_map/ppermute | solution.py:334
  7.6 4.7 %collective-permute-start.2 = (bf16[8,1152]{1,0:T(8,128)(2,1)S(1)}, bf16[8,1152]{1,0:T(8,128)(2,1)S(1)}, u32[]{:S(2)}, u32[]{:S(2)}) collective-permute-start(bf16[8,1152]{1,0:T(8,128)(2,1)S(1)} %get-tuple-element.28), channel_id=1, source_target_pairs={{0,1},{1,0},{2,3},{3,2},{4,5},{5,4},{6,7},{7,6},{8,9},{9,8},{10,11... | collective-permute-start | bytes 55304 | tf_op jit(solution)/shard_map/ppermute | solution.py:334
  12.7 3.5 %collective-permute-start.6 = (bf16[16,1152]{1,0:T(8,128)(2,1)S(1)}, bf16[16,1152]{1,0:T(8,128)(2,1)S(1)}, u32[]{:S(2)}, u32[]{:S(2)}) collective-permute-start(bf16[16,1152]{1,0:T(8,128)(2,1)S(1)} %get-tuple-element.37), channel_id=1, source_target_pairs={{0,4},{4,0},{8,12},{12,8},{1,5},{5,1},{9,13},{13,9},{2,6},{6,2},{1... | collective-permute-start | bytes 110600 | tf_op jit(solution)/shard_map/ppermute | solution.py:334
  12.8 4.0 %collective-permute-start.7 = (bf16[16,1152]{1,0:T(8,128)(2,1)S(1)}, bf16[16,1152]{1,0:T(8,128)(2,1)S(1)}, u32[]{:S(2)}, u32[]{:S(2)}) collective-permute-start(bf16[16,1152]{1,0:T(8,128)(2,1)S(1)} %get-tuple-element.38), channel_id=1, source_target_pairs={{0,8},{4,12},{8,0},{12,4},{1,9},{5,13},{9,1},{13,5},{2,10},{6,14},... | collective-permute-start | bytes 110600 | tf_op jit(solution)/shard_map/ppermute | solution.py:334
  14.3 3.4 %collective-permute-start.8 = (bf16[16,1152]{1,0:T(8,128)(2,1)S(1)}, bf16[16,1152]{1,0:T(8,128)(2,1)S(1)}, u32[]{:S(2)}, u32[]{:S(2)}) collective-permute-start(bf16[16,1152]{1,0:T(8,128)(2,1)S(1)} %get-tuple-element.39), channel_id=1, source_target_pairs={{0,12},{4,8},{8,4},{12,0},{1,13},{5,9},{9,5},{13,1},{2,14},{6,10},... | collective-permute-start | bytes 110600 | tf_op jit(solution)/shard_map/ppermute | solution.py:334
  16.2 5.9 %collective-permute-start.3 = (bf16[32,2048]{1,0:T(8,128)(2,1)S(1)}, bf16[32,2048]{1,0:T(8,128)(2,1)S(1)}, u32[]{:S(2)}, u32[]{:S(2)}) collective-permute-start(bf16[32,2048]{1,0:T(8,128)(2,1)S(1)} %get-tuple-element.33), channel_id=1, source_target_pairs={{0,1},{1,0},{2,3},{3,2},{4,5},{5,4},{6,7},{7,6},{8,9},{9,8},{10,11... | collective-permute-start | bytes 393224 | tf_op jit(solution)/shard_map/ppermute | solution.py:334
  18.1 7.7 %copy-start.1 = (bf16[4,128,2048]{2,1,0:T(8,128)(2,1)S(1)}, bf16[4,128,2048]{2,1,0:T(8,128)(2,1)}, u32[]{:S(2)}) copy-start(bf16[4,128,2048]{2,1,0:T(8,128)(2,1)} %up_ref.1) | copy-start | bytes 6291460
  18.1 7.4 %collective-permute-start.10 = (bf16[64,128]{1,0:T(8,128)(2,1)S(1)}, bf16[64,128]{1,0:T(8,128)(2,1)S(1)}, u32[]{:S(2)}, u32[]{:S(2)}) collective-permute-start(bf16[64,128]{1,0:T(8,128)(2,1)S(1)} %get-tuple-element.40.l0), channel_id=1, source_target_pairs={{0,2},{1,3},{2,0},{3,1},{4,6},{5,7},{6,4},{7,5},{8,10},{9,11},{10,... | collective-permute-start | bytes 49160 | tf_op jit(solution)/shard_map/ppermute | solution.py:334
  20.2 5.6 %collective-permute-start.11 = (bf16[64,128]{1,0:T(8,128)(2,1)S(1)}, bf16[64,128]{1,0:T(8,128)(2,1)S(1)}, u32[]{:S(2)}, u32[]{:S(2)}) collective-permute-start(bf16[64,128]{1,0:T(8,128)(2,1)S(1)} %get-tuple-element.40.l0), channel_id=1, source_target_pairs={{0,3},{1,2},{2,1},{3,0},{4,7},{5,6},{6,5},{7,4},{8,11},{9,10},{10,... | collective-permute-start | bytes 49160 | tf_op jit(solution)/shard_map/ppermute | solution.py:334
  21.0 4.8 %collective-permute-start.9 = (bf16[64,128]{1,0:T(8,128)(2,1)S(1)}, bf16[64,128]{1,0:T(8,128)(2,1)S(1)}, u32[]{:S(2)}, u32[]{:S(2)}) collective-permute-start(bf16[64,128]{1,0:T(8,128)(2,1)S(1)} %get-tuple-element.40.l0), channel_id=1, source_target_pairs={{0,1},{1,0},{2,3},{3,2},{4,5},{5,4},{6,7},{7,6},{8,9},{9,8},{10,11... | collective-permute-start | bytes 49160 | tf_op jit(solution)/shard_map/ppermute | solution.py:334
  22.9 8.6 %collective-permute-start.4 = (bf16[32,2048]{1,0:T(8,128)(2,1)S(1)}, bf16[32,2048]{1,0:T(8,128)(2,1)S(1)}, u32[]{:S(2)}, u32[]{:S(2)}) collective-permute-start(bf16[32,2048]{1,0:T(8,128)(2,1)S(1)} %get-tuple-element.34), channel_id=1, source_target_pairs={{0,1},{1,0},{2,3},{3,2},{4,5},{5,4},{6,7},{7,6},{8,9},{9,8},{10,11... | collective-permute-start | bytes 393224 | tf_op jit(solution)/shard_map/ppermute | solution.py:334
  23.9 7.7 %collective-permute-start.5 = (bf16[32,2048]{1,0:T(8,128)(2,1)S(1)}, bf16[32,2048]{1,0:T(8,128)(2,1)S(1)}, u32[]{:S(2)}, u32[]{:S(2)}) collective-permute-start(bf16[32,2048]{1,0:T(8,128)(2,1)S(1)} %project.5), channel_id=1, source_target_pairs={{0,2},{1,3},{2,0},{3,1},{4,6},{5,7},{6,4},{7,5},{8,10},{9,11},{10,... | collective-permute-start | bytes 393224 | tf_op jit(solution)/shard_map/ppermute | solution.py:334
  26.3 4.8 %collective-permute-start.12 = (bf16[16,2048]{1,0:T(8,128)(2,1)S(1)}, bf16[16,2048]{1,0:T(8,128)(2,1)S(1)}, u32[]{:S(2)}, u32[]{:S(2)}) collective-permute-start(bf16[16,2048]{1,0:T(8,128)(2,1)S(1)} %get-tuple-element.43), channel_id=1, source_target_pairs={{0,8},{4,12},{8,0},{12,4},{1,9},{5,13},{9,1},{13,5},{2,10},{6,14},... | collective-permute-start | bytes 196616 | tf_op jit(solution)/shard_map/ppermute | solution.py:334
  27.2 4.4 %collective-permute-start.13 = (bf16[16,2048]{1,0:T(8,128)(2,1)S(1)}, bf16[16,2048]{1,0:T(8,128)(2,1)S(1)}, u32[]{:S(2)}, u32[]{:S(2)}) collective-permute-start(bf16[16,2048]{1,0:T(8,128)(2,1)S(1)} %get-tuple-element.44), channel_id=1, source_target_pairs={{0,12},{4,8},{8,4},{12,0},{1,13},{5,9},{9,5},{13,1},{2,14},{6,10},... | collective-permute-start | bytes 196616 | tf_op jit(solution)/shard_map/ppermute | solution.py:334
  27.2 4.4 %collective-permute-start.14 = (bf16[16,2048]{1,0:T(8,128)(2,1)S(1)}, bf16[16,2048]{1,0:T(8,128)(2,1)S(1)}, u32[]{:S(2)}, u32[]{:S(2)}) collective-permute-start(bf16[16,2048]{1,0:T(8,128)(2,1)S(1)} %get-tuple-element.45), channel_id=1, source_target_pairs={{0,4},{4,0},{8,12},{12,8},{1,5},{5,1},{9,13},{13,9},{2,6},{6,2},{1... | collective-permute-start | bytes 196616 | tf_op jit(solution)/shard_map/ppermute | solution.py:334

commit v10 on v9

--- a/solution.py
+++ b/solution.py
@@ -288,7 +288,7 @@
         span = slice(start, start + tile)
         block = up_ref[:, :, span].reshape(local * depth, tile)
         adapted = jnp.dot(kept, block, preferred_element_type=F32).astype(BF16)
-        for r, out in zip((2, 3, 1, 0), outs):
+        for r, out in zip((3, 2, 1, 0), outs):
             out[:, span] = adapted[r * cap : (r + 1) * cap]
 
 
@@ -308,7 +308,7 @@
     )(*shares, slot, factor, weight)
 
 
-def finish_kernel(pick_ref, y0, y1, y2, a2, a3, a1, a0, out):
+def finish_kernel(pick_ref, y0, y1, y2, a3, a2, a1, a0, out):
     rows = jnp.concatenate([a[...] for a in (a0, a1, a2, a3)], axis=0)
     pick = pick_ref[...][:, : rows.shape[0]]
     adapted = jnp.dot(pick, rows, preferred_element_type=F32)
@@ -379,7 +379,7 @@
     near_in = across(near, "tensor", 1)
 
     lifted = up(shares, slot, factor, adapter_up_weight, batch_count)
-    lifted = [across(a, "batch", r) for a, r in zip(lifted, (2, 3, 1))] + [lifted[3]]
+    lifted = [across(a, "batch", r) for a, r in zip(lifted, (3, 2, 1))] + [lifted[3]]
     return finish(pick, (mine, near_in, cross_in), lifted)
 
 

time: 32.5 us -> 32.4 us (level)
  no operation moved by 1% of the time
where the time goes in v10:
time: 32.4 us; the launch traced here: 32.2 us
  starting transfers between devices  15.7 us (48%)
  waiting for transfers between devices  8.72 us (27%)
  Pallas kernels  7.68 us (24%)
    ppermute x15, starting transfers between devices, across(): return lax.ppermute(value, axis, [(i, i ^ r) for i in range(n)])  15.7 us
    ppermute x15, waiting for transfers between devices, across(): return lax.ppermute(value, axis, [(i, i ^ r) for i in range(n)])  8.72 us
    pallas_call x3, Pallas kernels, project(): pl.pallas_call(functools.partial(project_kernel, which=which, tile=tile,...  3.17 us
    pallas_call x1, Pallas kernels, attend_blocks(): pl.pallas_call(functools.partial(attend_kernel, kv=kv), in_specs=[hbm] *...  2.47 us
    pallas_call x1, Pallas kernels, finish(): pl.pallas_call(finish_kernel, in_specs=[vmem] * 8, out_specs=vmem, out_sh...  0.83 us
  transfers between devices with their start and end apart: 15, of which 8 were waited for; matrix products, arithmetic and copies ran while one was open for 0% of the time, Pallas kernels for 12%

profile of v10, /device:TPU:0, one launch (start us, length us, event | category | flops | bytes accessed | tf_op | source)
XLA Modules:
  0.0 32.2 jit_solution(11469909226522486157)
XLA Ops:
  0.0 2.5 %attend.1 = (bf16[8,1152]{1,0:T(8,128)(2,1)S(1)}, bf16[8,1152]{1,0:T(8,128)(2,1)S(1)}, bf16[8,1152]{1,0:T(8,128)(2,1)S(1)}, bf16[8,1152]{1,0:T(8,128)(2,1)S(1)}) custom-call(s32[8]{0:T(128)} %refs_0_.1, s32[8]{0:T(128)} %refs_1_.1, s32[16]{0:T(128)} %refs_2_.1, bf16[8,4096]{1,0:T(8,128)(2,1)} %refs_3_.1, bf16[8,512]{1,0:T(8,128)(2,1)} %refs_4_.1, ...), custom_call_target="tpu_custom_call" | custom-call | flops 34359738368 | bytes 2097152 | tf_op jit(solution)/shard_map/attend/pallas_call | solution.py:138
  2.5 5.1 %collective-permute-start = (bf16[8,1152]{1,0:T(8,128)(2,1)S(1)}, bf16[8,1152]{1,0:T(8,128)(2,1)S(1)}, u32[]{:S(2)}, u32[]{:S(2)}) collective-permute-start(bf16[8,1152]{1,0:T(8,128)(2,1)S(1)} %get-tuple-element.26), channel_id=1, source_target_pairs={{0,3},{1,2},{2,1},{3,0},{4,7},{5,6},{6,5},{7,4},{8,11},{9,10},{10,... | collective-permute-start | bytes 55304 | tf_op jit(solution)/shard_map/ppermute | solution.py:334
  7.6 0.6 %collective-permute-start.2 = (bf16[8,1152]{1,0:T(8,128)(2,1)S(1)}, bf16[8,1152]{1,0:T(8,128)(2,1)S(1)}, u32[]{:S(2)}, u32[]{:S(2)}) collective-permute-start(bf16[8,1152]{1,0:T(8,128)(2,1)S(1)} %get-tuple-element.28), channel_id=1, source_target_pairs={{0,1},{1,0},{2,3},{3,2},{4,5},{5,4},{6,7},{7,6},{8,9},{9,8},{10,11... | collective-permute-start | bytes 55304 | tf_op jit(solution)/shard_map/ppermute | solution.py:334
  8.2 1.1 %collective-permute-done.x0 = bf16[8,1152]{1,0:T(8,128)(2,1)S(1)} collective-permute-done((bf16[8,1152]{1,0:T(8,128)(2,1)S(1)}, bf16[8,1152]{1,0:T(8,128)(2,1)S(1)}, u32[]{:S(2)}, u32[]{:S(2)}) %collective-permute-start) | collective-permute-done | bytes 18464 | tf_op jit(solution)/shard_map/ppermute | solution.py:334
  9.3 2.9 %collective-permute-done.1.x1 = bf16[8,1152]{1,0:T(8,128)(2,1)S(1)} collective-permute-done((bf16[8,1152]{1,0:T(8,128)(2,1)S(1)}, bf16[8,1152]{1,0:T(8,128)(2,1)S(1)}, u32[]{:S(2)}, u32[]{:S(2)}) %collective-permute-start.1) | collective-permute-done | bytes 18464 | tf_op jit(solution)/shard_map/ppermute | solution.py:334
  12.3 0.4 %route.1 = (bf16[32,1024]{1,0:T(8,128)(2,1)S(1)}, bf16[32,128]{1,0:T(8,128)(2,1)S(1)}, bf16[16,1152]{1,0:T(8,128)(2,1)S(1)}, bf16[16,1152]{1,0:T(8,128)(2,1)S(1)...) custom-call(bf16[8,1152]{1,0:T(8,128)(2,1)S(1)} %collective-permute-done.x0, ...), custom_call_target="tpu_custom_call" | custom-call | flops 1048576 | bytes 294912 | tf_op jit(solution)/shard_map/route/pallas_call | solution.py:198
  12.8 1.6 %collective-permute-start.7 = (bf16[16,1152]{1,0:T(8,128)(2,1)S(1)}, bf16[16,1152]{1,0:T(8,128)(2,1)S(1)}, u32[]{:S(2)}, u32[]{:S(2)}) collective-permute-start(bf16[16,1152]{1,0:T(8,128)(2,1)S(1)} %get-tuple-element.38), channel_id=1, source_target_pairs={{0,8},{4,12},{8,0},{12,4},{1,9},{5,13},{9,1},{13,5},{2,10},{6,14},... | collective-permute-start | bytes 110600 | tf_op jit(solution)/shard_map/ppermute | solution.py:334
  14.6 1.5 %project.4 = (bf16[32,2048]{1,0:T(8,128)(2,1)S(1)}, bf16[32,2048]{1,0:T(8,128)(2,1)S(1)}) custom-call(bf16[32,1024]{1,0:T(8,128)(2,1)S(1)} %get-tuple-element.31.rows_ref, bf16[1024,8192]{1,0:T(8,128)(2,1)S(1)} %copy-done), custom_call_target="tpu_custom_call" | custom-call | flops 268435456 | bytes 8388608 | tf_op jit(solution)/shard_map/project/pallas_call | solution.py:231
  16.2 0.6 %collective-permute-done.7.c2 = bf16[16,1152]{1,0:T(8,128)(2,1)S(1)} collective-permute-done((bf16[16,1152]{1,0:T(8,128)(2,1)S(1)}, bf16[16,1152]{1,0:T(8,128)(2,1)S(1)}, u32[]{:S(2)}, u32[]{:S(2)}) %collective-permute-start.7) | collective-permute-done | bytes 36896 | tf_op jit(solution)/shard_map/ppermute | solution.py:334
  16.8 1.0 %collective-permute-done.8.c3 = bf16[16,1152]{1,0:T(8,128)(2,1)S(1)} collective-permute-done((bf16[16,1152]{1,0:T(8,128)(2,1)S(1)}, bf16[16,1152]{1,0:T(8,128)(2,1)S(1)}, u32[]{:S(2)}, u32[]{:S(2)}) %collective-permute-start.8) | collective-permute-done | bytes 36896 | tf_op jit(solution)/shard_map/ppermute | solution.py:334
  18.1 2.1 %collective-permute-start.10 = (bf16[64,128]{1,0:T(8,128)(2,1)S(1)}, bf16[64,128]{1,0:T(8,128)(2,1)S(1)}, u32[]{:S(2)}, u32[]{:S(2)}) collective-permute-start(bf16[64,128]{1,0:T(8,128)(2,1)S(1)} %get-tuple-element.40.l0), channel_id=1, source_target_pairs={{0,2},{1,3},{2,0},{3,1},{4,6},{5,7},{6,4},{7,5},{8,10},{9,11},{10,... | collective-permute-start | bytes 49160 | tf_op jit(solution)/shard_map/ppermute | solution.py:334
  20.2 0.8 %collective-permute-start.11 = (bf16[64,128]{1,0:T(8,128)(2,1)S(1)}, bf16[64,128]{1,0:T(8,128)(2,1)S(1)}, u32[]{:S(2)}, u32[]{:S(2)}) collective-permute-start(bf16[64,128]{1,0:T(8,128)(2,1)S(1)} %get-tuple-element.40.l0), channel_id=1, source_target_pairs={{0,3},{1,2},{2,1},{3,0},{4,7},{5,6},{6,5},{7,4},{8,11},{9,10},{10,... | collective-permute-start | bytes 49160 | tf_op jit(solution)/shard_map/ppermute | solution.py:334
  21.0 0.6 %collective-permute-start.9 = (bf16[64,128]{1,0:T(8,128)(2,1)S(1)}, bf16[64,128]{1,0:T(8,128)(2,1)S(1)}, u32[]{:S(2)}, u32[]{:S(2)}) collective-permute-start(bf16[64,128]{1,0:T(8,128)(2,1)S(1)} %get-tuple-element.40.l0), channel_id=1, source_target_pairs={{0,1},{1,0},{2,3},{3,2},{4,5},{5,4},{6,7},{7,6},{8,9},{9,8},{10,11... | collective-permute-start | bytes 49160 | tf_op jit(solution)/shard_map/ppermute | solution.py:334
  21.6 0.5 %collective-permute-done.3.refs_0_ = bf16[32,2048]{1,0:T(8,128)(2,1)S(1)} collective-permute-done((bf16[32,2048]{1,0:T(8,128)(2,1)S(1)}, bf16[32,2048]{1,0:T(8,128)(2,1)S(1)}, u32[]{:S(2)}, u32[]{:S(2)}) %collective-permute-start.3) | collective-permute-done | bytes 131104 | tf_op jit(solution)/shard_map/ppermute | solution.py:334
  22.1 0.8 %project.5 = bf16[32,2048]{1,0:T(8,128)(2,1)S(1)} custom-call(bf16[32,1024]{1,0:T(8,128)(2,1)S(1)} %get-tuple-element.31.rows_ref, bf16[1024,8192]{1,0:T(8,128)(2,1)S(1)} %copy-done, bf16[32,2048]{1,0:T(8,128)(2,1)S(1)} %collective-permute-done.3.refs_0_), custom_call_target="tpu_custom_call" | custom-call | flops 134217728 | bytes 4194304 | tf_op jit(solution)/shard_map/project/pallas_call | solution.py:231
  22.9 0.9 %collective-permute-start.4 = (bf16[32,2048]{1,0:T(8,128)(2,1)S(1)}, bf16[32,2048]{1,0:T(8,128)(2,1)S(1)}, u32[]{:S(2)}, u32[]{:S(2)}) collective-permute-start(bf16[32,2048]{1,0:T(8,128)(2,1)S(1)} %get-tuple-element.34), channel_id=1, source_target_pairs={{0,1},{1,0},{2,3},{3,2},{4,5},{5,4},{6,7},{7,6},{8,9},{9,8},{10,11... | collective-permute-start | bytes 393224 | tf_op jit(solution)/shard_map/ppermute | solution.py:334
  23.9 1.6 %collective-permute-start.5 = (bf16[32,2048]{1,0:T(8,128)(2,1)S(1)}, bf16[32,2048]{1,0:T(8,128)(2,1)S(1)}, u32[]{:S(2)}, u32[]{:S(2)}) collective-permute-start(bf16[32,2048]{1,0:T(8,128)(2,1)S(1)} %project.5), channel_id=1, source_target_pairs={{0,2},{1,3},{2,0},{3,1},{4,6},{5,7},{6,4},{7,5},{8,10},{9,11},{10,... | collective-permute-start | bytes 393224 | tf_op jit(solution)/shard_map/ppermute | solution.py:334
  25.8 0.5 %up.1 = (bf16[16,2048]{1,0:T(8,128)(2,1)S(1)}, bf16[16,2048]{1,0:T(8,128)(2,1)S(1)}, bf16[16,2048]{1,0:T(8,128)(2,1)S(1)}, bf16[16,2048]{1,0:T(8,128)(2,1)S(1)}) custom-call(bf16[64,128]{1,0:T(8,128)(2,1)S(1)} %get-tuple-element.40.l0, bf16[64,128]{1,0:T(8,128)(2,1)S(1)} %collective-permute-done.9.l1, bf16[64,128]{1,0:T(8,128)(2,1)S(1)} %collective-permute-done.10.l2, ...), custom_call_target="tpu_custom_call" | custom-call | flops 17179869184 | bytes 2097152 | tf_op jit(solution)/shard_map/up/pallas_call | solution.py:300
  26.4 0.8 %collective-permute-start.13 = (bf16[16,2048]{1,0:T(8,128)(2,1)S(1)}, bf16[16,2048]{1,0:T(8,128)(2,1)S(1)}, u32[]{:S(2)}, u32[]{:S(2)}) collective-permute-start(bf16[16,2048]{1,0:T(8,128)(2,1)S(1)} %get-tuple-element.44), channel_id=1, source_target_pairs={{0,8},{4,12},{8,0},{12,4},{1,9},{5,13},{9,1},{13,5},{2,10},{6,14},... | collective-permute-start | bytes 196616 | tf_op jit(solution)/shard_map/ppermute | solution.py:334
  27.2 1.0 %collective-permute-start.14 = (bf16[16,2048]{1,0:T(8,128)(2,1)S(1)}, bf16[16,2048]{1,0:T(8,128)(2,1)S(1)}, u32[]{:S(2)}, u32[]{:S(2)}) collective-permute-start(bf16[16,2048]{1,0:T(8,128)(2,1)S(1)} %get-tuple-element.45), channel_id=1, source_target_pairs={{0,4},{4,0},{8,12},{12,8},{1,5},{5,1},{9,13},{13,9},{2,6},{6,2},{1... | collective-permute-start | bytes 196616 | tf_op jit(solution)/shard_map/ppermute | solution.py:334
  28.2 0.8 %project.3.y0 = bf16[32,2048]{1,0:T(8,128)(2,1)S(1)} custom-call(bf16[32,1024]{1,0:T(8,128)(2,1)S(1)} %get-tuple-element.31.rows_ref, bf16[1024,8192]{1,0:T(8,128)(2,1)S(1)} %copy-done), custom_call_target="tpu_custom_call" | custom-call | flops 134217728 | bytes 4194304 | tf_op jit(solution)/shard_map/project/pallas_call | solution.py:231
  29.0 1.2 %collective-permute-done.12.a3 = bf16[16,2048]{1,0:T(8,128)(2,1)S(1)} collective-permute-done((bf16[16,2048]{1,0:T(8,128)(2,1)S(1)}, bf16[16,2048]{1,0:T(8,128)(2,1)S(1)}, u32[]{:S(2)}, u32[]{:S(2)}) %collective-permute-start.12) | collective-permute-done | bytes 65568 | tf_op jit(solution)/shard_map/ppermute | solution.py:334
  30.2 1.1 %collective-permute-done.13.a2 = bf16[16,2048]{1,0:T(8,128)(2,1)S(1)} collective-permute-done((bf16[16,2048]{1,0:T(8,128)(2,1)S(1)}, bf16[16,2048]{1,0:T(8,128)(2,1)S(1)}, u32[]{:S(2)}, u32[]{:S(2)}) %collective-permute-start.13) | collective-permute-done | bytes 65568 | tf_op jit(solution)/shard_map/ppermute | solution.py:334
  31.4 0.8 %finish.1 = bf16[32,2048]{1,0:T(8,128)(2,1)} custom-call(bf16[32,128]{1,0:T(8,128)(2,1)S(1)} %get-tuple-element.30.pick_ref, bf16[32,2048]{1,0:T(8,128)(2,1)S(1)} %project.3.y0, bf16[32,2048]{1,0:T(8,128)(2,1)S(1)} %collective-permute-done.4.y1, bf16[32,2048]{1,0:T(8,128)(2,1)S(1)} %collective-permute-done.5.y2, ...), custom_call_target="tpu_custom_call" | custom-call | flops 16777216 | bytes 1048576 | tf_op jit(solution)/shard_map/finish/pallas_call | solution.py:321
  (20 shorter events, 1.1 us)
Async XLA Ops:
  0.0 14.6 %copy-start = (bf16[1024,8192]{1,0:T(8,128)(2,1)S(1)}, bf16[1024,8192]{1,0:T(8,128)(2,1)}, u32[]{:S(2)}) copy-start(bf16[1024,8192]{1,0:T(8,128)(2,1)} %w_ref.5) | copy-start | bytes 50331652
  2.5 15.3 %copy-start.2 = (bf16[4,1024,128]{2,1,0:T(8,128)(2,1)S(1)}, bf16[4,1024,128]{2,1,0:T(8,128)(2,1)}, u32[]{:S(2)}) copy-start(bf16[4,1024,128]{2,1,0:T(8,128)(2,1)} %down_ref.1) | copy-start | bytes 3145732
  2.5 6.8 %collective-permute-start = (bf16[8,1152]{1,0:T(8,128)(2,1)S(1)}, bf16[8,1152]{1,0:T(8,128)(2,1)S(1)}, u32[]{:S(2)}, u32[]{:S(2)}) collective-permute-start(bf16[8,1152]{1,0:T(8,128)(2,1)S(1)} %get-tuple-element.26), channel_id=1, source_target_pairs={{0,3},{1,2},{2,1},{3,0},{4,7},{5,6},{6,5},{7,4},{8,11},{9,10},{10,... | collective-permute-start | bytes 55304 | tf_op jit(solution)/shard_map/ppermute | solution.py:334
  7.6 4.7 %collective-permute-start.1 = (bf16[8,1152]{1,0:T(8,128)(2,1)S(1)}, bf16[8,1152]{1,0:T(8,128)(2,1)S(1)}, u32[]{:S(2)}, u32[]{:S(2)}) collective-permute-start(bf16[8,1152]{1,0:T(8,128)(2,1)S(1)} %get-tuple-element.27), channel_id=1, source_target_pairs={{0,2},{1,3},{2,0},{3,1},{4,6},{5,7},{6,4},{7,5},{8,10},{9,11},{10,... | collective-permute-start | bytes 55304 | tf_op jit(solution)/shard_map/ppermute | solution.py:334
  7.6 4.7 %collective-permute-start.2 = (bf16[8,1152]{1,0:T(8,128)(2,1)S(1)}, bf16[8,1152]{1,0:T(8,128)(2,1)S(1)}, u32[]{:S(2)}, u32[]{:S(2)}) collective-permute-start(bf16[8,1152]{1,0:T(8,128)(2,1)S(1)} %get-tuple-element.28), channel_id=1, source_target_pairs={{0,1},{1,0},{2,3},{3,2},{4,5},{5,4},{6,7},{7,6},{8,9},{9,8},{10,11... | collective-permute-start | bytes 55304 | tf_op jit(solution)/shard_map/ppermute | solution.py:334
  12.7 3.5 %collective-permute-start.6 = (bf16[16,1152]{1,0:T(8,128)(2,1)S(1)}, bf16[16,1152]{1,0:T(8,128)(2,1)S(1)}, u32[]{:S(2)}, u32[]{:S(2)}) collective-permute-start(bf16[16,1152]{1,0:T(8,128)(2,1)S(1)} %get-tuple-element.37), channel_id=1, source_target_pairs={{0,4},{4,0},{8,12},{12,8},{1,5},{5,1},{9,13},{13,9},{2,6},{6,2},{1... | collective-permute-start | bytes 110600 | tf_op jit(solution)/shard_map/ppermute | solution.py:334
  12.8 4.0 %collective-permute-start.7 = (bf16[16,1152]{1,0:T(8,128)(2,1)S(1)}, bf16[16,1152]{1,0:T(8,128)(2,1)S(1)}, u32[]{:S(2)}, u32[]{:S(2)}) collective-permute-start(bf16[16,1152]{1,0:T(8,128)(2,1)S(1)} %get-tuple-element.38), channel_id=1, source_target_pairs={{0,8},{4,12},{8,0},{12,4},{1,9},{5,13},{9,1},{13,5},{2,10},{6,14},... | collective-permute-start | bytes 110600 | tf_op jit(solution)/shard_map/ppermute | solution.py:334
  14.3 3.4 %collective-permute-start.8 = (bf16[16,1152]{1,0:T(8,128)(2,1)S(1)}, bf16[16,1152]{1,0:T(8,128)(2,1)S(1)}, u32[]{:S(2)}, u32[]{:S(2)}) collective-permute-start(bf16[16,1152]{1,0:T(8,128)(2,1)S(1)} %get-tuple-element.39), channel_id=1, source_target_pairs={{0,12},{4,8},{8,4},{12,0},{1,13},{5,9},{9,5},{13,1},{2,14},{6,10},... | collective-permute-start | bytes 110600 | tf_op jit(solution)/shard_map/ppermute | solution.py:334
  16.2 5.9 %collective-permute-start.3 = (bf16[32,2048]{1,0:T(8,128)(2,1)S(1)}, bf16[32,2048]{1,0:T(8,128)(2,1)S(1)}, u32[]{:S(2)}, u32[]{:S(2)}) collective-permute-start(bf16[32,2048]{1,0:T(8,128)(2,1)S(1)} %get-tuple-element.33), channel_id=1, source_target_pairs={{0,1},{1,0},{2,3},{3,2},{4,5},{5,4},{6,7},{7,6},{8,9},{9,8},{10,11... | collective-permute-start | bytes 393224 | tf_op jit(solution)/shard_map/ppermute | solution.py:334
  18.1 7.7 %copy-start.1 = (bf16[4,128,2048]{2,1,0:T(8,128)(2,1)S(1)}, bf16[4,128,2048]{2,1,0:T(8,128)(2,1)}, u32[]{:S(2)}) copy-start(bf16[4,128,2048]{2,1,0:T(8,128)(2,1)} %up_ref.1) | copy-start | bytes 6291460
  18.1 7.4 %collective-permute-start.10 = (bf16[64,128]{1,0:T(8,128)(2,1)S(1)}, bf16[64,128]{1,0:T(8,128)(2,1)S(1)}, u32[]{:S(2)}, u32[]{:S(2)}) collective-permute-start(bf16[64,128]{1,0:T(8,128)(2,1)S(1)} %get-tuple-element.40.l0), channel_id=1, source_target_pairs={{0,2},{1,3},{2,0},{3,1},{4,6},{5,7},{6,4},{7,5},{8,10},{9,11},{10,... | collective-permute-start | bytes 49160 | tf_op jit(solution)/shard_map/ppermute | solution.py:334
  20.2 5.6 %collective-permute-start.11 = (bf16[64,128]{1,0:T(8,128)(2,1)S(1)}, bf16[64,128]{1,0:T(8,128)(2,1)S(1)}, u32[]{:S(2)}, u32[]{:S(2)}) collective-permute-start(bf16[64,128]{1,0:T(8,128)(2,1)S(1)} %get-tuple-element.40.l0), channel_id=1, source_target_pairs={{0,3},{1,2},{2,1},{3,0},{4,7},{5,6},{6,5},{7,4},{8,11},{9,10},{10,... | collective-permute-start | bytes 49160 | tf_op jit(solution)/shard_map/ppermute | solution.py:334
  21.0 4.8 %collective-permute-start.9 = (bf16[64,128]{1,0:T(8,128)(2,1)S(1)}, bf16[64,128]{1,0:T(8,128)(2,1)S(1)}, u32[]{:S(2)}, u32[]{:S(2)}) collective-permute-start(bf16[64,128]{1,0:T(8,128)(2,1)S(1)} %get-tuple-element.40.l0), channel_id=1, source_target_pairs={{0,1},{1,0},{2,3},{3,2},{4,5},{5,4},{6,7},{7,6},{8,9},{9,8},{10,11... | collective-permute-start | bytes 49160 | tf_op jit(solution)/shard_map/ppermute | solution.py:334
  22.9 8.5 %collective-permute-start.4 = (bf16[32,2048]{1,0:T(8,128)(2,1)S(1)}, bf16[32,2048]{1,0:T(8,128)(2,1)S(1)}, u32[]{:S(2)}, u32[]{:S(2)}) collective-permute-start(bf16[32,2048]{1,0:T(8,128)(2,1)S(1)} %get-tuple-element.34), channel_id=1, source_target_pairs={{0,1},{1,0},{2,3},{3,2},{4,5},{5,4},{6,7},{7,6},{8,9},{9,8},{10,11... | collective-permute-start | bytes 393224 | tf_op jit(solution)/shard_map/ppermute | solution.py:334
  23.9 7.5 %collective-permute-start.5 = (bf16[32,2048]{1,0:T(8,128)(2,1)S(1)}, bf16[32,2048]{1,0:T(8,128)(2,1)S(1)}, u32[]{:S(2)}, u32[]{:S(2)}) collective-permute-start(bf16[32,2048]{1,0:T(8,128)(2,1)S(1)} %project.5), channel_id=1, source_target_pairs={{0,2},{1,3},{2,0},{3,1},{4,6},{5,7},{6,4},{7,5},{8,10},{9,11},{10,... | collective-permute-start | bytes 393224 | tf_op jit(solution)/shard_map/ppermute | solution.py:334
  26.3 3.9 %collective-permute-start.12 = (bf16[16,2048]{1,0:T(8,128)(2,1)S(1)}, bf16[16,2048]{1,0:T(8,128)(2,1)S(1)}, u32[]{:S(2)}, u32[]{:S(2)}) collective-permute-start(bf16[16,2048]{1,0:T(8,128)(2,1)S(1)} %get-tuple-element.43), channel_id=1, source_target_pairs={{0,12},{4,8},{8,4},{12,0},{1,13},{5,9},{9,5},{13,1},{2,14},{6,10},... | collective-permute-start | bytes 196616 | tf_op jit(solution)/shard_map/ppermute | solution.py:334
  26.4 5.0 %collective-permute-start.13 = (bf16[16,2048]{1,0:T(8,128)(2,1)S(1)}, bf16[16,2048]{1,0:T(8,128)(2,1)S(1)}, u32[]{:S(2)}, u32[]{:S(2)}) collective-permute-start(bf16[16,2048]{1,0:T(8,128)(2,1)S(1)} %get-tuple-element.44), channel_id=1, source_target_pairs={{0,8},{4,12},{8,0},{12,4},{1,9},{5,13},{9,1},{13,5},{2,10},{6,14},... | collective-permute-start | bytes 196616 | tf_op jit(solution)/shard_map/ppermute | solution.py:334
  27.2 4.1 %collective-permute-start.14 = (bf16[16,2048]{1,0:T(8,128)(2,1)S(1)}, bf16[16,2048]{1,0:T(8,128)(2,1)S(1)}, u32[]{:S(2)}, u32[]{:S(2)}) collective-permute-start(bf16[16,2048]{1,0:T(8,128)(2,1)S(1)} %get-tuple-element.45), channel_id=1, source_target_pairs={{0,4},{4,0},{8,12},{12,8},{1,5},{5,1},{9,13},{13,9},{2,6},{6,2},{1... | collective-permute-start | bytes 196616 | tf_op jit(solution)/shard_map/ppermute | solution.py:334
